TPU v7x, 32 devices: a whole 2x2x4 slice. The times are simulated.
32 devices in a mesh: row: 8 (over y, x, core), col: 4 (over z).
Axes of the slice: x: 2, y: 2, z: 4, core: 2. Of those that a mesh axis runs over, the one named last changes fastest.
Arguments:
- features: float32 [16384, 256], P(('col', 'row')), may hold values from -6 to 6
- weight_matrix: float32 [256, 256], replicated, may hold values from -0.375 to 0.375
- cotangent: float32 [16384, 256], P(('row', 'col')), may hold values from -6 to 6
- block_rows: int32 [8, 4, 96], P('row', 'col'), may hold values from 0 to 15
- block_cols: int32 [8, 4, 96], P('row', 'col'), may hold values from 0 to 31
- blocks: float32 [8, 4, 96, 128, 128], P('row', 'col'), may hold values from -0.109375 to 0.109375
Outputs:
- hidden: float32 [16384, 256], P(('row', 'col'))
- weight_grad: float32 [256, 256], replicated
- feature_grad: float32 [16384, 256], P(('col', 'row'))
All inputs are finite; a program needn't handle non-finite values.
Results may differ from a plain program's by a relative error of at most 0.0001.
Values sent between devices are 32-bit elements; how exact they have to be, the bound alone decides.
No kernel may reach another device: no remote copies, remote signals or barrier semaphores. Data moves between devices by JAX's collectives and lax.ppermute only.
A program may use at most 128 MiB of HBM per device.

v0:
```python
import jax
import jax.numpy as jnp
from jax import lax
from jax.sharding import PartitionSpec as P


def activate(pre, cotangent):
    sigmoid_v = 1.0 / (1.0 + jnp.exp(-pre))
    return (pre * sigmoid_v, cotangent * sigmoid_v * (1.0 + pre * (1.0 - sigmoid_v)))


def tile_product(values, take_ids, put_ids, source, put_count, form):
    size_block = values.shape[-1]
    width = source.shape[1]
    chosen = source.reshape(-1, size_block, width)[take_ids]
    products = jnp.einsum(form, values, chosen, precision=lax.Precision.HIGHEST)
    summed = jnp.zeros((put_count, size_block, width), jnp.float32).at[put_ids].add(products)
    return summed.reshape(put_count * size_block, width)


def shards(features, weight_matrix, cotangent, block_rows, block_cols, blocks):
    high = lax.Precision.HIGHEST
    tile_values = blocks[0, 0]
    rows_here = block_rows[0, 0]
    cols_here = block_cols[0, 0]
    size_block = tile_values.shape[-1]
    rows_dev = features.shape[0]
    count_row = lax.axis_size("row")
    count_col = lax.axis_size("col")
    row_blocks = rows_dev * count_col // size_block
    col_blocks = rows_dev * count_row // size_block
    total_nodes = rows_dev * count_row * count_col
    feature_tile = lax.all_gather(features, "row", axis=0, tiled=True)
    partial_value = tile_product(
        tile_values, cols_here, rows_here, feature_tile, row_blocks, "kij,kjf->kif"
    )
    row_cotangent = lax.all_gather(cotangent, "col", axis=0, tiled=True)
    row_inputs = lax.psum(partial_value, "col")
    pre = jnp.dot(row_inputs, weight_matrix, precision=high)
    activated, dpre = activate(pre, row_cotangent)
    start = lax.axis_index("col") * rows_dev
    hidden = lax.dynamic_slice_in_dim(activated, start, rows_dev, 0)
    own_inputs = lax.dynamic_slice_in_dim(row_inputs, start, rows_dev, 0)
    own_dpre = lax.dynamic_slice_in_dim(dpre, start, rows_dev, 0)
    back_rows = jnp.dot(dpre, weight_matrix.T, precision=high)
    local_grad = lax.dot_general(own_inputs, own_dpre, (((0,), (0,)), ((), ())), precision=high)
    local_grad = local_grad / jnp.sqrt(jnp.float32(total_nodes))
    weight_grad = lax.psum(local_grad, ("row", "col"))
    grad_part = tile_product(
        tile_values, rows_here, cols_here, back_rows, col_blocks, "kji,kjf->kif"
    )
    feature_grad = lax.psum_scatter(grad_part, "row", scatter_dimension=0, tiled=True)
    return (hidden, weight_grad, feature_grad)


def solution(mesh):
    in_specs = (
        P(("col", "row"), None),
        P(),
        P(("row", "col"), None),
        P("row", "col", None),
        P("row", "col", None),
        P("row", "col", None, None, None),
    )
    out_specs = (P(("row", "col"), None), P(), P(("col", "row"), None))
    return jax.shard_map(shards, mesh=mesh, in_specs=in_specs, out_specs=out_specs, check_vma=False)
```

profile of v0, /device:TPU:0, one launch (start us, length us, event | category | flops | bytes accessed | tf_op | source)
XLA Modules:
  0.0 404.5 jit_solution(9342732112793179747)
XLA Ops:
  7.2 0.0 copy-start
  7.2 0.0 all-gather.3.cloned.1.call-start
  7.2 0.7 all-gather.3.cloned.1.call-update
  7.9 0.0 all-gather.5.cloned.1.call-start
  8.0 0.7 all-gather.5.cloned.1.call-update
  8.7 0.0 all-reduce.3.cloned.1.call-start
  8.7 0.7 fusion.14
  9.4 0.7 fusion.13
  10.0 39.3 %all-gather.3.cloned.1.call-done = f32[4096,256]{1,0:T(8,128)} async-done(((f32[512,256]{1,0:T(8,128)}), f32[4096,256]{1,0:T(8,128)}) %all-gather.3.cloned.1.call-update) | async-done | bytes 4194320 | tf_op jit(solution)/shard_map/all_gather | solution.py:33
  49.4 11.0 %gather_fusion = f32[96,128,256]{2,1,0:T(8,128)} fusion(f32[32,128,256]{2,1,0:T(8,128)} %bitcast.34, s32[1024]{0:T(1024)S(1)} %pad_clamp_fusion.1), kind=kCustom, calls=%fused_computation | custom fusion | bytes 25166208 | tf_op jit(solution)/shard_map/gather | solution.py:15
  60.4 27.0 %fusion.4 = f32[96,128,256]{1,2,0:T(8,128)} fusion(f32[96,128,256]{2,1,0:T(8,128)} %gather_fusion, f32[1,1,96,128,128]{4,3,2,1,0:T(8,128)} %param.11), kind=kOutput, calls=%fused_computation.8 | convolution fusion | flops 4831838208 | bytes 31457280 | tf_op jit(solution)/shard_map/kij,kjf->kif/dot_general | solution.py:16
  87.3 12.6 %copy.12 = f32[96,128,256]{2,1,0:T(8,128)} copy(f32[96,128,256]{1,2,0:T(8,128)} %fusion.4) | data formatting | bytes 25165824 | tf_op jit(solution)/shard_map/kij,kjf->kif/dot_general | solution.py:16
  99.9 0.2 broadcast_in_dim.4
  100.1 18.3 %scatter_fusion = f32[16,128,256]{2,1,0:T(8,128)S(1)} fusion(f32[16,128,256]{2,1,0:T(8,128)S(1)} %broadcast_in_dim.4, s32[96]{0:T(128)S(1)} %fusion.13, f32[96,128,256]{2,1,0:T(8,128)} %copy.12), kind=kCustom, calls=%fused_computation.2 | custom fusion | flops 3145728 | bytes 37749120 | tf_op jit(solution)/shard_map/scatter-add | solution.py:17
  118.5 0.0 copy-start.2
  118.5 1.3 copy-done.2
  119.8 0.0 all-reduce.3.cloned.1.call-update
  119.8 0.2 all-reduce.5.cloned.1.call-start
  120.0 0.0 all-gather.5.cloned.1.call-done
  120.1 86.4 %all-reduce.3.cloned.1.call-done = f32[2048,256]{1,0:T(8,128)} async-done(((f32[2048,256]{1,0:T(8,128)}), f32[2048,256]{1,0:T(8,128)}) %all-reduce.3.cloned.1.call-update) | async-done | bytes 2097168 | tf_op jit(solution)/shard_map/psum | solution.py:38
  206.5 0.0 copy-done
  206.5 6.5 %add_multiply_fusion = (f32[2048,256]{1,0:T(8,128)S(1)}, f32[2048,256]{1,0:T(8,128)}, f32[2048,256]{1,0:T(8,128)}) fusion(f32[2048,256]{1,0:T(8,128)} %all-gather.5.cloned.1.call-done, f32[2048,256]{1,0:T(8,128)} %all-reduce.3.cloned.1.call-done, f32[256,256]{1,0:T(8,128)S(1)} %copy-done), kind=kOutput, calls=%fused_computation.10 | convolution fusion | flops 1614807040 | bytes 10747904 | tf_op jit(solution)/shard_map/dot_general | solution.py:39
  213.0 1.8 fusion.15
  214.8 2.8 convolution_multiply_fusion
  217.6 0.0 all-reduce.5.cloned.1.call-update
  217.6 0.0 reduce-scatter.2.cloned.1.call-start
  217.7 5.9 %gather_fusion.1 = f32[96,128,256]{2,1,0:T(8,128)} fusion(f32[16,128,256]{2,1,0:T(8,128)S(1)} %bitcast.33, s32[1024]{0:T(1024)S(1)} %pad_clamp_fusion), kind=kCustom, calls=%fused_computation.1 | custom fusion | bytes 25166208 | tf_op jit(solution)/shard_map/gather | solution.py:15
  223.6 26.9 %fusion.7 = f32[96,128,256]{1,2,0:T(8,128)} fusion(f32[96,128,256]{2,1,0:T(8,128)} %gather_fusion.1, f32[1,1,96,128,128]{4,3,2,1,0:T(8,128)} %param.11), kind=kOutput, calls=%fused_computation.9 | convolution fusion | flops 4831838208 | bytes 31457280 | tf_op jit(solution)/shard_map/kji,kjf->kif/dot_general | solution.py:16
  250.5 12.6 %copy.14 = f32[96,128,256]{2,1,0:T(8,128)} copy(f32[96,128,256]{1,2,0:T(8,128)} %fusion.7) | data formatting | bytes 25165824 | tf_op jit(solution)/shard_map/kji,kjf->kif/dot_general | solution.py:16
  263.1 2.4 broadcast_in_dim.5
  265.5 0.0 copy-start.1
  265.5 28.9 %scatter_fusion.1 = f32[32,128,256]{2,1,0:T(8,128)} fusion(f32[32,128,256]{2,1,0:T(8,128)} %broadcast_in_dim.5, s32[96]{0:T(128)S(1)} %fusion.14, f32[96,128,256]{2,1,0:T(8,128)} %copy.14), kind=kCustom, calls=%fused_computation.3 | custom fusion | flops 3145728 | bytes 37749120 | tf_op jit(solution)/shard_map/scatter-add | solution.py:17
  294.4 0.0 reduce-scatter.2.cloned.1.call-update
  294.4 2.1 dynamic-slice_multiply_fusion
  296.5 45.3 %all-reduce.5.cloned.1.call-done = f32[256,256]{1,0:T(8,128)} async-done(((f32[256,256]{1,0:T(8,128)}), f32[256,256]{1,0:T(8,128)}) %all-reduce.5.cloned.1.call-update) | async-done | bytes 262160 | tf_op jit(solution)/shard_map/psum | solution.py:48
  341.7 54.5 %reduce-scatter.2.cloned.1.call-done = f32[512,256]{1,0:T(8,128)} async-done(((f32[4096,256]{1,0:T(8,128)}), f32[512,256]{1,0:T(8,128)}) %reduce-scatter.2.cloned.1.call-update) | async-done | bytes 524304 | tf_op jit(solution)/shard_map/reduce_scatter | solution.py:52
  396.3 1.7 copy.21
  397.9 0.0 copy-done.1
  (2 shorter events, 0.0 us)
Async XLA Ops:
  7.2 199.3 %copy-start = (f32[256,256]{1,0:T(8,128)S(1)}, f32[256,256]{1,0:T(8,128)}, u32[]{:S(2)}) copy-start(f32[256,256]{1,0:T(8,128)} %param.7) | copy-start | bytes 786436
  7.2 42.2 %all-gather.3.cloned.1.call-start = ((), (), s32[]{:S(2)}) async-start(), calls=%async_computation.1 | async-start | bytes 4718592 | tf_op jit(solution)/shard_map/all_gather | solution.py:33
  7.9 112.1 %all-gather.5.cloned.1.call-start = ((), (), s32[]{:S(2)}) async-start(), calls=%async_computation.3 | async-start | bytes 2621440 | tf_op jit(solution)/shard_map/all_gather | solution.py:37
  8.7 197.8 %all-reduce.3.cloned.1.call-start = ((), (), s32[]{:S(2)}) async-start(), calls=%async_computation.2 | async-start | bytes 4194304 | tf_op jit(solution)/shard_map/psum | solution.py:38
  118.5 1.3 copy-start.2
  119.8 222.0 %all-reduce.5.cloned.1.call-start = ((), (), s32[]{:S(2)}) async-start(), calls=%async_computation.4 | async-start | bytes 524288 | tf_op jit(solution)/shard_map/psum | solution.py:48
  217.6 178.7 %reduce-scatter.2.cloned.1.call-start = ((), (), s32[]{:S(2)}) async-start(), calls=%async_computation.5 | async-start | bytes 4718592 | tf_op jit(solution)/shard_map/reduce_scatter | solution.py:52
  265.5 132.5 %copy-start.1 = (f32[256,256]{1,0:T(8,128)S(1)}, f32[256,256]{1,0:T(8,128)}, u32[]{:S(2)}) copy-start(f32[256,256]{1,0:T(8,128)} %param.7) | copy-start | bytes 786436
Sparse Core Ops, SparseCore 0:
  9.9 39.4 all-gather.2
  50.9 45.9 all-gather.4
  119.9 86.5 all-reduce.2
  217.7 123.9 all-reduce.4
  345.9 50.3 reduce-scatter.1
where the time goes:
time: 405 us; the launch traced here: 404 us
  waiting for transfers between devices  227 us (56%)
  matrix products  65 us (16%)
  other arithmetic  50.6 us (12%)
  local copies, waits for them, and re-layouts  47.7 us (12%)
  between operations  13.8 us (3%)
    psum x1, waiting for transfers between devices, shards(): row_inputs = lax.psum(partial_value, 'col')  86.4 us
    reduce_scatter x1, waiting for transfers between devices, shards(): lax.psum_scatter(grad_part, 'row', scatter_dimension=0, tiled=True)  54.5 us
    dot_general x2, matrix products, tile_product(): products = jnp.einsum(form, values, chosen, precision=lax.Precision.HIGHEST)  53.9 us
    scatter-add x2, other arithmetic, tile_product(): jnp.zeros((put_count, size_block, width), jnp.float32).at[put_ids]  47.2 us
    psum x1, waiting for transfers between devices, shards(): weight_grad = lax.psum(local_grad, ('row', 'col'))  45.3 us
    all_gather x1, waiting for transfers between devices, shards(): feature_tile = lax.all_gather(features, 'row', axis=0, tiled=True)  39.3 us
    dot_general x2, local copies, waits for them, and re-layouts, tile_product(): products = jnp.einsum(form, values, chosen, precision=lax.Precision.HIGHEST)  25.1 us
    gather x2, local copies, waits for them, and re-layouts, tile_product(): chosen = source.reshape(-1, size_block, width)[take_ids]  16.9 us
  transfers between devices with their start and end apart: 5, of which 4 were waited for; matrix products, arithmetic and copies ran while one was open for 37% of the time, Pallas kernels for 0%

commit v1 on v0

v1 whole, which is shorter than its diff:
```python
import functools

import jax
import jax.numpy as jnp
from jax import lax
from jax.experimental import pallas as pl
from jax.experimental.pallas import tpu as pltpu
from jax.sharding import PartitionSpec as P

VMEM_LIMIT = 52 * 1024 * 1024

OUTER = ((0, 1), (1, 0), (2, 3), (3, 2))
MIDDLE = ((1, 2), (2, 1))
INWARD = ((0, 1), (3, 2))
OUTWARD = ((1, 0), (2, 3))
ACROSS = ((0, 2), (1, 3), (2, 0), (3, 1))


def two_terms(x):
    high = x.astype(jnp.bfloat16)
    low = (x - high.astype(jnp.float32)).astype(jnp.bfloat16)
    return high, low


def dot_terms(left, right, dims):
    left_high, left_low = two_terms(left)
    right_high, right_low = two_terms(right)
    dot = functools.partial(
        lax.dot_general, dimension_numbers=(dims, ((), ())), preferred_element_type=jnp.float32
    )
    return dot(left_high, right_high) + (dot(left_high, right_low) + dot(left_low, right_high))


def row_slot(block, place, per, swap):
    group = (block // per) ^ place[1]
    if swap:
        group = group ^ (place[2] & (2 * (group & 1)))
    return group * per + block % per


def col_slot(block, place, per):
    return ((block // per) ^ place[0]) * per + block % per


def spmm_kernel(count_in, count_out, per_step, per, transposed, place, rows_ref, cols_ref, values_ref, *refs):
    pieces, outs = refs[:count_in], refs[count_in : count_in + count_out]
    source, total = refs[count_in + count_out :]
    size = values_ref.shape[-1]
    width = total.shape[-1]
    step = pl.program_id(0)

    @pl.when(step == 0)
    def _():
        slot = 0
        for piece in pieces:
            for block in range(piece.shape[0] // size):
                high, low = two_terms(piece[pl.ds(block * size, size), :])
                both = jnp.concatenate([high, low], axis=1)
                source[slot, pl.ds(0, size), :] = both
                source[slot, pl.ds(size, size), :] = both
                slot += 1
        total[...] = jnp.zeros_like(total)

    for k in range(per_step):
        row, col = rows_ref[step * per_step + k], cols_ref[step * per_step + k]
        if transposed:
            take, put = row_slot(row, place, per, False), col_slot(col, place, per)
        else:
            take, put = col_slot(col, place, per), row_slot(row, place, per, True)
        axis = 0 if transposed else 1
        left = jnp.concatenate(two_terms(values_ref[k]), axis=axis)
        product = lax.dot_general(
            left, source[take], (((axis,), (0,)), ((), ())), preferred_element_type=jnp.float32
        )
        total[put] += product[:, :width] + product[:, width:]

    @pl.when(step == pl.num_programs(0) - 1)
    def _():
        slot = 0
        for out in outs:
            for block in range(out.shape[0] // size):
                out[pl.ds(block * size, size), :] = total[slot]
                slot += 1


def spmm(place, rows, cols, values, pieces, out_rows, per, transposed):
    count, size = values.shape[0], values.shape[-1]
    width = pieces[0].shape[1]
    per_step = next(p for p in (8, 4, 2, 1) if count % p == 0)
    in_blocks = sum(p.shape[0] for p in pieces) // size
    out_blocks = sum(out_rows) // size
    whole = lambda rows: pl.BlockSpec((rows, width), lambda i, *_: (0, 0))
    return pl.pallas_call(
        functools.partial(spmm_kernel, len(pieces), len(out_rows), per_step, per, transposed),
        out_shape=[jax.ShapeDtypeStruct((rows, width), jnp.float32) for rows in out_rows],
        grid_spec=pltpu.PrefetchScalarGridSpec(
            num_scalar_prefetch=3,
            grid=(count // per_step,),
            in_specs=[pl.BlockSpec((per_step, size, size), lambda i, *_: (i, 0, 0))]
            + [whole(p.shape[0]) for p in pieces],
            out_specs=[whole(rows) for rows in out_rows],
            scratch_shapes=[
                pltpu.VMEM((in_blocks, 2 * size, 2 * width), jnp.bfloat16),
                pltpu.VMEM((out_blocks, size, width), jnp.float32),
            ],
        ),
        compiler_params=pltpu.CompilerParams(vmem_limit_bytes=VMEM_LIMIT),
        cost_estimate=pl.CostEstimate(
            flops=8 * count * size * size * width,
            bytes_accessed=4 * (values.size + (in_blocks + out_blocks) * size * width),
            transcendentals=0,
        ),
    )(place, rows, cols, values, *pieces)


def dense_kernel(count_parts, place, *refs):
    halves = []
    for half in range(2):
        parts = refs[half * count_parts : (half + 1) * count_parts]
        rows = parts[0][...]
        if count_parts > 1:
            rows = rows + jnp.where(place[2] != 0, parts[1][...], 0.0)
            for part in parts[2:]:
                rows = rows + part[...]
        halves.append(rows)
    cotangent, weight, hidden, back_first, back_second, grad_out = refs[2 * count_parts :]
    width = back_first.shape[1]
    rows = jnp.concatenate(halves, axis=1)
    pre = dot_terms(rows, weight[...], ((1,), (0,)))
    sigmoid_v = 1.0 / (1.0 + jnp.exp(-pre))
    hidden[...] = pre * sigmoid_v
    dpre = cotangent[...] * sigmoid_v * (1.0 + pre * (1.0 - sigmoid_v))
    back = dot_terms(dpre, weight[...], ((1,), (1,)))
    back_first[...] = back[:, :width]
    back_second[...] = back[:, width:]
    grad_out[...] = dot_terms(rows, dpre, ((0,), (0,)))


def dense(place, parts, cotangent, weight):
    rows, width = cotangent.shape
    vmem = pl.BlockSpec(memory_space=pltpu.VMEM)
    return pl.pallas_call(
        functools.partial(dense_kernel, len(parts) // 2),
        in_specs=[pl.BlockSpec(memory_space=pltpu.SMEM)] + [vmem] * (len(parts) + 2),
        out_shape=[
            jax.ShapeDtypeStruct((rows, width), jnp.float32),
            jax.ShapeDtypeStruct((rows, width // 2), jnp.float32),
            jax.ShapeDtypeStruct((rows, width // 2), jnp.float32),
            jax.ShapeDtypeStruct((width, width), jnp.float32),
        ],
        compiler_params=pltpu.CompilerParams(vmem_limit_bytes=VMEM_LIMIT),
        cost_estimate=pl.CostEstimate(
            flops=18 * rows * width * width,
            bytes_accessed=4 * (len(parts) // 2 + 3) * rows * width + 8 * width * width,
            transcendentals=rows * width,
        ),
    )(place, *parts, cotangent, weight)


def along_row(x, bit):
    return lax.ppermute(x, "row", [(i, i ^ bit) for i in range(lax.axis_size("row"))])


def along_col(x, pairs):
    return lax.ppermute(x, "col", pairs)


def plane_gather(own):
    mine = [own] + [along_row(own, bit) for bit in (2, 4, 6)]
    other = [along_row(piece, 1) for piece in mine]
    return [piece for pair in zip(mine, other) for piece in pair]


def plane_reduce(pieces):
    sums = [pieces[p] + along_row(pieces[p + 1], 1) for p in (0, 2, 4, 6)]
    return sums[0] + along_row(sums[1], 2) + along_row(sums[2], 4) + along_row(sums[3], 6)


def line_reduce(slots, edge):
    own, outer, across, inner = slots
    near = along_col(outer, OUTER)
    inward = along_col(inner, INWARD)
    middle = along_col(inner, MIDDLE)
    far = along_col(across + jnp.where(edge, 0.0, near), ACROSS)
    return [own, near, inward, middle, far]


def line_gather(own):
    across = along_col(own, ACROSS)
    near = along_col(own, OUTER)
    middle = along_col(own, MIDDLE)
    outward = along_col(across, OUTWARD)
    return [own, near, across, middle + outward]


def grad_sum(grad):
    me = lax.axis_index("row")
    rows = grad.shape[0]
    for bit in (1, 2, 4):
        rows //= 2
        upper = (me // bit) % 2
        keep = lax.dynamic_slice_in_dim(grad, upper * rows, rows, 0)
        send = lax.dynamic_slice_in_dim(grad, (1 - upper) * rows, rows, 0)
        grad = keep + along_row(send, bit)
    grad = grad + along_col(grad, OUTER)
    grad = grad + along_col(grad, ACROSS)
    for bit in (4, 2, 1):
        upper = (me // bit) % 2
        other = along_row(grad, bit)
        grad = jnp.where(upper == 1, jnp.concatenate([other, grad], axis=0), jnp.concatenate([grad, other], axis=0))
    return grad


def shards(features, weight_matrix, cotangent, block_rows, block_cols, blocks):
    tile = (block_rows[0, 0], block_cols[0, 0], blocks[0, 0])
    size = blocks.shape[-1]
    rows_dev, width = features.shape
    per = rows_dev // size
    count_row, count_col = lax.axis_size("row"), lax.axis_size("col")
    total_nodes = rows_dev * count_row * count_col
    me_row, me_col = lax.axis_index("row"), lax.axis_index("col")
    half = width // 2
    features = (features[:, :half], features[:, half:])

    if (count_row, count_col) == (8, 4):
        edge = (me_col == 0) | (me_col == 3)
        place = jnp.stack([me_row, me_col, jnp.where(edge, 2, 0)]).astype(jnp.int32)
        parts = []
        for own in features:
            slots = spmm(place, *tile, plane_gather(own), [rows_dev] * 4, per, False)
            parts += line_reduce(slots, edge)
        hidden, *backs, grad = dense(place, parts, cotangent, weight_matrix)
        grads = []
        for back in backs:
            sums = spmm(place, *tile, line_gather(back), [rows_dev] * 8, per, True)
            grads.append(plane_reduce(sums))
        grad = grad_sum(grad)
    else:
        place = jnp.zeros((3,), jnp.int32)
        parts = []
        for own in features:
            gathered = lax.all_gather(own, "row", axis=0, tiled=True)
            (partial,) = spmm(place, *tile, [gathered], [rows_dev * count_col], per, False)
            parts.append(lax.psum_scatter(partial, "col", scatter_dimension=0, tiled=True))
        hidden, *backs, grad = dense(place, parts, cotangent, weight_matrix)
        grads = []
        for back in backs:
            gathered = lax.all_gather(back, "col", axis=0, tiled=True)
            (partial,) = spmm(place, *tile, [gathered], [rows_dev * count_row], per, True)
            grads.append(lax.psum_scatter(partial, "row", scatter_dimension=0, tiled=True))
        grad = lax.psum(grad, ("row", "col"))

    weight_grad = grad / jnp.sqrt(jnp.float32(total_nodes))
    return (hidden, weight_grad, jnp.concatenate(grads, axis=1))


def solution(mesh):
    in_specs = (
        P(("col", "row"), None),
        P(),
        P(("row", "col"), None),
        P("row", "col", None),
        P("row", "col", None),
        P("row", "col", None, None, None),
    )
    out_specs = (P(("row", "col"), None), P(), P(("col", "row"), None))
    return jax.shard_map(shards, mesh=mesh, in_specs=in_specs, out_specs=out_specs, check_vma=False)
```

time: 405 us -> 206 us (0.51)
  waiting for transfers between devices: 227 us -> 82.6 us
  matrix products: 65 us -> 0 us
  starting transfers between devices: 0.38 us -> 59.1 us
  Pallas kernels: 0 us -> 45.5 us
  local copies, waits for them, and re-layouts: 47.7 us -> 6.71 us
  other arithmetic: 50.6 us -> 10.2 us
  between operations: 13.8 us -> 1.16 us
    psum x2 -> x0, waiting for transfers between devices: 132 us -> none  [the longest x1 86.4 us: shards(): row_inputs = lax.psum(partial_value, 'col')]
    ppermute x0 -> x52, waiting for transfers between devices: none -> 82.6 us  [the longest x18 49.2 us: along_col(): return lax.ppermute(x, 'col', pairs)]
    dot_general x5 -> x0, matrix products: 65 us -> none  [the longest x2 53.9 us: tile_product(): products = jnp.einsum(form, values, chosen, precision=lax.Precision.HIGHEST)]
    ppermute x0 -> x52, starting transfers between devices: none -> 59.1 us  [the longest x18 29.6 us: along_col(): return lax.ppermute(x, 'col', pairs)]
    reduce_scatter x1 -> x0, waiting for transfers between devices: 54.5 us -> none  [shards(): lax.psum_scatter(grad_part, 'row', scatter_dimension=0, tiled=True)]
    scatter-add x2 -> x0, other arithmetic: 47.2 us -> none  [tile_product(): jnp.zeros((put_count, size_block, width), jnp.float32).at[put_ids]]
    pallas_call x0 -> x5, Pallas kernels: none -> 45.5 us  [the longest x4 42.6 us: spmm(): pl.pallas_call(functools.partial(spmm_kernel, len(pieces), len(out_rows),...]
    all_gather x2 -> x0, waiting for transfers between devices: 39.3 us -> none  [the longest x1 39.3 us: shards(): feature_tile = lax.all_gather(features, 'row', axis=0, tiled=True)]
  transfers between devices with their start and end apart: 5 -> 52, of which waited for: 4 -> 18; matrix products, arithmetic and copies ran while one was open for 37% -> 4% of each run, Pallas kernels for 0% -> 21%
where the time goes in v1:
time: 206 us; the launch traced here: 205 us
  waiting for transfers between devices  82.6 us (40%)
  starting transfers between devices  59.1 us (29%)
  Pallas kernels  45.5 us (22%)
  other arithmetic  10.2 us (5%)
  local copies, waits for them, and re-layouts  6.71 us (3%)
    ppermute x18, waiting for transfers between devices, along_col(): return lax.ppermute(x, 'col', pairs)  49.2 us
    pallas_call x4, Pallas kernels, spmm(): pl.pallas_call(functools.partial(spmm_kernel, len(pieces), len(out_rows),...  42.6 us
    ppermute x34, waiting for transfers between devices, along_row(): lax.ppermute(x, 'row', [(i, i ^ bit) for i in range(lax.axis_size('row'))])  33.4 us
    ppermute x18, starting transfers between devices, along_col(): return lax.ppermute(x, 'col', pairs)  29.6 us
    ppermute x34, starting transfers between devices, along_row(): lax.ppermute(x, 'row', [(i, i ^ bit) for i in range(lax.axis_size('row'))])  29.5 us
    add x6, other arithmetic, plane_reduce(): sums = [pieces[p] + along_row(pieces[p + 1], 1) for p in (0, 2, 4, 6)]  5.62 us
    unnamed x52, local copies, waits for them, and re-layouts  5.61 us
  transfers between devices with their start and end apart: 52, of which 18 were waited for; matrix products, arithmetic and copies ran while one was open for 4% of the time, Pallas kernels for 21%

profile of v1, /device:TPU:0, one launch (start us, length us, event | category | flops | bytes accessed | tf_op | source)
XLA Modules:
  0.0 205.2 jit_solution(10292253949945475346)
XLA Ops:
  0.6 1.1 fusion.1
  1.7 3.0 %collective-permute-start.12 = (f32[512,128]{1,0:T(8,128)S(1)}, f32[512,128]{1,0:T(8,128)S(1)}, u32[]{:S(2)}, u32[]{:S(2)}) collective-permute-start(f32[512,128]{1,0:T(8,128)S(1)} %get-tuple-element.59.refs_0_), channel_id=1, source_target_pairs={{0,8},{4,12},{8,0},{12,4},{16,24},{20,28},{24,16},{28,20},{1,9},{5... | collective-permute-start | bytes 786440 | tf_op jit(solution)/shard_map/ppermute | solution.py:161
  4.7 1.5 collective-permute-start.14
  6.2 1.9 collective-permute-start.1
  8.2 3.6 %collective-permute-done.12.refs_2_ = f32[512,128]{1,0:T(8,128)S(1)} collective-permute-done((f32[512,128]{1,0:T(8,128)S(1)}, f32[512,128]{1,0:T(8,128)S(1)}, u32[]{:S(2)}, u32[]{:S(2)}) %collective-permute-start.12) | collective-permute-done | bytes 262176 | tf_op jit(solution)/shard_map/ppermute | solution.py:161
  11.8 2.1 %collective-permute-start.3 = (f32[512,128]{1,0:T(8,128)S(1)}, f32[512,128]{1,0:T(8,128)S(1)}, u32[]{:S(2)}, u32[]{:S(2)}) collective-permute-start(f32[512,128]{1,0:T(8,128)S(1)} %get-tuple-element.60.refs_0_), channel_id=1, source_target_pairs={{0,16},{4,20},{8,24},{12,28},{16,0},{20,4},{24,8},{28,12},{1,17},{... | collective-permute-start | bytes 786440 | tf_op jit(solution)/shard_map/ppermute | solution.py:161
  13.9 4.5 %collective-permute-done.14.refs_4_ = f32[512,128]{1,0:T(8,128)S(1)} collective-permute-done((f32[512,128]{1,0:T(8,128)S(1)}, f32[512,128]{1,0:T(8,128)S(1)}, u32[]{:S(2)}, u32[]{:S(2)}) %collective-permute-start.14) | collective-permute-done | bytes 262176 | tf_op jit(solution)/shard_map/ppermute | solution.py:161
  19.5 3.6 %collective-permute-done.1.refs_2_ = f32[512,128]{1,0:T(8,128)S(1)} collective-permute-done((f32[512,128]{1,0:T(8,128)S(1)}, f32[512,128]{1,0:T(8,128)S(1)}, u32[]{:S(2)}, u32[]{:S(2)}) %collective-permute-start.1) | collective-permute-done | bytes 262176 | tf_op jit(solution)/shard_map/ppermute | solution.py:161
  23.1 6.2 %collective-permute-done.3.refs_4_ = f32[512,128]{1,0:T(8,128)S(1)} collective-permute-done((f32[512,128]{1,0:T(8,128)S(1)}, f32[512,128]{1,0:T(8,128)S(1)}, u32[]{:S(2)}, u32[]{:S(2)}) %collective-permute-start.3) | collective-permute-done | bytes 262176 | tf_op jit(solution)/shard_map/ppermute | solution.py:161
  32.5 10.2 %shard_map.86 = (f32[512,128]{1,0:T(8,128)S(1)}, f32[512,128]{1,0:T(8,128)S(1)}, f32[512,128]{1,0:T(8,128)S(1)}, f32[512,128]{1,0:T(8,128)S(1)}) custom-call(s32[3]{0:T(128)S(1)} %pad_add_fusion.place, s32[96]{0:T(128)S(1)} %bitcast.6, s32[96]{0:T(128)S(1)} %bitcast.10, f32[96,128,128]{2,1,0:T(8,128)} %bitcast.14, f32[512,128]{1,0:T(8,128)S(1)} %get-tuple-element.59.refs_0_, ...), custom_call_target="tpu_custom_call" | custom-call | flops 1610612736 | bytes 9437184 | tf_op jit(solution)/shard_map/pallas_call | solution.py:93
  42.8 1.6 collective-permute-start.18
  45.9 10.2 %shard_map.85 = (f32[512,128]{1,0:T(8,128)S(1)}, f32[512,128]{1,0:T(8,128)S(1)}, f32[512,128]{1,0:T(8,128)S(1)}, f32[512,128]{1,0:T(8,128)S(1)}) custom-call(s32[3]{0:T(128)S(1)} %pad_add_fusion.place, s32[96]{0:T(128)S(1)} %bitcast.7, s32[96]{0:T(128)S(1)} %bitcast.11, f32[96,128,128]{2,1,0:T(8,128)} %bitcast.15, f32[512,128]{1,0:T(8,128)S(1)} %get-tuple-element.60.refs_0_, ...), custom_call_target="tpu_custom_call" | custom-call | flops 1610612736 | bytes 9437184 | tf_op jit(solution)/shard_map/pallas_call | solution.py:93
  56.7 3.5 %collective-permute-start.19 = (f32[512,128]{1,0:T(8,128)S(1)}, f32[512,128]{1,0:T(8,128)S(1)}, u32[]{:S(2)}, u32[]{:S(2)}) collective-permute-start(f32[512,128]{1,0:T(8,128)S(1)} %get-tuple-element.37), channel_id=1, source_target_pairs={{0,1},{3,2},{4,5},{7,6},{8,9},{11,10},{12,13},{15,14},{16,17},{19,... | collective-permute-start | bytes 786440 | tf_op jit(solution)/shard_map/ppermute | solution.py:165
  60.8 4.1 %collective-permute-start.8 = (f32[512,128]{1,0:T(8,128)S(1)}, f32[512,128]{1,0:T(8,128)S(1)}, u32[]{:S(2)}, u32[]{:S(2)}) collective-permute-start(f32[512,128]{1,0:T(8,128)S(1)} %get-tuple-element.33), channel_id=1, source_target_pairs={{0,1},{3,2},{4,5},{7,6},{8,9},{11,10},{12,13},{15,14},{16,17},{19,... | collective-permute-start | bytes 786440 | tf_op jit(solution)/shard_map/ppermute | solution.py:165
  65.7 2.3 %collective-permute-start.21 = (f32[512,128]{1,0:T(8,128)S(1)}, f32[512,128]{1,0:T(8,128)S(1)}, u32[]{:S(2)}, u32[]{:S(2)}) collective-permute-start(f32[512,128]{1,0:T(8,128)S(1)} %select_add_fusion), channel_id=1, source_target_pairs={{0,2},{1,3},{2,0},{3,1},{4,6},{5,7},{6,4},{7,5},{8,10},{9,11},{10,... | collective-permute-start | bytes 786440 | tf_op jit(solution)/shard_map/ppermute | solution.py:165
  68.0 1.0 collective-permute-done.19.refs_7_
  69.0 4.6 %collective-permute-start.10 = (f32[512,128]{1,0:T(8,128)S(1)}, f32[512,128]{1,0:T(8,128)S(1)}, u32[]{:S(2)}, u32[]{:S(2)}) collective-permute-start(f32[512,128]{1,0:T(8,128)S(1)} %select_add_fusion.1), channel_id=1, source_target_pairs={{0,2},{1,3},{2,0},{3,1},{4,6},{5,7},{6,4},{7,5},{8,10},{9,11},{10,... | collective-permute-start | bytes 786440 | tf_op jit(solution)/shard_map/ppermute | solution.py:165
  73.6 1.0 collective-permute-done.8.refs_2_
  74.7 17.4 %collective-permute-done.21.refs_9_ = f32[512,128]{1,0:T(8,128)S(1)} collective-permute-done((f32[512,128]{1,0:T(8,128)S(1)}, f32[512,128]{1,0:T(8,128)S(1)}, u32[]{:S(2)}, u32[]{:S(2)}) %collective-permute-start.21) | collective-permute-done | bytes 262176 | tf_op jit(solution)/shard_map/ppermute | solution.py:165
  92.1 4.6 %collective-permute-done.10.refs_4_ = f32[512,128]{1,0:T(8,128)S(1)} collective-permute-done((f32[512,128]{1,0:T(8,128)S(1)}, f32[512,128]{1,0:T(8,128)S(1)}, u32[]{:S(2)}, u32[]{:S(2)}) %collective-permute-start.10) | collective-permute-done | bytes 262176 | tf_op jit(solution)/shard_map/ppermute | solution.py:165
  97.4 2.9 %shard_map.87 = (f32[512,256]{1,0:T(8,128)}, f32[512,128]{1,0:T(8,128)S(1)}, f32[512,128]{1,0:T(8,128)S(1)}, f32[256,256]{1,0:T(8,128)S(1)}) custom-call(s32[3]{0:T(128)S(1)} %pad_add_fusion.place, f32[512,128]{1,0:T(8,128)S(1)} %get-tuple-element.31.refs_0_, f32[512,128]{1,0:T(8,128)S(1)} %collective-permute-done.7.refs_1_, ...), custom_call_target="tpu_custom_call" | custom-call | flops 603979776 | bytes 4718592 | tf_op jit(solution)/shard_map/pallas_call | solution.py:142
  100.4 1.3 collective-permute-done.22
  101.8 1.3 collective-permute-start.23
  103.0 3.1 %collective-permute-done.23 = f32[64,256]{1,0:T(8,128)S(1)} collective-permute-done((f32[64,256]{1,0:T(8,128)S(1)}, f32[64,256]{1,0:T(8,128)S(1)}, u32[]{:S(2)}, u32[]{:S(2)}) %collective-permute-start.23) | collective-permute-done | bytes 65568 | tf_op jit(solution)/shard_map/ppermute | solution.py:161
  106.1 1.6 collective-permute-start.24
  108.4 1.4 collective-permute-start.30
  109.8 1.7 collective-permute-start.42
  111.5 8.1 %collective-permute-done.31.refs_2_ = f32[512,128]{1,0:T(8,128)S(1)} collective-permute-done((f32[512,128]{1,0:T(8,128)S(1)}, f32[512,128]{1,0:T(8,128)S(1)}, u32[]{:S(2)}, u32[]{:S(2)}) %collective-permute-start.31) | collective-permute-done | bytes 262176 | tf_op jit(solution)/shard_map/ppermute | solution.py:165
  119.6 1.3 collective-permute-start.33
  120.9 2.7 %collective-permute-start.25 = (f32[32,256]{1,0:T(8,128)S(1)}, f32[32,256]{1,0:T(8,128)S(1)}, u32[]{:S(2)}, u32[]{:S(2)}) collective-permute-start(f32[32,256]{1,0:T(8,128)S(1)} %dynamic-slice_add_fusion.2), channel_id=1, source_target_pairs={{0,1},{1,0},{2,3},{3,2},{4,5},{5,4},{6,7},{7,6},{8,9},{9,8},{10,11... | collective-permute-start | bytes 98312 | tf_op jit(solution)/shard_map/ppermute | solution.py:165
  123.7 12.2 %collective-permute-done.25 = f32[32,256]{1,0:T(8,128)S(1)} collective-permute-done((f32[32,256]{1,0:T(8,128)S(1)}, f32[32,256]{1,0:T(8,128)S(1)}, u32[]{:S(2)}, u32[]{:S(2)}) %collective-permute-start.25) | collective-permute-done | bytes 32800 | tf_op jit(solution)/shard_map/ppermute | solution.py:165
  135.9 4.8 %collective-permute-done.26 = f32[32,256]{1,0:T(8,128)S(1)} collective-permute-done((f32[32,256]{1,0:T(8,128)S(1)}, f32[32,256]{1,0:T(8,128)S(1)}, u32[]{:S(2)}, u32[]{:S(2)}) %collective-permute-start.26) | collective-permute-done | bytes 32800 | tf_op jit(solution)/shard_map/ppermute | solution.py:165
  142.2 1.9 collective-permute-start.41
  144.6 1.3 collective-permute-start.44
  145.9 1.4 collective-permute-start.28
  148.7 11.1 %shard_map.88 = (f32[512,128]{1,0:T(8,128)S(1)}, f32[512,128]{1,0:T(8,128)S(1)}, f32[512,128]{1,0:T(8,128)S(1)}, f32[512,128]{1,0:T(8,128)}, f32[512,128]{1,0:T(...) custom-call(s32[3]{0:T(128)S(1)} %pad_add_fusion.place, s32[96]{0:T(128)S(1)} %bitcast.8, ...), custom_call_target="tpu_custom_call" | custom-call | flops 1610612736 | bytes 9437184 | tf_op jit(solution)/shard_map/pallas_call | solution.py:93
  161.9 11.0 %shard_map.89 = (f32[512,128]{1,0:T(8,128)S(1)}, f32[512,128]{1,0:T(8,128)S(1)}, f32[512,128]{1,0:T(8,128)S(1)}, f32[512,128]{1,0:T(8,128)}, f32[512,128]{1,0:T(...) custom-call(s32[3]{0:T(128)S(1)} %pad_add_fusion.place, s32[96]{0:T(128)S(1)} %bitcast.9, ...), custom_call_target="tpu_custom_call" | custom-call | flops 1610612736 | bytes 9437184 | tf_op jit(solution)/shard_map/pallas_call | solution.py:93
  173.9 1.7 add.121
  175.7 1.0 add.123
  177.2 1.0 add.125
  179.8 1.9 collective-permute-start.40
  183.4 1.0 add.131
  185.3 2.4 %collective-permute-done.36 = f32[512,128]{1,0:T(8,128)} collective-permute-done((f32[512,128]{1,0:T(8,128)}, f32[512,128]{1,0:T(8,128)}, u32[]{:S(2)}, u32[]{:S(2)}) %collective-permute-start.36) | collective-permute-done | bytes 262176 | tf_op jit(solution)/shard_map/ppermute | solution.py:161
  187.7 1.2 collective-permute-start.49
  188.9 6.1 %collective-permute-start.51 = (f32[512,128]{1,0:T(8,128)S(1)}, f32[512,128]{1,0:T(8,128)S(1)}, u32[]{:S(2)}, u32[]{:S(2)}) collective-permute-start(f32[512,128]{1,0:T(8,128)S(1)} %add.133), channel_id=1, source_target_pairs={{0,24},{4,28},{8,16},{12,20},{16,8},{20,12},{24,0},{28,4},{1,25},{... | collective-permute-start | bytes 786440 | tf_op jit(solution)/shard_map/ppermute | solution.py:161
  195.0 1.2 add_add_fusion.1
  196.1 2.8 %collective-permute-done.47 = f32[512,128]{1,0:T(8,128)S(1)} collective-permute-done((f32[512,128]{1,0:T(8,128)S(1)}, f32[512,128]{1,0:T(8,128)S(1)}, u32[]{:S(2)}, u32[]{:S(2)}) %collective-permute-start.47) | collective-permute-done | bytes 262176 | tf_op jit(solution)/shard_map/ppermute | solution.py:161
  199.4 4.8 %collective-permute-done.51 = f32[512,128]{1,0:T(8,128)S(1)} collective-permute-done((f32[512,128]{1,0:T(8,128)S(1)}, f32[512,128]{1,0:T(8,128)S(1)}, u32[]{:S(2)}, u32[]{:S(2)}) %collective-permute-start.51) | collective-permute-done | bytes 262176 | tf_op jit(solution)/shard_map/ppermute | solution.py:161
  (139 shorter events, 22.0 us)
Async XLA Ops:
  1.7 10.1 %collective-permute-start.12 = (f32[512,128]{1,0:T(8,128)S(1)}, f32[512,128]{1,0:T(8,128)S(1)}, u32[]{:S(2)}, u32[]{:S(2)}) collective-permute-start(f32[512,128]{1,0:T(8,128)S(1)} %get-tuple-element.59.refs_0_), channel_id=1, source_target_pairs={{0,8},{4,12},{8,0},{12,4},{16,24},{20,28},{24,16},{28,20},{1,9},{5... | collective-permute-start | bytes 786440 | tf_op jit(solution)/shard_map/ppermute | solution.py:161
  4.7 13.8 %collective-permute-start.14 = (f32[512,128]{1,0:T(8,128)S(1)}, f32[512,128]{1,0:T(8,128)S(1)}, u32[]{:S(2)}, u32[]{:S(2)}) collective-permute-start(f32[512,128]{1,0:T(8,128)S(1)} %get-tuple-element.59.refs_0_), channel_id=1, source_target_pairs={{0,16},{4,20},{8,24},{12,28},{16,0},{20,4},{24,8},{28,12},{1,17},{... | collective-permute-start | bytes 786440 | tf_op jit(solution)/shard_map/ppermute | solution.py:161
  6.2 12.8 %collective-permute-start.16 = (f32[512,128]{1,0:T(8,128)S(1)}, f32[512,128]{1,0:T(8,128)S(1)}, u32[]{:S(2)}, u32[]{:S(2)}) collective-permute-start(f32[512,128]{1,0:T(8,128)S(1)} %get-tuple-element.59.refs_0_), channel_id=1, source_target_pairs={{0,24},{4,28},{8,16},{12,20},{16,8},{20,12},{24,0},{28,4},{1,25},{... | collective-permute-start | bytes 786440 | tf_op jit(solution)/shard_map/ppermute | solution.py:161
  6.2 12.8 %collective-permute-start.11 = (f32[512,128]{1,0:T(8,128)S(1)}, f32[512,128]{1,0:T(8,128)S(1)}, u32[]{:S(2)}, u32[]{:S(2)}) collective-permute-start(f32[512,128]{1,0:T(8,128)S(1)} %get-tuple-element.59.refs_0_), channel_id=1, source_target_pairs={{0,4},{4,0},{8,12},{12,8},{16,20},{20,16},{24,28},{28,24},{1,5},{5... | collective-permute-start | bytes 786440 | tf_op jit(solution)/shard_map/ppermute | solution.py:161
  6.2 16.9 %collective-permute-start.1 = (f32[512,128]{1,0:T(8,128)S(1)}, f32[512,128]{1,0:T(8,128)S(1)}, u32[]{:S(2)}, u32[]{:S(2)}) collective-permute-start(f32[512,128]{1,0:T(8,128)S(1)} %get-tuple-element.60.refs_0_), channel_id=1, source_target_pairs={{0,8},{4,12},{8,0},{12,4},{16,24},{20,28},{24,16},{28,20},{1,9},{5... | collective-permute-start | bytes 786440 | tf_op jit(solution)/shard_map/ppermute | solution.py:161
  11.8 17.5 %collective-permute-start.3 = (f32[512,128]{1,0:T(8,128)S(1)}, f32[512,128]{1,0:T(8,128)S(1)}, u32[]{:S(2)}, u32[]{:S(2)}) collective-permute-start(f32[512,128]{1,0:T(8,128)S(1)} %get-tuple-element.60.refs_0_), channel_id=1, source_target_pairs={{0,16},{4,20},{8,24},{12,28},{16,0},{20,4},{24,8},{28,12},{1,17},{... | collective-permute-start | bytes 786440 | tf_op jit(solution)/shard_map/ppermute | solution.py:161
  18.5 10.9 %collective-permute-start.5 = (f32[512,128]{1,0:T(8,128)S(1)}, f32[512,128]{1,0:T(8,128)S(1)}, u32[]{:S(2)}, u32[]{:S(2)}) collective-permute-start(f32[512,128]{1,0:T(8,128)S(1)} %get-tuple-element.60.refs_0_), channel_id=1, source_target_pairs={{0,24},{4,28},{8,16},{12,20},{16,8},{20,12},{24,0},{28,4},{1,25},{... | collective-permute-start | bytes 786440 | tf_op jit(solution)/shard_map/ppermute | solution.py:161
  19.0 10.8 %collective-permute-start.13 = (f32[512,128]{1,0:T(8,128)S(1)}, f32[512,128]{1,0:T(8,128)S(1)}, u32[]{:S(2)}, u32[]{:S(2)}) collective-permute-start(f32[512,128]{1,0:T(8,128)S(1)} %collective-permute-done.12.refs_2_), channel_id=1, source_target_pairs={{0,4},{4,0},{8,12},{12,8},{16,20},{20,16},{24,28},{28,24},{1,5},{5... | collective-permute-start | bytes 786440 | tf_op jit(solution)/shard_map/ppermute | solution.py:161
  19.0 10.9 %collective-permute-start.15 = (f32[512,128]{1,0:T(8,128)S(1)}, f32[512,128]{1,0:T(8,128)S(1)}, u32[]{:S(2)}, u32[]{:S(2)}) collective-permute-start(f32[512,128]{1,0:T(8,128)S(1)} %collective-permute-done.14.refs_4_), channel_id=1, source_target_pairs={{0,4},{4,0},{8,12},{12,8},{16,20},{20,16},{24,28},{28,24},{1,5},{5... | collective-permute-start | bytes 786440 | tf_op jit(solution)/shard_map/ppermute | solution.py:161
  23.1 7.3 %collective-permute-start.17 = (f32[512,128]{1,0:T(8,128)S(1)}, f32[512,128]{1,0:T(8,128)S(1)}, u32[]{:S(2)}, u32[]{:S(2)}) collective-permute-start(f32[512,128]{1,0:T(8,128)S(1)} %collective-permute-done.16.refs_6_), channel_id=1, source_target_pairs={{0,4},{4,0},{8,12},{12,8},{16,20},{20,16},{24,28},{28,24},{1,5},{5... | collective-permute-start | bytes 786440 | tf_op jit(solution)/shard_map/ppermute | solution.py:161
  29.3 15.1 %collective-permute-start = (f32[512,128]{1,0:T(8,128)S(1)}, f32[512,128]{1,0:T(8,128)S(1)}, u32[]{:S(2)}, u32[]{:S(2)}) collective-permute-start(f32[512,128]{1,0:T(8,128)S(1)} %get-tuple-element.60.refs_0_), channel_id=1, source_target_pairs={{0,4},{4,0},{8,12},{12,8},{16,20},{20,16},{24,28},{28,24},{1,5},{5... | collective-permute-start | bytes 786440 | tf_op jit(solution)/shard_map/ppermute | solution.py:161
  29.3 15.1 %collective-permute-start.2 = (f32[512,128]{1,0:T(8,128)S(1)}, f32[512,128]{1,0:T(8,128)S(1)}, u32[]{:S(2)}, u32[]{:S(2)}) collective-permute-start(f32[512,128]{1,0:T(8,128)S(1)} %collective-permute-done.1.refs_2_), channel_id=1, source_target_pairs={{0,4},{4,0},{8,12},{12,8},{16,20},{20,16},{24,28},{28,24},{1,5},{5... | collective-permute-start | bytes 786440 | tf_op jit(solution)/shard_map/ppermute | solution.py:161
  29.8 14.6 %collective-permute-start.4 = (f32[512,128]{1,0:T(8,128)S(1)}, f32[512,128]{1,0:T(8,128)S(1)}, u32[]{:S(2)}, u32[]{:S(2)}) collective-permute-start(f32[512,128]{1,0:T(8,128)S(1)} %collective-permute-done.3.refs_4_), channel_id=1, source_target_pairs={{0,4},{4,0},{8,12},{12,8},{16,20},{20,16},{24,28},{28,24},{1,5},{5... | collective-permute-start | bytes 786440 | tf_op jit(solution)/shard_map/ppermute | solution.py:161
  29.9 14.5 %collective-permute-start.6 = (f32[512,128]{1,0:T(8,128)S(1)}, f32[512,128]{1,0:T(8,128)S(1)}, u32[]{:S(2)}, u32[]{:S(2)}) collective-permute-start(f32[512,128]{1,0:T(8,128)S(1)} %collective-permute-done.5.refs_6_), channel_id=1, source_target_pairs={{0,4},{4,0},{8,12},{12,8},{16,20},{20,16},{24,28},{28,24},{1,5},{5... | collective-permute-start | bytes 786440 | tf_op jit(solution)/shard_map/ppermute | solution.py:161
  42.8 22.2 %collective-permute-start.18 = (f32[512,128]{1,0:T(8,128)S(1)}, f32[512,128]{1,0:T(8,128)S(1)}, u32[]{:S(2)}, u32[]{:S(2)}) collective-permute-start(f32[512,128]{1,0:T(8,128)S(1)} %get-tuple-element.36), channel_id=1, source_target_pairs={{0,1},{1,0},{2,3},{3,2},{4,5},{5,4},{6,7},{7,6},{8,9},{9,8},{10,11... | collective-permute-start | bytes 786440 | tf_op jit(solution)/shard_map/ppermute | solution.py:165
  56.2 9.6 %collective-permute-start.7 = (f32[512,128]{1,0:T(8,128)S(1)}, f32[512,128]{1,0:T(8,128)S(1)}, u32[]{:S(2)}, u32[]{:S(2)}) collective-permute-start(f32[512,128]{1,0:T(8,128)S(1)} %get-tuple-element.32), channel_id=1, source_target_pairs={{0,1},{1,0},{2,3},{3,2},{4,5},{5,4},{6,7},{7,6},{8,9},{9,8},{10,11... | collective-permute-start | bytes 786440 | tf_op jit(solution)/shard_map/ppermute | solution.py:165
  56.7 12.3 %collective-permute-start.19 = (f32[512,128]{1,0:T(8,128)S(1)}, f32[512,128]{1,0:T(8,128)S(1)}, u32[]{:S(2)}, u32[]{:S(2)}) collective-permute-start(f32[512,128]{1,0:T(8,128)S(1)} %get-tuple-element.37), channel_id=1, source_target_pairs={{0,1},{3,2},{4,5},{7,6},{8,9},{11,10},{12,13},{15,14},{16,17},{19,... | collective-permute-start | bytes 786440 | tf_op jit(solution)/shard_map/ppermute | solution.py:165
  60.2 13.5 %collective-permute-start.20 = (f32[512,128]{1,0:T(8,128)S(1)}, f32[512,128]{1,0:T(8,128)S(1)}, u32[]{:S(2)}, u32[]{:S(2)}) collective-permute-start(f32[512,128]{1,0:T(8,128)S(1)} %get-tuple-element.37), channel_id=1, source_target_pairs={{1,2},{2,1},{5,6},{6,5},{9,10},{10,9},{13,14},{14,13},{17,18},{18,... | collective-permute-start | bytes 786440 | tf_op jit(solution)/shard_map/ppermute | solution.py:165
  60.8 13.8 %collective-permute-start.8 = (f32[512,128]{1,0:T(8,128)S(1)}, f32[512,128]{1,0:T(8,128)S(1)}, u32[]{:S(2)}, u32[]{:S(2)}) collective-permute-start(f32[512,128]{1,0:T(8,128)S(1)} %get-tuple-element.33), channel_id=1, source_target_pairs={{0,1},{3,2},{4,5},{7,6},{8,9},{11,10},{12,13},{15,14},{16,17},{19,... | collective-permute-start | bytes 786440 | tf_op jit(solution)/shard_map/ppermute | solution.py:165
  65.0 9.7 %collective-permute-start.9 = (f32[512,128]{1,0:T(8,128)S(1)}, f32[512,128]{1,0:T(8,128)S(1)}, u32[]{:S(2)}, u32[]{:S(2)}) collective-permute-start(f32[512,128]{1,0:T(8,128)S(1)} %get-tuple-element.33), channel_id=1, source_target_pairs={{1,2},{2,1},{5,6},{6,5},{9,10},{10,9},{13,14},{14,13},{17,18},{18,... | collective-permute-start | bytes 786440 | tf_op jit(solution)/shard_map/ppermute | solution.py:165
  65.7 26.3 %collective-permute-start.21 = (f32[512,128]{1,0:T(8,128)S(1)}, f32[512,128]{1,0:T(8,128)S(1)}, u32[]{:S(2)}, u32[]{:S(2)}) collective-permute-start(f32[512,128]{1,0:T(8,128)S(1)} %select_add_fusion), channel_id=1, source_target_pairs={{0,2},{1,3},{2,0},{3,1},{4,6},{5,7},{6,4},{7,5},{8,10},{9,11},{10,... | collective-permute-start | bytes 786440 | tf_op jit(solution)/shard_map/ppermute | solution.py:165
  69.0 27.7 %collective-permute-start.10 = (f32[512,128]{1,0:T(8,128)S(1)}, f32[512,128]{1,0:T(8,128)S(1)}, u32[]{:S(2)}, u32[]{:S(2)}) collective-permute-start(f32[512,128]{1,0:T(8,128)S(1)} %select_add_fusion.1), channel_id=1, source_target_pairs={{0,2},{1,3},{2,0},{3,1},{4,6},{5,7},{6,4},{7,5},{8,10},{9,11},{10,... | collective-permute-start | bytes 786440 | tf_op jit(solution)/shard_map/ppermute | solution.py:165
  103.0 16.6 %collective-permute-start.31 = (f32[512,128]{1,0:T(8,128)S(1)}, f32[512,128]{1,0:T(8,128)S(1)}, u32[]{:S(2)}, u32[]{:S(2)}) collective-permute-start(f32[512,128]{1,0:T(8,128)S(1)} %get-tuple-element.41.refs_0_), channel_id=1, source_target_pairs={{0,2},{1,3},{2,0},{3,1},{4,6},{5,7},{6,4},{7,5},{8,10},{9,11},{10,... | collective-permute-start | bytes 786440 | tf_op jit(solution)/shard_map/ppermute | solution.py:165
  106.1 14.8 %collective-permute-start.24 = (f32[32,256]{1,0:T(8,128)S(1)}, f32[32,256]{1,0:T(8,128)S(1)}, u32[]{:S(2)}, u32[]{:S(2)}) collective-permute-start(f32[32,256]{1,0:T(8,128)S(1)} %constant_dynamic-slice_fusion), channel_id=1, source_target_pairs={{0,16},{4,20},{8,24},{12,28},{16,0},{20,4},{24,8},{28,12},{1,17},{... | collective-permute-start | bytes 98312 | tf_op jit(solution)/shard_map/ppermute | solution.py:161
  107.7 33.8 %collective-permute-start.32 = (f32[512,128]{1,0:T(8,128)S(1)}, f32[512,128]{1,0:T(8,128)S(1)}, u32[]{:S(2)}, u32[]{:S(2)}) collective-permute-start(f32[512,128]{1,0:T(8,128)S(1)} %get-tuple-element.41.refs_0_), channel_id=1, source_target_pairs={{1,2},{2,1},{5,6},{6,5},{9,10},{10,9},{13,14},{14,13},{17,18},{18,... | collective-permute-start | bytes 786440 | tf_op jit(solution)/shard_map/ppermute | solution.py:165
  108.4 39.6 %collective-permute-start.30 = (f32[512,128]{1,0:T(8,128)S(1)}, f32[512,128]{1,0:T(8,128)S(1)}, u32[]{:S(2)}, u32[]{:S(2)}) collective-permute-start(f32[512,128]{1,0:T(8,128)S(1)} %get-tuple-element.41.refs_0_), channel_id=1, source_target_pairs={{0,1},{1,0},{2,3},{3,2},{4,5},{5,4},{6,7},{7,6},{8,9},{9,8},{10,11... | collective-permute-start | bytes 786440 | tf_op jit(solution)/shard_map/ppermute | solution.py:165
  109.8 32.4 %collective-permute-start.42 = (f32[512,128]{1,0:T(8,128)S(1)}, f32[512,128]{1,0:T(8,128)S(1)}, u32[]{:S(2)}, u32[]{:S(2)}) collective-permute-start(f32[512,128]{1,0:T(8,128)S(1)} %get-tuple-element.50.refs_0_), channel_id=1, source_target_pairs={{0,2},{1,3},{2,0},{3,1},{4,6},{5,7},{6,4},{7,5},{8,10},{9,11},{10,... | collective-permute-start | bytes 786440 | tf_op jit(solution)/shard_map/ppermute | solution.py:165
  119.6 26.3 %collective-permute-start.33 = (f32[512,128]{1,0:T(8,128)S(1)}, f32[512,128]{1,0:T(8,128)S(1)}, u32[]{:S(2)}, u32[]{:S(2)}) collective-permute-start(f32[512,128]{1,0:T(8,128)S(1)} %collective-permute-done.31.refs_2_), channel_id=1, source_target_pairs={{1,0},{2,3},{5,4},{6,7},{9,8},{10,11},{13,12},{14,15},{17,16},{18,... | collective-permute-start | bytes 786440 | tf_op jit(solution)/shard_map/ppermute | solution.py:165
  120.9 14.9 %collective-permute-start.25 = (f32[32,256]{1,0:T(8,128)S(1)}, f32[32,256]{1,0:T(8,128)S(1)}, u32[]{:S(2)}, u32[]{:S(2)}) collective-permute-start(f32[32,256]{1,0:T(8,128)S(1)} %dynamic-slice_add_fusion.2), channel_id=1, source_target_pairs={{0,1},{1,0},{2,3},{3,2},{4,5},{5,4},{6,7},{7,6},{8,9},{9,8},{10,11... | collective-permute-start | bytes 98312 | tf_op jit(solution)/shard_map/ppermute | solution.py:165
  135.9 4.8 %collective-permute-start.26 = (f32[32,256]{1,0:T(8,128)S(1)}, f32[32,256]{1,0:T(8,128)S(1)}, u32[]{:S(2)}, u32[]{:S(2)}) collective-permute-start(f32[32,256]{1,0:T(8,128)S(1)} %add.117), channel_id=1, source_target_pairs={{0,2},{1,3},{2,0},{3,1},{4,6},{5,7},{6,4},{7,5},{8,10},{9,11},{10,... | collective-permute-start | bytes 98312 | tf_op jit(solution)/shard_map/ppermute | solution.py:165
  141.5 18.3 %collective-permute-start.43 = (f32[512,128]{1,0:T(8,128)S(1)}, f32[512,128]{1,0:T(8,128)S(1)}, u32[]{:S(2)}, u32[]{:S(2)}) collective-permute-start(f32[512,128]{1,0:T(8,128)S(1)} %get-tuple-element.50.refs_0_), channel_id=1, source_target_pairs={{1,2},{2,1},{5,6},{6,5},{9,10},{10,9},{13,14},{14,13},{17,18},{18,... | collective-permute-start | bytes 786440 | tf_op jit(solution)/shard_map/ppermute | solution.py:165
  142.2 18.9 %collective-permute-start.41 = (f32[512,128]{1,0:T(8,128)S(1)}, f32[512,128]{1,0:T(8,128)S(1)}, u32[]{:S(2)}, u32[]{:S(2)}) collective-permute-start(f32[512,128]{1,0:T(8,128)S(1)} %get-tuple-element.50.refs_0_), channel_id=1, source_target_pairs={{0,1},{1,0},{2,3},{3,2},{4,5},{5,4},{6,7},{7,6},{8,9},{9,8},{10,11... | collective-permute-start | bytes 786440 | tf_op jit(solution)/shard_map/ppermute | solution.py:165
  144.6 15.7 %collective-permute-start.44 = (f32[512,128]{1,0:T(8,128)S(1)}, f32[512,128]{1,0:T(8,128)S(1)}, u32[]{:S(2)}, u32[]{:S(2)}) collective-permute-start(f32[512,128]{1,0:T(8,128)S(1)} %collective-permute-done.42.refs_2_), channel_id=1, source_target_pairs={{1,0},{2,3},{5,4},{6,7},{9,8},{10,11},{13,12},{14,15},{17,16},{18,... | collective-permute-start | bytes 786440 | tf_op jit(solution)/shard_map/ppermute | solution.py:165
  145.9 27.4 %collective-permute-start.28 = (f32[64,256]{1,0:T(8,128)S(1)}, f32[64,256]{1,0:T(8,128)S(1)}, u32[]{:S(2)}, u32[]{:S(2)}) collective-permute-start(f32[64,256]{1,0:T(8,128)S(1)} %maximum_select_fusion.2), channel_id=1, source_target_pairs={{0,8},{4,12},{8,0},{12,4},{16,24},{20,28},{24,16},{28,20},{1,9},{5... | collective-permute-start | bytes 196616 | tf_op jit(solution)/shard_map/ppermute | solution.py:161
  159.8 13.6 %collective-permute-start.35 = (f32[512,128]{1,0:T(8,128)}, f32[512,128]{1,0:T(8,128)}, u32[]{:S(2)}, u32[]{:S(2)}) collective-permute-start(f32[512,128]{1,0:T(8,128)} %get-tuple-element.45), channel_id=1, source_target_pairs={{0,4},{4,0},{8,12},{12,8},{16,20},{20,16},{24,28},{28,24},{1,5},{5... | collective-permute-start | bytes 786440 | tf_op jit(solution)/shard_map/ppermute | solution.py:161
  159.8 15.8 %collective-permute-start.37 = (f32[512,128]{1,0:T(8,128)S(1)}, f32[512,128]{1,0:T(8,128)}, u32[]{:S(2)}, u32[]{:S(2)}) collective-permute-start(f32[512,128]{1,0:T(8,128)S(1)} %get-tuple-element.47), channel_id=1, source_target_pairs={{0,4},{4,0},{8,12},{12,8},{16,20},{20,16},{24,28},{28,24},{1,5},{5... | collective-permute-start | bytes 786440 | tf_op jit(solution)/shard_map/ppermute | solution.py:161
  160.3 16.4 %collective-permute-start.39 = (f32[512,128]{1,0:T(8,128)}, f32[512,128]{1,0:T(8,128)}, u32[]{:S(2)}, u32[]{:S(2)}) collective-permute-start(f32[512,128]{1,0:T(8,128)} %get-tuple-element.49), channel_id=1, source_target_pairs={{0,4},{4,0},{8,12},{12,8},{16,20},{20,16},{24,28},{28,24},{1,5},{5... | collective-permute-start | bytes 786440 | tf_op jit(solution)/shard_map/ppermute | solution.py:161
  172.9 6.1 %collective-permute-start.46 = (f32[512,128]{1,0:T(8,128)}, f32[512,128]{1,0:T(8,128)}, u32[]{:S(2)}, u32[]{:S(2)}) collective-permute-start(f32[512,128]{1,0:T(8,128)} %get-tuple-element.54), channel_id=1, source_target_pairs={{0,4},{4,0},{8,12},{12,8},{16,20},{20,16},{24,28},{28,24},{1,5},{5... | collective-permute-start | bytes 786440 | tf_op jit(solution)/shard_map/ppermute | solution.py:161
  173.3 6.5 %collective-permute-start.48 = (f32[512,128]{1,0:T(8,128)S(1)}, f32[512,128]{1,0:T(8,128)}, u32[]{:S(2)}, u32[]{:S(2)}) collective-permute-start(f32[512,128]{1,0:T(8,128)S(1)} %get-tuple-element.56), channel_id=1, source_target_pairs={{0,4},{4,0},{8,12},{12,8},{16,20},{20,16},{24,28},{28,24},{1,5},{5... | collective-permute-start | bytes 786440 | tf_op jit(solution)/shard_map/ppermute | solution.py:161
  175.6 8.8 %collective-permute-start.50 = (f32[512,128]{1,0:T(8,128)}, f32[512,128]{1,0:T(8,128)S(1)}, u32[]{:S(2)}, u32[]{:S(2)}) collective-permute-start(f32[512,128]{1,0:T(8,128)} %get-tuple-element.58), channel_id=1, source_target_pairs={{0,4},{4,0},{8,12},{12,8},{16,20},{20,16},{24,28},{28,24},{1,5},{5... | collective-permute-start | bytes 786440 | tf_op jit(solution)/shard_map/ppermute | solution.py:161
  176.7 7.9 %collective-permute-start.34 = (f32[512,128]{1,0:T(8,128)S(1)}, f32[512,128]{1,0:T(8,128)}, u32[]{:S(2)}, u32[]{:S(2)}) collective-permute-start(f32[512,128]{1,0:T(8,128)S(1)} %get-tuple-element.43), channel_id=1, source_target_pairs={{0,4},{4,0},{8,12},{12,8},{16,20},{20,16},{24,28},{28,24},{1,5},{5... | collective-permute-start | bytes 786440 | tf_op jit(solution)/shard_map/ppermute | solution.py:161
  178.2 9.5 %collective-permute-start.36 = (f32[512,128]{1,0:T(8,128)}, f32[512,128]{1,0:T(8,128)}, u32[]{:S(2)}, u32[]{:S(2)}) collective-permute-start(f32[512,128]{1,0:T(8,128)} %add.121), channel_id=1, source_target_pairs={{0,8},{4,12},{8,0},{12,4},{16,24},{20,28},{24,16},{28,20},{1,9},{5... | collective-permute-start | bytes 786440 | tf_op jit(solution)/shard_map/ppermute | solution.py:161
  178.9 9.9 %collective-permute-start.38 = (f32[512,128]{1,0:T(8,128)S(1)}, f32[512,128]{1,0:T(8,128)}, u32[]{:S(2)}, u32[]{:S(2)}) collective-permute-start(f32[512,128]{1,0:T(8,128)S(1)} %add.123), channel_id=1, source_target_pairs={{0,16},{4,20},{8,24},{12,28},{16,0},{20,4},{24,8},{28,12},{1,17},{... | collective-permute-start | bytes 786440 | tf_op jit(solution)/shard_map/ppermute | solution.py:161
  179.8 15.2 %collective-permute-start.40 = (f32[512,128]{1,0:T(8,128)S(1)}, f32[512,128]{1,0:T(8,128)S(1)}, u32[]{:S(2)}, u32[]{:S(2)}) collective-permute-start(f32[512,128]{1,0:T(8,128)S(1)} %add.125), channel_id=1, source_target_pairs={{0,24},{4,28},{8,16},{12,20},{16,8},{20,12},{24,0},{28,4},{1,25},{... | collective-permute-start | bytes 786440 | tf_op jit(solution)/shard_map/ppermute | solution.py:161
  184.4 11.7 %collective-permute-start.45 = (f32[512,128]{1,0:T(8,128)S(1)}, f32[512,128]{1,0:T(8,128)S(1)}, u32[]{:S(2)}, u32[]{:S(2)}) collective-permute-start(f32[512,128]{1,0:T(8,128)S(1)} %get-tuple-element.52), channel_id=1, source_target_pairs={{0,4},{4,0},{8,12},{12,8},{16,20},{20,16},{24,28},{28,24},{1,5},{5... | collective-permute-start | bytes 786440 | tf_op jit(solution)/shard_map/ppermute | solution.py:161
  184.6 14.3 %collective-permute-start.47 = (f32[512,128]{1,0:T(8,128)S(1)}, f32[512,128]{1,0:T(8,128)S(1)}, u32[]{:S(2)}, u32[]{:S(2)}) collective-permute-start(f32[512,128]{1,0:T(8,128)S(1)} %add.129), channel_id=1, source_target_pairs={{0,8},{4,12},{8,0},{12,4},{16,24},{20,28},{24,16},{28,20},{1,9},{5... | collective-permute-start | bytes 786440 | tf_op jit(solution)/shard_map/ppermute | solution.py:161
  187.7 11.7 %collective-permute-start.49 = (f32[512,128]{1,0:T(8,128)S(1)}, f32[512,128]{1,0:T(8,128)S(1)}, u32[]{:S(2)}, u32[]{:S(2)}) collective-permute-start(f32[512,128]{1,0:T(8,128)S(1)} %add.131), channel_id=1, source_target_pairs={{0,16},{4,20},{8,24},{12,28},{16,0},{20,4},{24,8},{28,12},{1,17},{... | collective-permute-start | bytes 786440 | tf_op jit(solution)/shard_map/ppermute | solution.py:161
  188.9 15.4 %collective-permute-start.51 = (f32[512,128]{1,0:T(8,128)S(1)}, f32[512,128]{1,0:T(8,128)S(1)}, u32[]{:S(2)}, u32[]{:S(2)}) collective-permute-start(f32[512,128]{1,0:T(8,128)S(1)} %add.133), channel_id=1, source_target_pairs={{0,24},{4,28},{8,16},{12,20},{16,8},{20,12},{24,0},{28,4},{1,25},{... | collective-permute-start | bytes 786440 | tf_op jit(solution)/shard_map/ppermute | solution.py:161
  (30 other events, 556.4 us)

commit v2 on v0

v2 whole, which is shorter than its diff:
```python
import functools

import jax
import jax.numpy as jnp
from jax import lax
from jax.experimental import pallas as pl
from jax.experimental.pallas import tpu as pltpu
from jax.sharding import PartitionSpec as P

VMEM_LIMIT = 52 * 1024 * 1024

OUTER = ((0, 1), (1, 0), (2, 3), (3, 2))
MIDDLE = ((1, 2), (2, 1))
INWARD = ((0, 1), (3, 2))
OUTWARD = ((1, 0), (2, 3))
ACROSS = ((0, 2), (1, 3), (2, 0), (3, 1))
REVERSED = ((0, 3), (1, 2), (2, 1), (3, 0))
ENDS_ACROSS = ((0, 2), (3, 1), (1, 0), (2, 3))
ENDS_INWARD = ((2, 0), (1, 3), (0, 1), (3, 2))


def two_terms(x):
    high = x.astype(jnp.bfloat16)
    low = (x - high.astype(jnp.float32)).astype(jnp.bfloat16)
    return high, low


def dot_terms(left, right, dims):
    left_high, left_low = two_terms(left)
    right_high, right_low = two_terms(right)
    dot = functools.partial(
        lax.dot_general, dimension_numbers=(dims, ((), ())), preferred_element_type=jnp.float32
    )
    return dot(left_high, right_high) + (dot(left_high, right_low) + dot(left_low, right_high))


def row_slot(block, place, per, gathered):
    group = (block // per) ^ place[1]
    if gathered:
        group = group ^ (place[3] * ((group ^ (group >> 1)) & 1))
    else:
        group = group ^ (place[2] * (group & 1))
    return group * per + block % per


def col_slot(block, place, per):
    return ((block // per) ^ place[0]) * per + block % per


def spmm_kernel(groups, only, has_base, count_out, steps, unroll, per, transposed, ids, values_hbm, *refs):
    count_in = sum(groups)
    pieces, refs = refs[:count_in], refs[count_in:]
    base, refs = (refs[0], refs[1:]) if has_base else (None, refs)
    outs, refs = refs[:count_out], refs[count_out:]
    landed, source, total, values, picked, value_sem, piece_sem, base_sem, out_sem = refs
    count, size = values.shape[0], values.shape[-1]
    halves = source.shape[1]
    width = total.shape[-1] // halves
    each = count // steps
    zero_slot = source.shape[0] - 1

    def value_copy(step):
        part = pl.ds(step * each, each)
        return pltpu.make_async_copy(values_hbm.at[part], values.at[part], value_sem.at[step])

    copies, start = [], 0
    for index, piece in enumerate(pieces):
        part = pl.ds(start, piece.shape[0])
        copies.append(pltpu.make_async_copy(piece, landed.at[part], piece_sem.at[index]))
        start += piece.shape[0]
    for copy in copies:
        copy.start()
    for step in range(steps):
        value_copy(step).start()
    if has_base:
        base_copy = pltpu.make_async_copy(base, total, base_sem.at[0])
        base_copy.start()
    else:
        total[...] = jnp.zeros_like(total)

    def slots_of(index):
        row, col = ids[4 + index], ids[4 + count + index]
        if transposed:
            return row_slot(row, ids, per, True), col_slot(col, ids, per)
        return col_slot(col, ids, per), row_slot(row, ids, per, False)

    if only is not None:
        source[zero_slot] = jnp.zeros_like(source[zero_slot])

        def pick(index, found):
            take, _ = slots_of(index)
            picked[found] = index
            return found + jnp.where((take >= only[0]) & (take < only[1]), 1, 0)

        found = lax.fori_loop(0, count, pick, 0)

    first, slot, start = 0, 0, 0
    for group in groups:
        rows = pieces[first].shape[0]
        for copy in copies[first : first + group]:
            copy.wait()
        for block in range(rows // size):
            terms = [landed[pl.ds(start + m * rows + block * size, size), :] for m in range(group)]
            whole = sum(terms[1:], terms[0])
            for half in range(halves):
                both = jnp.concatenate(two_terms(whole[:, half * width : (half + 1) * width]), axis=1)
                source[slot, half, pl.ds(0, size), :] = both
                source[slot, half, pl.ds(size, size), :] = both
            slot += 1
        first, start = first + group, start + group * rows

    def add_block(index, take, put):
        axis = 0 if transposed else 1
        left = jnp.concatenate(two_terms(values[index]), axis=axis)
        rows = pl.ds(pl.multiple_of(put * size, size), size)
        for half in range(halves):
            product = lax.dot_general(
                left, source[take, half], (((axis,), (0,)), ((), ())), preferred_element_type=jnp.float32
            )
            columns = pl.ds(half * width, width)
            total[rows, columns] += product[:, :width] + product[:, width:]

    if only is None:
        for step in range(steps):
            value_copy(step).wait()

            @pl.loop(0, each // unroll)
            def _(index):
                for k in range(unroll):
                    add_block(step * each + index * unroll + k, *slots_of(step * each + index * unroll + k))

    else:
        for step in range(steps):
            value_copy(step).wait()
        if has_base:
            base_copy.wait()

        def add_picked(step, carry):
            for k in range(unroll):
                place = step * unroll + k
                index = jnp.where(place < found, picked[jnp.minimum(place, count)], 0)
                take, put = slots_of(index)
                add_block(index, jnp.where(place < found, take - only[0], zero_slot), put)
            return carry

        lax.fori_loop(0, (found + unroll - 1) // unroll, add_picked, 0)

    copies, start = [], 0
    for index, out in enumerate(outs):
        part = pl.ds(start, out.shape[0])
        copies.append(pltpu.make_async_copy(total.at[part], out, out_sem.at[index]))
        copies[-1].start()
        start += out.shape[0]
    for copy in copies:
        copy.wait()


def spmm(ids, values, groups, out_rows, per, transposed, only=None, base=None):
    pieces = [piece for group in groups for piece in group]
    count, size = values.shape[0], values.shape[-1]
    width = pieces[0].shape[1]
    halves = max(1, width // size)
    unroll = next(p for p in ((32, 16, 8, 4, 2, 1) if only is None else (8, 4, 2, 1)) if count % p == 0)
    steps = count // unroll if only is None else 1
    in_rows = sum(group[0].shape[0] for group in groups)
    smem, anywhere = pl.BlockSpec(memory_space=pltpu.SMEM), pl.BlockSpec(memory_space=pl.ANY)
    bases = [] if base is None else [base]
    return pl.pallas_call(
        functools.partial(
            spmm_kernel,
            [len(group) for group in groups],
            only,
            base is not None,
            len(out_rows),
            steps,
            unroll,
            per,
            transposed,
        ),
        out_shape=[jax.ShapeDtypeStruct((rows, width), jnp.float32) for rows in out_rows],
        in_specs=[smem] + [anywhere] * (1 + len(pieces) + len(bases)),
        out_specs=[anywhere] * len(out_rows),
        scratch_shapes=[
            pltpu.VMEM((sum(piece.shape[0] for piece in pieces), width), jnp.float32),
            pltpu.VMEM((in_rows // size + 1, halves, 2 * size, 2 * (width // halves)), jnp.bfloat16),
            pltpu.VMEM((sum(out_rows), width), jnp.float32),
            pltpu.VMEM(values.shape, jnp.float32),
            pltpu.SMEM((count + 1,), jnp.int32),
            pltpu.SemaphoreType.DMA((steps,)),
            pltpu.SemaphoreType.DMA((len(pieces),)),
            pltpu.SemaphoreType.DMA((1,)),
            pltpu.SemaphoreType.DMA((len(out_rows),)),
        ],
        compiler_params=pltpu.CompilerParams(vmem_limit_bytes=VMEM_LIMIT),
        cost_estimate=pl.CostEstimate(
            flops=8 * count * size * size * width,
            bytes_accessed=4 * (values.size + (in_rows + sum(out_rows)) * width),
            transcendentals=0,
        ),
    )(ids, values, *pieces, *bases)


def dense_kernel(count_parts, ids, *refs):
    halves = []
    for half in range(2):
        parts = refs[half * count_parts : (half + 1) * count_parts]
        rows = parts[0][...]
        if count_parts > 1:
            rows = rows + jnp.where(ids[2] != 0, parts[1][...], 0.0)
            for part in parts[2:]:
                rows = rows + part[...]
        halves.append(rows)
    cotangent, weight, hidden, back, grad_out = refs[2 * count_parts :]
    rows = jnp.concatenate(halves, axis=1)
    pre = dot_terms(rows, weight[...], ((1,), (0,)))
    sigmoid_v = 1.0 / (1.0 + jnp.exp(-pre))
    hidden[...] = pre * sigmoid_v
    dpre = cotangent[...] * sigmoid_v * (1.0 + pre * (1.0 - sigmoid_v))
    back[...] = dot_terms(dpre, weight[...], ((1,), (1,)))
    grad_out[...] = dot_terms(rows, dpre, ((0,), (0,)))


def dense(ids, parts, cotangent, weight):
    rows, width = cotangent.shape
    vmem = pl.BlockSpec(memory_space=pltpu.VMEM)
    return pl.pallas_call(
        functools.partial(dense_kernel, len(parts) // 2),
        in_specs=[pl.BlockSpec(memory_space=pltpu.SMEM)] + [vmem] * (len(parts) + 2),
        out_shape=[
            jax.ShapeDtypeStruct((rows, width), jnp.float32),
            jax.ShapeDtypeStruct((rows, width), jnp.float32),
            jax.ShapeDtypeStruct((width, width), jnp.float32),
        ],
        compiler_params=pltpu.CompilerParams(vmem_limit_bytes=VMEM_LIMIT),
        cost_estimate=pl.CostEstimate(
            flops=1000,
            bytes_accessed=1000,
            transcendentals=0,
        ),
    )(ids, *parts, cotangent, weight)


def along_row(x, bit):
    return lax.ppermute(x, "row", [(i, i ^ bit) for i in range(lax.axis_size("row"))])


def along_col(x, pairs):
    return lax.ppermute(x, "col", pairs)


def after(x, *others):
    return lax.optimization_barrier((x, *others))[0]


def both_cores(mine, *others):
    return [piece for own in mine for piece in (own, along_row(after(own, *others), 1))]


def plane_exchange(pieces, *others):
    return [pieces[p] + along_row(after(pieces[p + 1], *others), 1) for p in (0, 2, 4, 6)]


def line_reduce(slots, edge, earlier):
    own, outer, across, inner = slots
    outer, middle = after(outer, *earlier), after(inner, *earlier)
    near, middle = along_col(outer, OUTER), along_col(middle, MIDDLE)
    far = along_col(after(across + jnp.where(edge, 0.0, near), middle), ACROSS)
    inward = along_col(after(inner, near, middle), INWARD)
    return [own, near, middle, far, inward]


def plane_sum(grad):
    upper = lax.axis_index("row") % 2
    rows = grad.shape[0] // 2
    keep = lax.dynamic_slice_in_dim(grad, upper * rows, rows, 0)
    send = lax.dynamic_slice_in_dim(grad, (1 - upper) * rows, rows, 0)
    grad = keep + along_row(send, 1)
    grad = grad + along_row(grad, 2)
    return grad + along_row(grad, 4)


def both_halves(grad, *others):
    other = along_row(after(grad, *others), 1)
    upper = lax.axis_index("row") % 2
    return jnp.where(upper == 1, jnp.concatenate([other, grad], axis=0), jnp.concatenate([grad, other], axis=0))


def shards(features, weight_matrix, cotangent, block_rows, block_cols, blocks):
    values = blocks[0, 0]
    size = blocks.shape[-1]
    rows_dev, width = features.shape
    per = rows_dev // size
    count_row, count_col = lax.axis_size("row"), lax.axis_size("col")
    total_nodes = rows_dev * count_row * count_col
    me_row, me_col = lax.axis_index("row"), lax.axis_index("col")
    half = width // 2
    features = (features[:, :half], features[:, half:])

    if (count_row, count_col) == (8, 4):
        edge = (me_col == 0) | (me_col == 3)
        place = jnp.stack([me_row, me_col, jnp.where(edge, 2, 0), jnp.where(edge, 0, 3)]).astype(jnp.int32)
        ids = jnp.concatenate([place, block_rows[0, 0], block_cols[0, 0]])
        first, second = features
        diagonal = along_row(first, 6)
        mine = [first, along_row(first, 2), along_row(first, 4), diagonal]
        pieces = both_cores(mine)
        slots = spmm(ids, values, [[p] for p in pieces], [rows_dev] * 4, per, False)
        second = after(second, diagonal)
        mine = [second, along_row(second, 2), along_row(second, 4), along_row(second, 6)]
        terms = line_reduce(slots, edge, [])
        pieces = both_cores(mine, slots[0])
        pieces[0] = after(pieces[0], *terms[1:3])
        slots = spmm(ids, values, [[p] for p in pieces], [rows_dev] * 4, per, False)
        terms += line_reduce(slots, edge, terms[3:5])
        hidden, back, grad = dense(ids, terms, cotangent, weight_matrix)

        ends_across = along_col(back, ENDS_ACROSS)
        later = after(back, ends_across)
        ends_inward, middle = along_col(later, ENDS_INWARD), along_col(later, MIDDLE)
        outward = along_col(ends_across, OUTWARD)
        near_part = spmm(
            ids, values, [[back], [ends_across]], [rows_dev * count_row], per, True, (0, 2 * per)
        )[0]
        grad = plane_sum(after(grad, ends_across))
        groups = [[after(ends_inward, grad)], [middle, outward]]
        sums = plane_exchange(
            spmm(ids, values, groups, [rows_dev] * 8, per, True, (2 * per, 4 * per), near_part)
        )
        others = [along_row(sums[k], 2 * k) for k in (3, 1, 2)]
        feature_grad = sums[0] + others[0] + others[1] + others[2]
        grad = after(grad, sums[3])
        grad = both_halves(grad + along_col(grad, OUTER) + along_col(grad, ACROSS) + along_col(grad, REVERSED), *others)
    else:
        place = jnp.zeros((4,), jnp.int32)
        ids = jnp.concatenate([place, block_rows[0, 0], block_cols[0, 0]])
        parts = []
        for own in features:
            gathered = lax.all_gather(own, "row", axis=0, tiled=True)
            (partial,) = spmm(ids, values, [[gathered]], [rows_dev * count_col], per, False)
            parts.append(lax.psum_scatter(partial, "col", scatter_dimension=0, tiled=True))
        hidden, back, grad = dense(ids, parts, cotangent, weight_matrix)
        gathered = lax.all_gather(back, "col", axis=0, tiled=True)
        (partial,) = spmm(ids, values, [[gathered]], [rows_dev * count_row], per, True)
        feature_grad = lax.psum_scatter(partial, "row", scatter_dimension=0, tiled=True)
        grad = lax.psum(grad, ("row", "col"))

    weight_grad = grad / jnp.sqrt(jnp.float32(total_nodes))
    return (hidden, weight_grad, feature_grad)


def solution(mesh):
    in_specs = (
        P(("col", "row"), None),
        P(),
        P(("row", "col"), None),
        P("row", "col", None),
        P("row", "col", None),
        P("row", "col", None, None, None),
    )
    out_specs = (P(("row", "col"), None), P(), P(("col", "row"), None))
    return jax.shard_map(shards, mesh=mesh, in_specs=in_specs, out_specs=out_specs, check_vma=False)
```

time: 405 us -> 170 us (0.42)
  waiting for transfers between devices: 227 us -> 75.6 us
  matrix products: 65 us -> 0 us
  starting transfers between devices: 0.38 us -> 46.9 us
  other arithmetic: 50.6 us -> 6.38 us
  local copies, waits for them, and re-layouts: 47.7 us -> 6.73 us
  Pallas kernels: 0 us -> 33 us
  between operations: 13.8 us -> 0.98 us
    psum x2 -> x0, waiting for transfers between devices: 132 us -> none  [the longest x1 86.4 us: shards(): row_inputs = lax.psum(partial_value, 'col')]
    ppermute x0 -> x40, waiting for transfers between devices: none -> 75.6 us  [the longest x15 50 us: along_col(): return lax.ppermute(x, 'col', pairs)]
    dot_general x5 -> x0, matrix products: 65 us -> none  [the longest x2 53.9 us: tile_product(): products = jnp.einsum(form, values, chosen, precision=lax.Precision.HIGHEST)]
    reduce_scatter x1 -> x0, waiting for transfers between devices: 54.5 us -> none  [shards(): lax.psum_scatter(grad_part, 'row', scatter_dimension=0, tiled=True)]
    scatter-add x2 -> x0, other arithmetic: 47.2 us -> none  [tile_product(): jnp.zeros((put_count, size_block, width), jnp.float32).at[put_ids]]
    ppermute x0 -> x40, starting transfers between devices: none -> 46.9 us  [the longest x15 30.5 us: along_col(): return lax.ppermute(x, 'col', pairs)]
    all_gather x2 -> x0, waiting for transfers between devices: 39.3 us -> none  [the longest x1 39.3 us: shards(): feature_tile = lax.all_gather(features, 'row', axis=0, tiled=True)]
    pallas_call x0 -> x5, Pallas kernels: none -> 33 us  [the longest x4 29.8 us: spmm(): pl.pallas_call(functools.partial(spmm_kernel, [len(group) for group in gr...]
  transfers between devices with their start and end apart: 5 -> 40, of which waited for: 4 -> 17; matrix products, arithmetic and copies ran while one was open for 37% -> 4% of each run, Pallas kernels for 0% -> 12%
where the time goes in v2:
time: 170 us
  waiting for transfers between devices  75.6 us (44%)
  starting transfers between devices  46.9 us (28%)
  Pallas kernels  33 us (19%)
  local copies, waits for them, and re-layouts  6.73 us (4%)
  other arithmetic  6.38 us (4%)
    ppermute x15, waiting for transfers between devices, along_col(): return lax.ppermute(x, 'col', pairs)  50 us
    ppermute x15, starting transfers between devices, along_col(): return lax.ppermute(x, 'col', pairs)  30.5 us
    pallas_call x4, Pallas kernels, spmm(): pl.pallas_call(functools.partial(spmm_kernel, [len(group) for group in gr...  29.8 us
    ppermute x25, waiting for transfers between devices, along_row(): lax.ppermute(x, 'row', [(i, i ^ bit) for i in range(lax.axis_size('row'))])  25.6 us
    ppermute x25, starting transfers between devices, along_row(): lax.ppermute(x, 'row', [(i, i ^ bit) for i in range(lax.axis_size('row'))])  16.5 us
    unnamed x36, local copies, waits for them, and re-layouts  4.91 us
  transfers between devices with their start and end apart: 40, of which 17 were waited for; matrix products, arithmetic and copies ran while one was open for 4% of the time, Pallas kernels for 12%

profile of v2, /device:TPU:0, one launch (start us, length us, event | category | flops | bytes accessed | tf_op | source)
XLA Modules:
  0.0 169.6 jit_solution(4486422456316241252)
XLA Ops:
  0.6 1.1 fusion.1
  1.7 4.0 %collective-permute-start.5 = (f32[512,128]{1,0:T(8,128)S(1)}, f32[512,128]{1,0:T(8,128)S(1)}, u32[]{:S(2)}, u32[]{:S(2)}) collective-permute-start(f32[512,128]{1,0:T(8,128)S(1)} %get-tuple-element.76.refs_0_), channel_id=1, source_target_pairs={{0,24},{4,28},{8,16},{12,20},{16,8},{20,12},{24,0},{28,4},{1,25},{... | collective-permute-start | bytes 786440 | tf_op jit(solution)/shard_map/ppermute | solution.py:244
  6.3 6.5 %collective-permute-done.5.refs_6_ = f32[512,128]{1,0:T(8,128)S(1)} collective-permute-done((f32[512,128]{1,0:T(8,128)S(1)}, f32[512,128]{1,0:T(8,128)S(1)}, u32[]{:S(2)}, u32[]{:S(2)}) %collective-permute-start.5) | collective-permute-done | bytes 262176 | tf_op jit(solution)/shard_map/ppermute | solution.py:244
  12.8 4.7 %collective-permute-done.3.refs_4_ = f32[512,128]{1,0:T(8,128)S(1)} collective-permute-done((f32[512,128]{1,0:T(8,128)S(1)}, f32[512,128]{1,0:T(8,128)S(1)}, u32[]{:S(2)}, u32[]{:S(2)}) %collective-permute-start.3) | collective-permute-done | bytes 262176 | tf_op jit(solution)/shard_map/ppermute | solution.py:244
  18.1 0.7 concatenate.9.ids
  18.8 1.8 %collective-permute-start.16 = (f32[512,128]{1,0:T(8,128)S(1)}, f32[512,128]{1,0:T(8,128)S(1)}, u32[]{:S(2)}, u32[]{:S(2)}) collective-permute-start(f32[512,128]{1,0:T(8,128)S(1)} %get-tuple-element.47.refs_0_), channel_id=1, source_target_pairs={{0,24},{4,28},{8,16},{12,20},{16,8},{20,12},{24,0},{28,4},{1,25},{... | collective-permute-start | bytes 786440 | tf_op jit(solution)/shard_map/ppermute | solution.py:244
  20.7 1.3 collective-permute-start.14
  23.1 5.6 %shard_map.85 = (f32[512,128]{1,0:T(8,128)S(1)}, f32[512,128]{1,0:T(8,128)S(1)}, f32[512,128]{1,0:T(8,128)S(1)}, f32[512,128]{1,0:T(8,128)S(1)}) custom-call(s32[196]{0:T(256)S(1)} %concatenate.9.ids, f32[96,128,128]{2,1,0:T(8,128)} %bitcast.7, f32[512,128]{1,0:T(8,128)S(1)} %get-tuple-element.76.refs_0_, f32[512,128]{1,0:T(8,128)S(1)} %collective-permute-done.refs_1_, ...), custom_call_target="tpu_custom_call" | custom-call | flops 1610612736 | bytes 9437184 | tf_op jit(solution)/shard_map/pallas_call | solution.py:168
  28.8 1.8 %collective-permute-start.7 = (f32[512,128]{1,0:T(8,128)S(1)}, f32[512,128]{1,0:T(8,128)S(1)}, u32[]{:S(2)}, u32[]{:S(2)}) collective-permute-start(f32[512,128]{1,0:T(8,128)S(1)} %get-tuple-element.40), channel_id=1, source_target_pairs={{0,1},{1,0},{2,3},{3,2},{4,5},{5,4},{6,7},{7,6},{8,9},{9,8},{10,11... | collective-permute-start | bytes 786440 | tf_op jit(solution)/shard_map/ppermute | solution.py:248
  31.4 2.5 %collective-permute-done.14.refs_4_ = f32[512,128]{1,0:T(8,128)S(1)} collective-permute-done((f32[512,128]{1,0:T(8,128)S(1)}, f32[512,128]{1,0:T(8,128)S(1)}, u32[]{:S(2)}, u32[]{:S(2)}) %collective-permute-start.14) | collective-permute-done | bytes 262176 | tf_op jit(solution)/shard_map/ppermute | solution.py:244
  34.5 2.0 %collective-permute-done.7.refs_1_ = f32[512,128]{1,0:T(8,128)S(1)} collective-permute-done((f32[512,128]{1,0:T(8,128)S(1)}, f32[512,128]{1,0:T(8,128)S(1)}, u32[]{:S(2)}, u32[]{:S(2)}) %collective-permute-start.7) | collective-permute-done | bytes 262176 | tf_op jit(solution)/shard_map/ppermute | solution.py:248
  36.5 5.8 %collective-permute-start.9 = (f32[512,128]{1,0:T(8,128)S(1)}, f32[512,128]{1,0:T(8,128)S(1)}, u32[]{:S(2)}, u32[]{:S(2)}) collective-permute-start(f32[512,128]{1,0:T(8,128)S(1)} %select_add_fusion.1), channel_id=1, source_target_pairs={{0,2},{1,3},{2,0},{3,1},{4,6},{5,7},{6,4},{7,5},{8,10},{9,11},{10,... | collective-permute-start | bytes 786440 | tf_op jit(solution)/shard_map/ppermute | solution.py:248
  42.4 1.3 collective-permute-start.10
  44.5 0.7 copy-done.14
  45.2 5.6 %shard_map.86 = (f32[512,128]{1,0:T(8,128)S(1)}, f32[512,128]{1,0:T(8,128)S(1)}, f32[512,128]{1,0:T(8,128)S(1)}, f32[512,128]{1,0:T(8,128)S(1)}) custom-call(s32[196]{0:T(256)S(1)} %concatenate.9.ids, f32[96,128,128]{2,1,0:T(8,128)} %bitcast.8, f32[512,128]{1,0:T(8,128)S(1)} %get-tuple-element.47.refs_0_, f32[512,128]{1,0:T(8,128)S(1)} %collective-permute-done.11.refs_1_, ...), custom_call_target="tpu_custom_call" | custom-call | flops 1610612736 | bytes 9437184 | tf_op jit(solution)/shard_map/pallas_call | solution.py:168
  50.8 1.7 collective-permute-done.9.refs_3_
  52.5 1.8 %collective-permute-start.18 = (f32[512,128]{1,0:T(8,128)S(1)}, f32[512,128]{1,0:T(8,128)S(1)}, u32[]{:S(2)}, u32[]{:S(2)}) collective-permute-start(f32[512,128]{1,0:T(8,128)S(1)} %get-tuple-element.53), channel_id=1, source_target_pairs={{0,1},{1,0},{2,3},{3,2},{4,5},{5,4},{6,7},{7,6},{8,9},{9,8},{10,11... | collective-permute-start | bytes 786440 | tf_op jit(solution)/shard_map/ppermute | solution.py:248
  55.0 4.5 %collective-permute-done.18.refs_6_ = f32[512,128]{1,0:T(8,128)S(1)} collective-permute-done((f32[512,128]{1,0:T(8,128)S(1)}, f32[512,128]{1,0:T(8,128)S(1)}, u32[]{:S(2)}, u32[]{:S(2)}) %collective-permute-start.18) | collective-permute-done | bytes 262176 | tf_op jit(solution)/shard_map/ppermute | solution.py:248
  59.5 6.0 %collective-permute-start.20 = (f32[512,128]{1,0:T(8,128)S(1)}, f32[512,128]{1,0:T(8,128)S(1)}, u32[]{:S(2)}, u32[]{:S(2)}) collective-permute-start(f32[512,128]{1,0:T(8,128)S(1)} %select_add_fusion), channel_id=1, source_target_pairs={{0,2},{1,3},{2,0},{3,1},{4,6},{5,7},{6,4},{7,5},{8,10},{9,11},{10,... | collective-permute-start | bytes 786440 | tf_op jit(solution)/shard_map/ppermute | solution.py:248
  65.5 1.3 collective-permute-start.21
  66.8 8.8 %collective-permute-done.20.refs_8_ = f32[512,128]{1,0:T(8,128)S(1)} collective-permute-done((f32[512,128]{1,0:T(8,128)S(1)}, f32[512,128]{1,0:T(8,128)S(1)}, u32[]{:S(2)}, u32[]{:S(2)}) %collective-permute-start.20) | collective-permute-done | bytes 262176 | tf_op jit(solution)/shard_map/ppermute | solution.py:248
  75.7 0.7 copy-done.16
  76.5 3.2 %shard_map.87 = (f32[512,256]{1,0:T(8,128)}, f32[512,256]{1,0:T(8,128)}, f32[256,256]{1,0:T(8,128)S(1)}) custom-call(s32[196]{0:T(256)S(1)} %concatenate.9.ids, f32[512,128]{1,0:T(8,128)S(1)} %get-tuple-element.39.refs_0_, f32[512,128]{1,0:T(8,128)S(1)} %collective-permute-done.7.refs_1_, f32[512,128]{1,0:T(8,128)S(1)} %collective-permute-done.8.refs_2_, ...), custom_call_target="tpu_custom_call" | custom-call | flops 1000 | bytes 1000 | tf_op jit(solution)/shard_map/pallas_call | solution.py:226
  79.7 1.7 collective-permute-start.22
  81.4 11.1 %collective-permute-done.22.refs_1_ = f32[512,256]{1,0:T(8,128)S(1)} collective-permute-done((f32[512,256]{1,0:T(8,128)}, f32[512,256]{1,0:T(8,128)S(1)}, u32[]{:S(2)}, u32[]{:S(2)}) %collective-permute-start.22) | collective-permute-done | bytes 524320 | tf_op jit(solution)/shard_map/ppermute | solution.py:248
  93.3 3.3 %collective-permute-start.26 = (f32[512,256]{1,0:T(8,128)}, f32[512,256]{1,0:T(8,128)S(1)}, u32[]{:S(2)}, u32[]{:S(2)}) collective-permute-start(f32[512,256]{1,0:T(8,128)} %get-tuple-element.63.refs_0_), channel_id=1, source_target_pairs={{2,0},{1,3},{0,1},{3,2},{6,4},{5,7},{4,5},{7,6},{10,8},{9,11},{8,9... | collective-permute-start | bytes 1572872 | tf_op jit(solution)/shard_map/ppermute | solution.py:248
  96.6 1.3 collective-permute-start.28
  97.9 1.6 collective-permute-start.24
  99.5 3.8 %collective-permute-done.24 = f32[128,256]{1,0:T(8,128)S(1)} collective-permute-done((f32[128,256]{1,0:T(8,128)S(1)}, f32[128,256]{1,0:T(8,128)S(1)}, u32[]{:S(2)}, u32[]{:S(2)}) %collective-permute-start.24) | collective-permute-done | bytes 131104 | tf_op jit(solution)/shard_map/ppermute | solution.py:244
  103.3 1.6 collective-permute-start.25
  105.0 1.0 copy-done
  106.0 9.8 %shard_map.88.refs_3_ = f32[4096,256]{1,0:T(8,128)} custom-call(s32[196]{0:T(256)S(1)} %concatenate.9.ids, f32[96,128,128]{2,1,0:T(8,128)} %bitcast.9, f32[512,256]{1,0:T(8,128)S(1)} %copy-done, f32[512,256]{1,0:T(8,128)S(1)} %collective-permute-done.22.refs_1_), custom_call_target="tpu_custom_call" | custom-call | flops 3221225472 | bytes 11534336 | tf_op jit(solution)/shard_map/pallas_call | solution.py:168
  115.9 4.7 %collective-permute-done.26.refs_0_ = f32[512,256]{1,0:T(8,128)S(1)} collective-permute-done((f32[512,256]{1,0:T(8,128)}, f32[512,256]{1,0:T(8,128)S(1)}, u32[]{:S(2)}, u32[]{:S(2)}) %collective-permute-start.26) | collective-permute-done | bytes 524320 | tf_op jit(solution)/shard_map/ppermute | solution.py:248
  120.6 2.9 %collective-permute-done.28.refs_2_ = f32[512,256]{1,0:T(8,128)S(1)} collective-permute-done((f32[512,256]{1,0:T(8,128)S(1)}, f32[512,256]{1,0:T(8,128)S(1)}, u32[]{:S(2)}, u32[]{:S(2)}) %collective-permute-start.28) | collective-permute-done | bytes 524320 | tf_op jit(solution)/shard_map/ppermute | solution.py:248
  123.5 0.8 copy-done.4
  124.3 8.7 %shard_map.89 = (f32[512,256]{1,0:T(8,128)S(1)}, f32[512,256]{1,0:T(8,128)S(1)}, f32[512,256]{1,0:T(8,128)S(1)}, f32[512,256]{1,0:T(8,128)}, f32[512,256]{1,0:T(...) custom-call(s32[196]{0:T(256)S(1)} %concatenate.9.ids, f32[96,128,128]{2,1,0:T(8,128)} %bitcast.10, ...), custom_call_target="tpu_custom_call" | custom-call | flops 3221225472 | bytes 11534336 | tf_op jit(solution)/shard_map/pallas_call | solution.py:168
  133.7 1.5 collective-permute-done.29
  135.2 1.1 add.64
  136.3 4.2 %collective-permute-start.32 = (f32[128,256]{1,0:T(8,128)S(1)}, f32[128,256]{1,0:T(8,128)S(1)}, u32[]{:S(2)}, u32[]{:S(2)}) collective-permute-start(f32[128,256]{1,0:T(8,128)S(1)} %add.63), channel_id=1, source_target_pairs={{0,3},{1,2},{2,1},{3,0},{4,7},{5,6},{6,5},{7,4},{8,11},{9,10},{10,... | collective-permute-start | bytes 393224 | tf_op jit(solution)/shard_map/ppermute | solution.py:248
  140.5 1.8 %collective-permute-start.33 = (f32[512,256]{1,0:T(8,128)S(1)}, f32[512,256]{1,0:T(8,128)S(1)}, u32[]{:S(2)}, u32[]{:S(2)}) collective-permute-start(f32[512,256]{1,0:T(8,128)S(1)} %add.64), channel_id=1, source_target_pairs={{0,24},{4,28},{8,16},{12,20},{16,8},{20,12},{24,0},{28,4},{1,25},{... | collective-permute-start | bytes 1572872 | tf_op jit(solution)/shard_map/ppermute | solution.py:244
  142.3 1.3 collective-permute-start.35
  143.6 1.1 add.69
  145.3 8.6 %collective-permute-done.31 = f32[128,256]{1,0:T(8,128)S(1)} collective-permute-done((f32[128,256]{1,0:T(8,128)S(1)}, f32[128,256]{1,0:T(8,128)S(1)}, u32[]{:S(2)}, u32[]{:S(2)}) %collective-permute-start.31) | collective-permute-done | bytes 131104 | tf_op jit(solution)/shard_map/ppermute | solution.py:248
  154.0 5.6 %collective-permute-done.30 = f32[128,256]{1,0:T(8,128)} collective-permute-done((f32[128,256]{1,0:T(8,128)S(1)}, f32[128,256]{1,0:T(8,128)}, u32[]{:S(2)}, u32[]{:S(2)}) %collective-permute-start.30) | collective-permute-done | bytes 131104 | tf_op jit(solution)/shard_map/ppermute | solution.py:248
  159.5 0.9 add_add_fusion.1
  160.5 6.1 %collective-permute-done.35 = f32[512,256]{1,0:T(8,128)} collective-permute-done((f32[512,256]{1,0:T(8,128)S(1)}, f32[512,256]{1,0:T(8,128)}, u32[]{:S(2)}, u32[]{:S(2)}) %collective-permute-start.35) | collective-permute-done | bytes 524320 | tf_op jit(solution)/shard_map/ppermute | solution.py:244
  166.6 2.3 %add_add_fusion = f32[512,256]{1,0:T(8,128)} fusion(f32[512,256]{1,0:T(8,128)} %collective-permute-done.37, f32[512,256]{1,0:T(8,128)} %collective-permute-done.35, f32[512,256]{1,0:T(8,128)S(1)} %collective-permute-done.33, f32[512,256]{1,0:T(8,128)S(1)} %get-tuple-element.73, f32[512,256]{1,0:T(8,128)} %collective-permute-done.39), kind=kLoop, calls=%fused_computation | loop fusion | flops 524288 | bytes 3145728 | tf_op jit(solution)/shard_map/add | solution.py:330
  168.9 0.7 fusion
  (87 shorter events, 7.3 us)
Async XLA Ops:
  1.7 11.1 %collective-permute-start.5 = (f32[512,128]{1,0:T(8,128)S(1)}, f32[512,128]{1,0:T(8,128)S(1)}, u32[]{:S(2)}, u32[]{:S(2)}) collective-permute-start(f32[512,128]{1,0:T(8,128)S(1)} %get-tuple-element.76.refs_0_), channel_id=1, source_target_pairs={{0,24},{4,28},{8,16},{12,20},{16,8},{20,12},{24,0},{28,4},{1,25},{... | collective-permute-start | bytes 786440 | tf_op jit(solution)/shard_map/ppermute | solution.py:244
  5.7 11.9 %collective-permute-start.3 = (f32[512,128]{1,0:T(8,128)S(1)}, f32[512,128]{1,0:T(8,128)S(1)}, u32[]{:S(2)}, u32[]{:S(2)}) collective-permute-start(f32[512,128]{1,0:T(8,128)S(1)} %get-tuple-element.76.refs_0_), channel_id=1, source_target_pairs={{0,16},{4,20},{8,24},{12,28},{16,0},{20,4},{24,8},{28,12},{1,17},{... | collective-permute-start | bytes 786440 | tf_op jit(solution)/shard_map/ppermute | solution.py:244
  6.2 11.7 %collective-permute-start.1 = (f32[512,128]{1,0:T(8,128)S(1)}, f32[512,128]{1,0:T(8,128)S(1)}, u32[]{:S(2)}, u32[]{:S(2)}) collective-permute-start(f32[512,128]{1,0:T(8,128)S(1)} %get-tuple-element.76.refs_0_), channel_id=1, source_target_pairs={{0,8},{4,12},{8,0},{12,4},{16,24},{20,28},{24,16},{28,20},{1,9},{5... | collective-permute-start | bytes 786440 | tf_op jit(solution)/shard_map/ppermute | solution.py:244
  6.3 14.4 %collective-permute-start = (f32[512,128]{1,0:T(8,128)S(1)}, f32[512,128]{1,0:T(8,128)S(1)}, u32[]{:S(2)}, u32[]{:S(2)}) collective-permute-start(f32[512,128]{1,0:T(8,128)S(1)} %get-tuple-element.76.refs_0_), channel_id=1, source_target_pairs={{0,4},{4,0},{8,12},{12,8},{16,20},{20,16},{24,28},{28,24},{1,5},{5... | collective-permute-start | bytes 786440 | tf_op jit(solution)/shard_map/ppermute | solution.py:244
  12.8 9.5 %copy-start.7 = (f32[512,128]{1,0:T(8,128)}, f32[512,128]{1,0:T(8,128)S(1)}, u32[]{:S(2)}) copy-start(f32[512,128]{1,0:T(8,128)S(1)} %collective-permute-done.5.refs_6_) | copy-start | bytes 786436
  12.8 9.2 %collective-permute-start.6 = (f32[512,128]{1,0:T(8,128)S(1)}, f32[512,128]{1,0:T(8,128)S(1)}, u32[]{:S(2)}, u32[]{:S(2)}) collective-permute-start(f32[512,128]{1,0:T(8,128)S(1)} %collective-permute-done.5.refs_6_), channel_id=1, source_target_pairs={{0,4},{4,0},{8,12},{12,8},{16,20},{20,16},{24,28},{28,24},{1,5},{5... | collective-permute-start | bytes 786440 | tf_op jit(solution)/shard_map/ppermute | solution.py:244
  17.6 4.8 %copy-start.8 = (f32[512,128]{1,0:T(8,128)}, f32[512,128]{1,0:T(8,128)S(1)}, u32[]{:S(2)}) copy-start(f32[512,128]{1,0:T(8,128)S(1)} %collective-permute-done.3.refs_4_) | copy-start | bytes 786436
  17.6 4.8 %collective-permute-start.4 = (f32[512,128]{1,0:T(8,128)S(1)}, f32[512,128]{1,0:T(8,128)S(1)}, u32[]{:S(2)}, u32[]{:S(2)}) collective-permute-start(f32[512,128]{1,0:T(8,128)S(1)} %collective-permute-done.3.refs_4_), channel_id=1, source_target_pairs={{0,4},{4,0},{8,12},{12,8},{16,20},{20,16},{24,28},{28,24},{1,5},{5... | collective-permute-start | bytes 786440 | tf_op jit(solution)/shard_map/ppermute | solution.py:244
  17.9 4.5 %collective-permute-start.2 = (f32[512,128]{1,0:T(8,128)S(1)}, f32[512,128]{1,0:T(8,128)S(1)}, u32[]{:S(2)}, u32[]{:S(2)}) collective-permute-start(f32[512,128]{1,0:T(8,128)S(1)} %collective-permute-done.1.refs_2_), channel_id=1, source_target_pairs={{0,4},{4,0},{8,12},{12,8},{16,20},{20,16},{24,28},{28,24},{1,5},{5... | collective-permute-start | bytes 786440 | tf_op jit(solution)/shard_map/ppermute | solution.py:244
  18.8 12.4 %collective-permute-start.16 = (f32[512,128]{1,0:T(8,128)S(1)}, f32[512,128]{1,0:T(8,128)S(1)}, u32[]{:S(2)}, u32[]{:S(2)}) collective-permute-start(f32[512,128]{1,0:T(8,128)S(1)} %get-tuple-element.47.refs_0_), channel_id=1, source_target_pairs={{0,24},{4,28},{8,16},{12,20},{16,8},{20,12},{24,0},{28,4},{1,25},{... | collective-permute-start | bytes 786440 | tf_op jit(solution)/shard_map/ppermute | solution.py:244
  20.7 13.2 %collective-permute-start.14 = (f32[512,128]{1,0:T(8,128)S(1)}, f32[512,128]{1,0:T(8,128)S(1)}, u32[]{:S(2)}, u32[]{:S(2)}) collective-permute-start(f32[512,128]{1,0:T(8,128)S(1)} %get-tuple-element.47.refs_0_), channel_id=1, source_target_pairs={{0,16},{4,20},{8,24},{12,28},{16,0},{20,4},{24,8},{28,12},{1,17},{... | collective-permute-start | bytes 786440 | tf_op jit(solution)/shard_map/ppermute | solution.py:244
  22.0 11.9 %collective-permute-start.12 = (f32[512,128]{1,0:T(8,128)S(1)}, f32[512,128]{1,0:T(8,128)S(1)}, u32[]{:S(2)}, u32[]{:S(2)}) collective-permute-start(f32[512,128]{1,0:T(8,128)S(1)} %get-tuple-element.47.refs_0_), channel_id=1, source_target_pairs={{0,8},{4,12},{8,0},{12,4},{16,24},{20,28},{24,16},{28,20},{1,9},{5... | collective-permute-start | bytes 786440 | tf_op jit(solution)/shard_map/ppermute | solution.py:244
  28.8 7.7 %collective-permute-start.7 = (f32[512,128]{1,0:T(8,128)S(1)}, f32[512,128]{1,0:T(8,128)S(1)}, u32[]{:S(2)}, u32[]{:S(2)}) collective-permute-start(f32[512,128]{1,0:T(8,128)S(1)} %get-tuple-element.40), channel_id=1, source_target_pairs={{0,1},{1,0},{2,3},{3,2},{4,5},{5,4},{6,7},{7,6},{8,9},{9,8},{10,11... | collective-permute-start | bytes 786440 | tf_op jit(solution)/shard_map/ppermute | solution.py:248
  30.6 5.9 %collective-permute-start.8 = (f32[512,128]{1,0:T(8,128)S(1)}, f32[512,128]{1,0:T(8,128)S(1)}, u32[]{:S(2)}, u32[]{:S(2)}) collective-permute-start(f32[512,128]{1,0:T(8,128)S(1)} %get-tuple-element.44), channel_id=1, source_target_pairs={{1,2},{2,1},{5,6},{6,5},{9,10},{10,9},{13,14},{14,13},{17,18},{18,... | collective-permute-start | bytes 786440 | tf_op jit(solution)/shard_map/ppermute | solution.py:248
  31.3 12.4 %copy-start.5 = (f32[512,128]{1,0:T(8,128)}, f32[512,128]{1,0:T(8,128)S(1)}, u32[]{:S(2)}) copy-start(f32[512,128]{1,0:T(8,128)S(1)} %collective-permute-done.16.refs_6_) | copy-start | bytes 786436
  31.3 11.1 %collective-permute-start.11 = (f32[512,128]{1,0:T(8,128)S(1)}, f32[512,128]{1,0:T(8,128)S(1)}, u32[]{:S(2)}, u32[]{:S(2)}) collective-permute-start(f32[512,128]{1,0:T(8,128)S(1)} %get-tuple-element.47.refs_0_), channel_id=1, source_target_pairs={{0,4},{4,0},{8,12},{12,8},{16,20},{20,16},{24,28},{28,24},{1,5},{5... | collective-permute-start | bytes 786440 | tf_op jit(solution)/shard_map/ppermute | solution.py:244
  33.9 9.9 %copy-start.6 = (f32[512,128]{1,0:T(8,128)}, f32[512,128]{1,0:T(8,128)S(1)}, u32[]{:S(2)}) copy-start(f32[512,128]{1,0:T(8,128)S(1)} %collective-permute-done.14.refs_4_) | copy-start | bytes 786436
  33.9 9.7 %collective-permute-start.13 = (f32[512,128]{1,0:T(8,128)S(1)}, f32[512,128]{1,0:T(8,128)S(1)}, u32[]{:S(2)}, u32[]{:S(2)}) collective-permute-start(f32[512,128]{1,0:T(8,128)S(1)} %collective-permute-done.12.refs_2_), channel_id=1, source_target_pairs={{0,4},{4,0},{8,12},{12,8},{16,20},{20,16},{24,28},{28,24},{1,5},{5... | collective-permute-start | bytes 786440 | tf_op jit(solution)/shard_map/ppermute | solution.py:244
  33.9 9.7 %collective-permute-start.15 = (f32[512,128]{1,0:T(8,128)S(1)}, f32[512,128]{1,0:T(8,128)S(1)}, u32[]{:S(2)}, u32[]{:S(2)}) collective-permute-start(f32[512,128]{1,0:T(8,128)S(1)} %collective-permute-done.14.refs_4_), channel_id=1, source_target_pairs={{0,4},{4,0},{8,12},{12,8},{16,20},{20,16},{24,28},{28,24},{1,5},{5... | collective-permute-start | bytes 786440 | tf_op jit(solution)/shard_map/ppermute | solution.py:244
  36.5 7.2 %collective-permute-start.17 = (f32[512,128]{1,0:T(8,128)S(1)}, f32[512,128]{1,0:T(8,128)S(1)}, u32[]{:S(2)}, u32[]{:S(2)}) collective-permute-start(f32[512,128]{1,0:T(8,128)S(1)} %collective-permute-done.16.refs_6_), channel_id=1, source_target_pairs={{0,4},{4,0},{8,12},{12,8},{16,20},{20,16},{24,28},{28,24},{1,5},{5... | collective-permute-start | bytes 786440 | tf_op jit(solution)/shard_map/ppermute | solution.py:244
  36.5 16.0 %collective-permute-start.9 = (f32[512,128]{1,0:T(8,128)S(1)}, f32[512,128]{1,0:T(8,128)S(1)}, u32[]{:S(2)}, u32[]{:S(2)}) collective-permute-start(f32[512,128]{1,0:T(8,128)S(1)} %select_add_fusion.1), channel_id=1, source_target_pairs={{0,2},{1,3},{2,0},{3,1},{4,6},{5,7},{6,4},{7,5},{8,10},{9,11},{10,... | collective-permute-start | bytes 786440 | tf_op jit(solution)/shard_map/ppermute | solution.py:248
  42.4 10.1 %collective-permute-start.10 = (f32[512,128]{1,0:T(8,128)S(1)}, f32[512,128]{1,0:T(8,128)S(1)}, u32[]{:S(2)}, u32[]{:S(2)}) collective-permute-start(f32[512,128]{1,0:T(8,128)S(1)} %get-tuple-element.44), channel_id=1, source_target_pairs={{0,1},{3,2},{4,5},{7,6},{8,9},{11,10},{12,13},{15,14},{16,17},{19,... | collective-permute-start | bytes 786440 | tf_op jit(solution)/shard_map/ppermute | solution.py:248
  52.5 7.0 %collective-permute-start.18 = (f32[512,128]{1,0:T(8,128)S(1)}, f32[512,128]{1,0:T(8,128)S(1)}, u32[]{:S(2)}, u32[]{:S(2)}) collective-permute-start(f32[512,128]{1,0:T(8,128)S(1)} %get-tuple-element.53), channel_id=1, source_target_pairs={{0,1},{1,0},{2,3},{3,2},{4,5},{5,4},{6,7},{7,6},{8,9},{9,8},{10,11... | collective-permute-start | bytes 786440 | tf_op jit(solution)/shard_map/ppermute | solution.py:248
  54.3 5.2 %collective-permute-start.19 = (f32[512,128]{1,0:T(8,128)S(1)}, f32[512,128]{1,0:T(8,128)S(1)}, u32[]{:S(2)}, u32[]{:S(2)}) collective-permute-start(f32[512,128]{1,0:T(8,128)S(1)} %get-tuple-element.58), channel_id=1, source_target_pairs={{1,2},{2,1},{5,6},{6,5},{9,10},{10,9},{13,14},{14,13},{17,18},{18,... | collective-permute-start | bytes 786440 | tf_op jit(solution)/shard_map/ppermute | solution.py:248
  59.5 16.2 %copy-start.1 = (f32[512,128]{1,0:T(8,128)}, f32[512,128]{1,0:T(8,128)S(1)}, u32[]{:S(2)}) copy-start(f32[512,128]{1,0:T(8,128)S(1)} %collective-permute-done.18.refs_6_) | copy-start | bytes 786436
  59.5 16.2 %copy-start.15 = (f32[512,128]{1,0:T(8,128)}, f32[512,128]{1,0:T(8,128)S(1)}, u32[]{:S(2)}) copy-start(f32[512,128]{1,0:T(8,128)S(1)} %collective-permute-done.19.refs_7_) | copy-start | bytes 786436
  59.5 16.1 %collective-permute-start.20 = (f32[512,128]{1,0:T(8,128)S(1)}, f32[512,128]{1,0:T(8,128)S(1)}, u32[]{:S(2)}, u32[]{:S(2)}) collective-permute-start(f32[512,128]{1,0:T(8,128)S(1)} %select_add_fusion), channel_id=1, source_target_pairs={{0,2},{1,3},{2,0},{3,1},{4,6},{5,7},{6,4},{7,5},{8,10},{9,11},{10,... | collective-permute-start | bytes 786440 | tf_op jit(solution)/shard_map/ppermute | solution.py:248
  65.5 10.1 %collective-permute-start.21 = (f32[512,128]{1,0:T(8,128)S(1)}, f32[512,128]{1,0:T(8,128)S(1)}, u32[]{:S(2)}, u32[]{:S(2)}) collective-permute-start(f32[512,128]{1,0:T(8,128)S(1)} %get-tuple-element.58), channel_id=1, source_target_pairs={{0,1},{3,2},{4,5},{7,6},{8,9},{11,10},{12,13},{15,14},{16,17},{19,... | collective-permute-start | bytes 786440 | tf_op jit(solution)/shard_map/ppermute | solution.py:248
  79.7 12.8 %collective-permute-start.22 = (f32[512,256]{1,0:T(8,128)}, f32[512,256]{1,0:T(8,128)S(1)}, u32[]{:S(2)}, u32[]{:S(2)}) collective-permute-start(f32[512,256]{1,0:T(8,128)} %get-tuple-element.63.refs_0_), channel_id=1, source_target_pairs={{0,2},{3,1},{1,0},{2,3},{4,6},{7,5},{5,4},{6,7},{8,10},{11,9},{9,8... | collective-permute-start | bytes 1572872 | tf_op jit(solution)/shard_map/ppermute | solution.py:248
  92.5 5.3 %collective-permute-start.23 = (f32[128,256]{1,0:T(8,128)S(1)}, f32[128,256]{1,0:T(8,128)S(1)}, u32[]{:S(2)}, u32[]{:S(2)}) collective-permute-start(f32[128,256]{1,0:T(8,128)S(1)} %constant_dynamic-slice_fusion), channel_id=1, source_target_pairs={{0,4},{4,0},{8,12},{12,8},{16,20},{20,16},{24,28},{28,24},{1,5},{5... | collective-permute-start | bytes 393224 | tf_op jit(solution)/shard_map/ppermute | solution.py:244
  92.6 28.0 %collective-permute-start.27 = (f32[512,256]{1,0:T(8,128)}, f32[512,256]{1,0:T(8,128)S(1)}, u32[]{:S(2)}, u32[]{:S(2)}) collective-permute-start(f32[512,256]{1,0:T(8,128)} %get-tuple-element.63.refs_0_), channel_id=1, source_target_pairs={{1,2},{2,1},{5,6},{6,5},{9,10},{10,9},{13,14},{14,13},{17,18},{18,... | collective-permute-start | bytes 1572872 | tf_op jit(solution)/shard_map/ppermute | solution.py:248
  93.3 27.3 %collective-permute-start.26 = (f32[512,256]{1,0:T(8,128)}, f32[512,256]{1,0:T(8,128)S(1)}, u32[]{:S(2)}, u32[]{:S(2)}) collective-permute-start(f32[512,256]{1,0:T(8,128)} %get-tuple-element.63.refs_0_), channel_id=1, source_target_pairs={{2,0},{1,3},{0,1},{3,2},{6,4},{5,7},{4,5},{7,6},{10,8},{9,11},{8,9... | collective-permute-start | bytes 1572872 | tf_op jit(solution)/shard_map/ppermute | solution.py:248
  96.6 26.9 %collective-permute-start.28 = (f32[512,256]{1,0:T(8,128)S(1)}, f32[512,256]{1,0:T(8,128)S(1)}, u32[]{:S(2)}, u32[]{:S(2)}) collective-permute-start(f32[512,256]{1,0:T(8,128)S(1)} %collective-permute-done.22.refs_1_), channel_id=1, source_target_pairs={{1,0},{2,3},{5,4},{6,7},{9,8},{10,11},{13,12},{14,15},{17,16},{18,... | collective-permute-start | bytes 1572872 | tf_op jit(solution)/shard_map/ppermute | solution.py:248
  97.9 5.4 %collective-permute-start.24 = (f32[128,256]{1,0:T(8,128)S(1)}, f32[128,256]{1,0:T(8,128)S(1)}, u32[]{:S(2)}, u32[]{:S(2)}) collective-permute-start(f32[128,256]{1,0:T(8,128)S(1)} %dynamic-slice_add_fusion), channel_id=1, source_target_pairs={{0,8},{4,12},{8,0},{12,4},{16,24},{20,28},{24,16},{28,20},{1,9},{5... | collective-permute-start | bytes 393224 | tf_op jit(solution)/shard_map/ppermute | solution.py:244
  103.3 12.5 %collective-permute-start.25 = (f32[128,256]{1,0:T(8,128)S(1)}, f32[128,256]{1,0:T(8,128)S(1)}, u32[]{:S(2)}, u32[]{:S(2)}) collective-permute-start(f32[128,256]{1,0:T(8,128)S(1)} %add.62), channel_id=1, source_target_pairs={{0,16},{4,20},{8,24},{12,28},{16,0},{20,4},{24,8},{28,12},{1,17},{... | collective-permute-start | bytes 393224 | tf_op jit(solution)/shard_map/ppermute | solution.py:244
  120.6 2.9 %copy-start.3 = (f32[512,256]{1,0:T(8,128)}, f32[512,256]{1,0:T(8,128)S(1)}, u32[]{:S(2)}) copy-start(f32[512,256]{1,0:T(8,128)S(1)} %collective-permute-done.26.refs_0_) | copy-start | bytes 1572868
  120.6 2.9 %copy-start.2 = (f32[512,256]{1,0:T(8,128)}, f32[512,256]{1,0:T(8,128)S(1)}, u32[]{:S(2)}) copy-start(f32[512,256]{1,0:T(8,128)S(1)} %collective-permute-done.27.refs_1_) | copy-start | bytes 1572868
  133.0 2.2 %collective-permute-start.29 = (f32[512,256]{1,0:T(8,128)}, f32[512,256]{1,0:T(8,128)S(1)}, u32[]{:S(2)}, u32[]{:S(2)}) collective-permute-start(f32[512,256]{1,0:T(8,128)} %get-tuple-element.66), channel_id=1, source_target_pairs={{0,4},{4,0},{8,12},{12,8},{16,20},{20,16},{24,28},{28,24},{1,5},{5... | collective-permute-start | bytes 1572872 | tf_op jit(solution)/shard_map/ppermute | solution.py:244
  133.1 9.2 %collective-permute-start.34 = (f32[512,256]{1,0:T(8,128)}, f32[512,256]{1,0:T(8,128)S(1)}, u32[]{:S(2)}, u32[]{:S(2)}) collective-permute-start(f32[512,256]{1,0:T(8,128)} %get-tuple-element.69), channel_id=1, source_target_pairs={{0,4},{4,0},{8,12},{12,8},{16,20},{20,16},{24,28},{28,24},{1,5},{5... | collective-permute-start | bytes 1572872 | tf_op jit(solution)/shard_map/ppermute | solution.py:244
  133.6 10.1 %collective-permute-start.36 = (f32[512,256]{1,0:T(8,128)}, f32[512,256]{1,0:T(8,128)S(1)}, u32[]{:S(2)}, u32[]{:S(2)}) collective-permute-start(f32[512,256]{1,0:T(8,128)} %get-tuple-element.71), channel_id=1, source_target_pairs={{0,4},{4,0},{8,12},{12,8},{16,20},{20,16},{24,28},{28,24},{1,5},{5... | collective-permute-start | bytes 1572872 | tf_op jit(solution)/shard_map/ppermute | solution.py:244
  136.3 9.0 %collective-permute-start.32 = (f32[128,256]{1,0:T(8,128)S(1)}, f32[128,256]{1,0:T(8,128)S(1)}, u32[]{:S(2)}, u32[]{:S(2)}) collective-permute-start(f32[128,256]{1,0:T(8,128)S(1)} %add.63), channel_id=1, source_target_pairs={{0,3},{1,2},{2,1},{3,0},{4,7},{5,6},{6,5},{7,4},{8,11},{9,10},{10,... | collective-permute-start | bytes 393224 | tf_op jit(solution)/shard_map/ppermute | solution.py:248
  140.5 20.0 %collective-permute-start.33 = (f32[512,256]{1,0:T(8,128)S(1)}, f32[512,256]{1,0:T(8,128)S(1)}, u32[]{:S(2)}, u32[]{:S(2)}) collective-permute-start(f32[512,256]{1,0:T(8,128)S(1)} %add.64), channel_id=1, source_target_pairs={{0,24},{4,28},{8,16},{12,20},{16,8},{20,12},{24,0},{28,4},{1,25},{... | collective-permute-start | bytes 1572872 | tf_op jit(solution)/shard_map/ppermute | solution.py:244
  142.3 24.2 %collective-permute-start.35 = (f32[512,256]{1,0:T(8,128)S(1)}, f32[512,256]{1,0:T(8,128)}, u32[]{:S(2)}, u32[]{:S(2)}) collective-permute-start(f32[512,256]{1,0:T(8,128)S(1)} %add.68), channel_id=1, source_target_pairs={{0,8},{4,12},{8,0},{12,4},{16,24},{20,28},{24,16},{28,20},{1,9},{5... | collective-permute-start | bytes 1572872 | tf_op jit(solution)/shard_map/ppermute | solution.py:244
  144.8 21.8 %collective-permute-start.37 = (f32[512,256]{1,0:T(8,128)S(1)}, f32[512,256]{1,0:T(8,128)}, u32[]{:S(2)}, u32[]{:S(2)}) collective-permute-start(f32[512,256]{1,0:T(8,128)S(1)} %add.69), channel_id=1, source_target_pairs={{0,16},{4,20},{8,24},{12,28},{16,0},{20,4},{24,8},{28,12},{1,17},{... | collective-permute-start | bytes 1572872 | tf_op jit(solution)/shard_map/ppermute | solution.py:244
  145.3 21.3 %collective-permute-start.39 = (f32[512,256]{1,0:T(8,128)S(1)}, f32[512,256]{1,0:T(8,128)}, u32[]{:S(2)}, u32[]{:S(2)}) collective-permute-start(f32[512,256]{1,0:T(8,128)S(1)} %get-tuple-element.74), channel_id=1, source_target_pairs={{0,4},{4,0},{8,12},{12,8},{16,20},{20,16},{24,28},{28,24},{1,5},{5... | collective-permute-start | bytes 1572872 | tf_op jit(solution)/shard_map/ppermute | solution.py:244
  145.3 8.6 %collective-permute-start.31 = (f32[128,256]{1,0:T(8,128)S(1)}, f32[128,256]{1,0:T(8,128)S(1)}, u32[]{:S(2)}, u32[]{:S(2)}) collective-permute-start(f32[128,256]{1,0:T(8,128)S(1)} %add.63), channel_id=1, source_target_pairs={{0,2},{1,3},{2,0},{3,1},{4,6},{5,7},{6,4},{7,5},{8,10},{9,11},{10,... | collective-permute-start | bytes 393224 | tf_op jit(solution)/shard_map/ppermute | solution.py:248
  154.0 5.6 %collective-permute-start.30 = (f32[128,256]{1,0:T(8,128)S(1)}, f32[128,256]{1,0:T(8,128)}, u32[]{:S(2)}, u32[]{:S(2)}) collective-permute-start(f32[128,256]{1,0:T(8,128)S(1)} %add.63), channel_id=1, source_target_pairs={{0,1},{1,0},{2,3},{3,2},{4,5},{5,4},{6,7},{7,6},{8,9},{9,8},{10,11... | collective-permute-start | bytes 393224 | tf_op jit(solution)/shard_map/ppermute | solution.py:248
  166.5 2.3 %collective-permute-start.38 = (f32[128,256]{1,0:T(8,128)S(1)}, f32[128,256]{1,0:T(8,128)S(1)}, u32[]{:S(2)}, u32[]{:S(2)}) collective-permute-start(f32[128,256]{1,0:T(8,128)S(1)} %add_add_fusion.1), channel_id=1, source_target_pairs={{0,4},{4,0},{8,12},{12,8},{16,20},{20,16},{24,28},{28,24},{1,5},{5... | collective-permute-start | bytes 393224 | tf_op jit(solution)/shard_map/ppermute | solution.py:244
  (10 other events, 7.8 us)

commit v3 on v2

--- a/solution.py
+++ b/solution.py
@@ -14,7 +14,6 @@
 INWARD = ((0, 1), (3, 2))
 OUTWARD = ((1, 0), (2, 3))
 ACROSS = ((0, 2), (1, 3), (2, 0), (3, 1))
-REVERSED = ((0, 3), (1, 2), (2, 1), (3, 0))
 ENDS_ACROSS = ((0, 2), (3, 1), (1, 0), (2, 3))
 ENDS_INWARD = ((2, 0), (1, 3), (0, 1), (3, 2))
 
@@ -34,25 +33,35 @@
     return dot(left_high, right_high) + (dot(left_high, right_low) + dot(left_low, right_high))
 
 
+def split_index(block, per):
+    if per & (per - 1) == 0:
+        return block >> (per.bit_length() - 1), block & (per - 1)
+    return block // per, block % per
+
+
 def row_slot(block, place, per, gathered):
-    group = (block // per) ^ place[1]
+    chunk, inside = split_index(block, per)
+    group = chunk ^ place[1]
     if gathered:
         group = group ^ (place[3] * ((group ^ (group >> 1)) & 1))
     else:
         group = group ^ (place[2] * (group & 1))
-    return group * per + block % per
+    return group * per + inside
 
 
 def col_slot(block, place, per):
-    return ((block // per) ^ place[0]) * per + block % per
+    chunk, inside = split_index(block, per)
+    return (chunk ^ place[0]) * per + inside
 
 
 def spmm_kernel(groups, only, has_base, count_out, steps, unroll, per, transposed, ids, values_hbm, *refs):
     count_in = sum(groups)
     pieces, refs = refs[:count_in], refs[count_in:]
-    base, refs = (refs[0], refs[1:]) if has_base else (None, refs)
+    (base, listed), refs = (refs[:2], refs[2:]) if has_base else ((None, None), refs)
     outs, refs = refs[:count_out], refs[count_out:]
-    landed, source, total, values, picked, value_sem, piece_sem, base_sem, out_sem = refs
+    if only is not None and not has_base:
+        listed, refs = refs[0], refs[1:]
+    landed, source, total, values, value_sem, piece_sem, base_sem, out_sem = refs
     count, size = values.shape[0], values.shape[-1]
     halves = source.shape[1]
     width = total.shape[-1] // halves
@@ -68,14 +77,15 @@
         part = pl.ds(start, piece.shape[0])
         copies.append(pltpu.make_async_copy(piece, landed.at[part], piece_sem.at[index]))
         start += piece.shape[0]
-    for copy in copies:
-        copy.start()
-    for step in range(steps):
-        value_copy(step).start()
     if has_base:
         base_copy = pltpu.make_async_copy(base, total, base_sem.at[0])
         base_copy.start()
-    else:
+    for copy in copies:
+        copy.start()
+    if only is None:
+        for step in range(steps):
+            value_copy(step).start()
+    if not has_base:
         total[...] = jnp.zeros_like(total)
 
     def slots_of(index):
@@ -87,12 +97,29 @@
     if only is not None:
         source[zero_slot] = jnp.zeros_like(source[zero_slot])
 
-        def pick(index, found):
-            take, _ = slots_of(index)
-            picked[found] = index
-            return found + jnp.where((take >= only[0]) & (take < only[1]), 1, 0)
-
-        found = lax.fori_loop(0, count, pick, 0)
+        if not has_base:
+
+            def pick(index, found):
+                take, _ = slots_of(index)
+                wanted = (take >= only[0]) & (take < only[1])
+                listed[jnp.where(wanted, found, count - 1 - index + found)] = index
+                return found + wanted.astype(jnp.int32)
+
+            listed[count] = lax.fori_loop(0, count, pick, 0)
+
+        found = count - listed[count] if has_base else listed[count]
+
+        def picked(place):
+            return listed[count - 1 - place if has_base else place]
+
+        def picked_copy(place):
+            return pltpu.make_async_copy(values_hbm.at[picked(place)], values.at[place], value_sem.at[place])
+
+        def start_copy(place, carry):
+            picked_copy(place).start()
+            return carry
+
+        lax.fori_loop(0, found, start_copy, 0)
 
     first, slot, start = 0, 0, 0
     for group in groups:
@@ -109,9 +136,9 @@
             slot += 1
         first, start = first + group, start + group * rows
 
-    def add_block(index, take, put):
+    def add_block(place, take, put):
         axis = 0 if transposed else 1
-        left = jnp.concatenate(two_terms(values[index]), axis=axis)
+        left = jnp.concatenate(two_terms(values[place]), axis=axis)
         rows = pl.ds(pl.multiple_of(put * size, size), size)
         for half in range(halves):
             product = lax.dot_general(
@@ -130,17 +157,23 @@
                     add_block(step * each + index * unroll + k, *slots_of(step * each + index * unroll + k))
 
     else:
-        for step in range(steps):
-            value_copy(step).wait()
         if has_base:
             base_copy.wait()
 
         def add_picked(step, carry):
             for k in range(unroll):
                 place = step * unroll + k
-                index = jnp.where(place < found, picked[jnp.minimum(place, count)], 0)
-                take, put = slots_of(index)
-                add_block(index, jnp.where(place < found, take - only[0], zero_slot), put)
+
+                @pl.when(place < found)
+                def _():
+                    picked_copy(place).wait()
+
+            for k in range(unroll):
+                place = step * unroll + k
+                inside = place < found
+                place = jnp.where(inside, place, 0)
+                take, put = slots_of(picked(place))
+                add_block(place, jnp.where(inside, take - only[0], zero_slot), put)
             return carry
 
         lax.fori_loop(0, (found + unroll - 1) // unroll, add_picked, 0)
@@ -155,7 +188,7 @@
         copy.wait()
 
 
-def spmm(ids, values, groups, out_rows, per, transposed, only=None, base=None):
+def spmm(ids, values, groups, out_rows, per, transposed, only=None, rest=()):
     pieces = [piece for group in groups for piece in group]
     count, size = values.shape[0], values.shape[-1]
     width = pieces[0].shape[1]
@@ -164,29 +197,29 @@
     steps = count // unroll if only is None else 1
     in_rows = sum(group[0].shape[0] for group in groups)
     smem, anywhere = pl.BlockSpec(memory_space=pltpu.SMEM), pl.BlockSpec(memory_space=pl.ANY)
-    bases = [] if base is None else [base]
+    lists = only is not None and not rest
     return pl.pallas_call(
         functools.partial(
             spmm_kernel,
             [len(group) for group in groups],
             only,
-            base is not None,
+            bool(rest),
             len(out_rows),
             steps,
             unroll,
             per,
             transposed,
         ),
-        out_shape=[jax.ShapeDtypeStruct((rows, width), jnp.float32) for rows in out_rows],
-        in_specs=[smem] + [anywhere] * (1 + len(pieces) + len(bases)),
-        out_specs=[anywhere] * len(out_rows),
+        out_shape=[jax.ShapeDtypeStruct((rows, width), jnp.float32) for rows in out_rows]
+        + [jax.ShapeDtypeStruct((count + 1,), jnp.int32)] * lists,
+        in_specs=[smem] + [anywhere] * (1 + len(pieces)) + [anywhere, smem][: len(rest)],
+        out_specs=[anywhere] * len(out_rows) + [smem] * lists,
         scratch_shapes=[
             pltpu.VMEM((sum(piece.shape[0] for piece in pieces), width), jnp.float32),
             pltpu.VMEM((in_rows // size + 1, halves, 2 * size, 2 * (width // halves)), jnp.bfloat16),
             pltpu.VMEM((sum(out_rows), width), jnp.float32),
             pltpu.VMEM(values.shape, jnp.float32),
-            pltpu.SMEM((count + 1,), jnp.int32),
-            pltpu.SemaphoreType.DMA((steps,)),
+            pltpu.SemaphoreType.DMA((steps if only is None else count,)),
             pltpu.SemaphoreType.DMA((len(pieces),)),
             pltpu.SemaphoreType.DMA((1,)),
             pltpu.SemaphoreType.DMA((len(out_rows),)),
@@ -197,7 +230,7 @@
             bytes_accessed=4 * (values.size + (in_rows + sum(out_rows)) * width),
             transcendentals=0,
         ),
-    )(ids, values, *pieces, *bases)
+    )(ids, values, *pieces, *rest)
 
 
 def dense_kernel(count_parts, ids, *refs):
@@ -269,18 +302,16 @@
     return [own, near, middle, far, inward]
 
 
-def plane_sum(grad):
+def core_half(grad):
     upper = lax.axis_index("row") % 2
     rows = grad.shape[0] // 2
     keep = lax.dynamic_slice_in_dim(grad, upper * rows, rows, 0)
     send = lax.dynamic_slice_in_dim(grad, (1 - upper) * rows, rows, 0)
-    grad = keep + along_row(send, 1)
-    grad = grad + along_row(grad, 2)
-    return grad + along_row(grad, 4)
-
-
-def both_halves(grad, *others):
-    other = along_row(after(grad, *others), 1)
+    return keep + along_row(send, 1)
+
+
+def both_halves(grad):
+    other = along_row(grad, 1)
     upper = lax.axis_index("row") % 2
     return jnp.where(upper == 1, jnp.concatenate([other, grad], axis=0), jnp.concatenate([grad, other], axis=0))
 
@@ -318,18 +349,23 @@
         later = after(back, ends_across)
         ends_inward, middle = along_col(later, ENDS_INWARD), along_col(later, MIDDLE)
         outward = along_col(ends_across, OUTWARD)
-        near_part = spmm(
-            ids, values, [[back], [ends_across]], [rows_dev * count_row], per, True, (0, 2 * per)
-        )[0]
-        grad = plane_sum(after(grad, ends_across))
-        groups = [[after(ends_inward, grad)], [middle, outward]]
+        rest = spmm(ids, values, [[back], [ends_across]], [rows_dev * count_row], per, True, (0, 2 * per))
+        grad = core_half(grad)
+        grads = [along_row(after(grad, ends_across), bit) for bit in (2, 4, 6)]
+        groups = [[after(ends_inward, *grads)], [middle, outward]]
         sums = plane_exchange(
-            spmm(ids, values, groups, [rows_dev] * 8, per, True, (2 * per, 4 * per), near_part)
+            spmm(ids, values, groups, [rows_dev] * 8, per, True, (2 * per, 4 * per), rest)
         )
-        others = [along_row(sums[k], 2 * k) for k in (3, 1, 2)]
-        feature_grad = sums[0] + others[0] + others[1] + others[2]
-        grad = after(grad, sums[3])
-        grad = both_halves(grad + along_col(grad, OUTER) + along_col(grad, ACROSS) + along_col(grad, REVERSED), *others)
+        grad = after(grad + grads[0] + grads[1] + grads[2], ends_inward, middle, outward)
+        grad = grad + along_col(grad, OUTER)
+        upper, lower = sums[3][: rows_dev // 2], sums[3][rows_dev // 2 :]
+        upper, lower = after(along_row(upper, 2), grad), along_row(lower, 4)
+        others = [
+            along_row(sums[1] + jnp.pad(lower, ((rows_dev // 2, 0), (0, 0))), 2),
+            along_row(sums[2] + jnp.pad(upper, ((0, rows_dev // 2), (0, 0))), 4),
+        ]
+        feature_grad = sums[0] + others[0] + others[1]
+        grad = both_halves(grad + along_col(grad, ACROSS))
     else:
         place = jnp.zeros((4,), jnp.int32)
         ids = jnp.concatenate([place, block_rows[0, 0], block_cols[0, 0]])

time: 170 us -> 159 us (0.935)
  waiting for transfers between devices: 75.6 us -> 68.4 us
    ppermute x15 -> x14, waiting for transfers between devices: 50 us -> 42.4 us  [along_col(): return lax.ppermute(x, 'col', pairs)]
    ppermute x15 -> x14, starting transfers between devices: 30.5 us -> 26.4 us  [along_col(): return lax.ppermute(x, 'col', pairs)]
    ppermute x25 -> x27, starting transfers between devices: 16.5 us -> 18.8 us  [along_row(): lax.ppermute(x, 'row', [(i, i ^ bit) for i in range(lax.axis_size('row'))])]
    ppermute x25 -> x27, waiting for transfers between devices: 25.6 us -> 26 us  [along_row(): lax.ppermute(x, 'row', [(i, i ^ bit) for i in range(lax.axis_size('row'))])]
  transfers between devices with their start and end apart: 40 -> 41, of which waited for: 17 -> 18; matrix products, arithmetic and copies ran while one was open for 4% -> 3% of each run, Pallas kernels for 12% -> 13%
where the time goes in v3:
time: 159 us; the launch traced here: 160 us
  waiting for transfers between devices  68.4 us (43%)
  starting transfers between devices  45.3 us (28%)
  Pallas kernels  33.4 us (21%)
  local copies, waits for them, and re-layouts  6.73 us (4%)
  other arithmetic  4.92 us (3%)
    ppermute x14, waiting for transfers between devices, along_col(): return lax.ppermute(x, 'col', pairs)  42.4 us
    pallas_call x4, Pallas kernels, spmm(): pl.pallas_call(functools.partial(spmm_kernel, [len(group) for group in gr...  30.2 us
    ppermute x14, starting transfers between devices, along_col(): return lax.ppermute(x, 'col', pairs)  26.4 us
    ppermute x27, waiting for transfers between devices, along_row(): lax.ppermute(x, 'row', [(i, i ^ bit) for i in range(lax.axis_size('row'))])  26 us
    ppermute x27, starting transfers between devices, along_row(): lax.ppermute(x, 'row', [(i, i ^ bit) for i in range(lax.axis_size('row'))])  18.8 us
    unnamed x36, local copies, waits for them, and re-layouts  4.87 us
    pallas_call x1, Pallas kernels, dense(): pl.pallas_call(functools.partial(dense_kernel, len(parts) // 2), in_specs...  3.22 us
  transfers between devices with their start and end apart: 41, of which 18 were waited for; matrix products, arithmetic and copies ran while one was open for 3% of the time, Pallas kernels for 13%

profile of v3, /device:TPU:0, one launch (start us, length us, event | category | flops | bytes accessed | tf_op | source)
XLA Modules:
  0.0 159.8 jit_solution(9651323126409092219)
XLA Ops:
  0.6 1.1 fusion.2
  1.7 4.0 %collective-permute-start.5 = (f32[512,128]{1,0:T(8,128)S(1)}, f32[512,128]{1,0:T(8,128)S(1)}, u32[]{:S(2)}, u32[]{:S(2)}) collective-permute-start(f32[512,128]{1,0:T(8,128)S(1)} %get-tuple-element.82.refs_0_), channel_id=1, source_target_pairs={{0,24},{4,28},{8,16},{12,20},{16,8},{20,12},{24,0},{28,4},{1,25},{... | collective-permute-start | bytes 786440 | tf_op jit(solution)/shard_map/ppermute | solution.py:277
  6.3 6.5 %collective-permute-done.5.refs_6_ = f32[512,128]{1,0:T(8,128)S(1)} collective-permute-done((f32[512,128]{1,0:T(8,128)S(1)}, f32[512,128]{1,0:T(8,128)S(1)}, u32[]{:S(2)}, u32[]{:S(2)}) %collective-permute-start.5) | collective-permute-done | bytes 262176 | tf_op jit(solution)/shard_map/ppermute | solution.py:277
  12.8 4.7 %collective-permute-done.3.refs_4_ = f32[512,128]{1,0:T(8,128)S(1)} collective-permute-done((f32[512,128]{1,0:T(8,128)S(1)}, f32[512,128]{1,0:T(8,128)S(1)}, u32[]{:S(2)}, u32[]{:S(2)}) %collective-permute-start.3) | collective-permute-done | bytes 262176 | tf_op jit(solution)/shard_map/ppermute | solution.py:277
  18.1 0.7 concatenate.9.ids
  18.8 1.8 %collective-permute-start.16 = (f32[512,128]{1,0:T(8,128)S(1)}, f32[512,128]{1,0:T(8,128)S(1)}, u32[]{:S(2)}, u32[]{:S(2)}) collective-permute-start(f32[512,128]{1,0:T(8,128)S(1)} %get-tuple-element.49.refs_0_), channel_id=1, source_target_pairs={{0,24},{4,28},{8,16},{12,20},{16,8},{20,12},{24,0},{28,4},{1,25},{... | collective-permute-start | bytes 786440 | tf_op jit(solution)/shard_map/ppermute | solution.py:277
  20.7 1.3 collective-permute-start.14
  23.1 5.6 %shard_map.85 = (f32[512,128]{1,0:T(8,128)S(1)}, f32[512,128]{1,0:T(8,128)S(1)}, f32[512,128]{1,0:T(8,128)S(1)}, f32[512,128]{1,0:T(8,128)S(1)}) custom-call(s32[196]{0:T(256)S(1)} %concatenate.9.ids, f32[96,128,128]{2,1,0:T(8,128)} %bitcast.7, f32[512,128]{1,0:T(8,128)S(1)} %get-tuple-element.82.refs_0_, f32[512,128]{1,0:T(8,128)S(1)} %collective-permute-done.refs_1_, ...), custom_call_target="tpu_custom_call" | custom-call | flops 1610612736 | bytes 9437184 | tf_op jit(solution)/shard_map/pallas_call | solution.py:201
  28.7 1.8 %collective-permute-start.7 = (f32[512,128]{1,0:T(8,128)S(1)}, f32[512,128]{1,0:T(8,128)S(1)}, u32[]{:S(2)}, u32[]{:S(2)}) collective-permute-start(f32[512,128]{1,0:T(8,128)S(1)} %get-tuple-element.42), channel_id=1, source_target_pairs={{0,1},{1,0},{2,3},{3,2},{4,5},{5,4},{6,7},{7,6},{8,9},{9,8},{10,11... | collective-permute-start | bytes 786440 | tf_op jit(solution)/shard_map/ppermute | solution.py:281
  31.3 2.5 %collective-permute-done.14.refs_4_ = f32[512,128]{1,0:T(8,128)S(1)} collective-permute-done((f32[512,128]{1,0:T(8,128)S(1)}, f32[512,128]{1,0:T(8,128)S(1)}, u32[]{:S(2)}, u32[]{:S(2)}) %collective-permute-start.14) | collective-permute-done | bytes 262176 | tf_op jit(solution)/shard_map/ppermute | solution.py:277
  34.5 2.0 %collective-permute-done.7.refs_1_ = f32[512,128]{1,0:T(8,128)S(1)} collective-permute-done((f32[512,128]{1,0:T(8,128)S(1)}, f32[512,128]{1,0:T(8,128)S(1)}, u32[]{:S(2)}, u32[]{:S(2)}) %collective-permute-start.7) | collective-permute-done | bytes 262176 | tf_op jit(solution)/shard_map/ppermute | solution.py:281
  36.5 5.8 %collective-permute-start.9 = (f32[512,128]{1,0:T(8,128)S(1)}, f32[512,128]{1,0:T(8,128)S(1)}, u32[]{:S(2)}, u32[]{:S(2)}) collective-permute-start(f32[512,128]{1,0:T(8,128)S(1)} %select_add_fusion.1), channel_id=1, source_target_pairs={{0,2},{1,3},{2,0},{3,1},{4,6},{5,7},{6,4},{7,5},{8,10},{9,11},{10,... | collective-permute-start | bytes 786440 | tf_op jit(solution)/shard_map/ppermute | solution.py:281
  42.3 1.3 collective-permute-start.10
  45.2 5.6 %shard_map.86 = (f32[512,128]{1,0:T(8,128)S(1)}, f32[512,128]{1,0:T(8,128)S(1)}, f32[512,128]{1,0:T(8,128)S(1)}, f32[512,128]{1,0:T(8,128)S(1)}) custom-call(s32[196]{0:T(256)S(1)} %concatenate.9.ids, f32[96,128,128]{2,1,0:T(8,128)} %bitcast.8, f32[512,128]{1,0:T(8,128)S(1)} %get-tuple-element.49.refs_0_, f32[512,128]{1,0:T(8,128)S(1)} %collective-permute-done.11.refs_1_, ...), custom_call_target="tpu_custom_call" | custom-call | flops 1610612736 | bytes 9437184 | tf_op jit(solution)/shard_map/pallas_call | solution.py:201
  50.8 1.7 %collective-permute-done.9.refs_3_ = f32[512,128]{1,0:T(8,128)S(1)} collective-permute-done((f32[512,128]{1,0:T(8,128)S(1)}, f32[512,128]{1,0:T(8,128)S(1)}, u32[]{:S(2)}, u32[]{:S(2)}) %collective-permute-start.9) | collective-permute-done | bytes 262176 | tf_op jit(solution)/shard_map/ppermute | solution.py:281
  52.5 1.8 %collective-permute-start.18 = (f32[512,128]{1,0:T(8,128)S(1)}, f32[512,128]{1,0:T(8,128)S(1)}, u32[]{:S(2)}, u32[]{:S(2)}) collective-permute-start(f32[512,128]{1,0:T(8,128)S(1)} %get-tuple-element.55), channel_id=1, source_target_pairs={{0,1},{1,0},{2,3},{3,2},{4,5},{5,4},{6,7},{7,6},{8,9},{9,8},{10,11... | collective-permute-start | bytes 786440 | tf_op jit(solution)/shard_map/ppermute | solution.py:281
  54.9 4.5 %collective-permute-done.18.refs_6_ = f32[512,128]{1,0:T(8,128)S(1)} collective-permute-done((f32[512,128]{1,0:T(8,128)S(1)}, f32[512,128]{1,0:T(8,128)S(1)}, u32[]{:S(2)}, u32[]{:S(2)}) %collective-permute-start.18) | collective-permute-done | bytes 262176 | tf_op jit(solution)/shard_map/ppermute | solution.py:281
  59.5 6.0 %collective-permute-start.20 = (f32[512,128]{1,0:T(8,128)S(1)}, f32[512,128]{1,0:T(8,128)S(1)}, u32[]{:S(2)}, u32[]{:S(2)}) collective-permute-start(f32[512,128]{1,0:T(8,128)S(1)} %select_add_fusion), channel_id=1, source_target_pairs={{0,2},{1,3},{2,0},{3,1},{4,6},{5,7},{6,4},{7,5},{8,10},{9,11},{10,... | collective-permute-start | bytes 786440 | tf_op jit(solution)/shard_map/ppermute | solution.py:281
  65.5 1.3 collective-permute-start.21
  66.8 8.8 %collective-permute-done.20.refs_8_ = f32[512,128]{1,0:T(8,128)S(1)} collective-permute-done((f32[512,128]{1,0:T(8,128)S(1)}, f32[512,128]{1,0:T(8,128)S(1)}, u32[]{:S(2)}, u32[]{:S(2)}) %collective-permute-start.20) | collective-permute-done | bytes 262176 | tf_op jit(solution)/shard_map/ppermute | solution.py:281
  76.5 3.2 %shard_map.87 = (f32[512,256]{1,0:T(8,128)}, f32[512,256]{1,0:T(8,128)}, f32[256,256]{1,0:T(8,128)S(1)}) custom-call(s32[196]{0:T(256)S(1)} %concatenate.9.ids, f32[512,128]{1,0:T(8,128)S(1)} %get-tuple-element.41.refs_0_, f32[512,128]{1,0:T(8,128)S(1)} %collective-permute-done.7.refs_1_, f32[512,128]{1,0:T(8,128)S(1)} %collective-permute-done.8.refs_2_, ...), custom_call_target="tpu_custom_call" | custom-call | flops 1000 | bytes 1000 | tf_op jit(solution)/shard_map/pallas_call | solution.py:259
  79.7 1.7 %collective-permute-start.23 = (f32[512,256]{1,0:T(8,128)}, f32[512,256]{1,0:T(8,128)S(1)}, u32[]{:S(2)}, u32[]{:S(2)}) collective-permute-start(f32[512,256]{1,0:T(8,128)} %get-tuple-element.65.refs_0_), channel_id=1, source_target_pairs={{0,2},{3,1},{1,0},{2,3},{4,6},{7,5},{5,4},{6,7},{8,10},{11,9},{9,8... | collective-permute-start | bytes 1572872 | tf_op jit(solution)/shard_map/ppermute | solution.py:281
  81.5 11.0 %collective-permute-done.23.refs_1_ = f32[512,256]{1,0:T(8,128)S(1)} collective-permute-done((f32[512,256]{1,0:T(8,128)}, f32[512,256]{1,0:T(8,128)S(1)}, u32[]{:S(2)}, u32[]{:S(2)}) %collective-permute-start.23) | collective-permute-done | bytes 524320 | tf_op jit(solution)/shard_map/ppermute | solution.py:281
  93.2 3.3 %collective-permute-start.27 = (f32[512,256]{1,0:T(8,128)}, f32[512,256]{1,0:T(8,128)S(1)}, u32[]{:S(2)}, u32[]{:S(2)}) collective-permute-start(f32[512,256]{1,0:T(8,128)} %get-tuple-element.65.refs_0_), channel_id=1, source_target_pairs={{2,0},{1,3},{0,1},{3,2},{6,4},{5,7},{4,5},{7,6},{10,8},{9,11},{8,9... | collective-permute-start | bytes 1572872 | tf_op jit(solution)/shard_map/ppermute | solution.py:281
  96.4 1.3 collective-permute-start.29
  97.8 1.9 %collective-permute-start.26 = (f32[128,256]{1,0:T(8,128)S(1)}, f32[128,256]{1,0:T(8,128)S(1)}, u32[]{:S(2)}, u32[]{:S(2)}) collective-permute-start(f32[128,256]{1,0:T(8,128)S(1)} %dynamic-slice_add_fusion), channel_id=1, source_target_pairs={{0,24},{4,28},{8,16},{12,20},{16,8},{20,12},{24,0},{28,4},{1,25},{... | collective-permute-start | bytes 393224 | tf_op jit(solution)/shard_map/ppermute | solution.py:277
  99.6 1.2 collective-permute-start.25
  100.8 4.2 %collective-permute-done.26 = f32[128,256]{1,0:T(8,128)S(1)} collective-permute-done((f32[128,256]{1,0:T(8,128)S(1)}, f32[128,256]{1,0:T(8,128)S(1)}, u32[]{:S(2)}, u32[]{:S(2)}) %collective-permute-start.26) | collective-permute-done | bytes 131104 | tf_op jit(solution)/shard_map/ppermute | solution.py:277
  105.0 1.2 collective-permute-start.24
  106.1 1.0 copy-done
  107.2 9.7 %shard_map.88 = (f32[4096,256]{1,0:T(8,128)}, s32[97]{0:T(128)S(1)}) custom-call(s32[196]{0:T(256)S(1)} %concatenate.9.ids, f32[96,128,128]{2,1,0:T(8,128)} %bitcast.9, f32[512,256]{1,0:T(8,128)S(1)} %copy-done, f32[512,256]{1,0:T(8,128)S(1)} %collective-permute-done.23.refs_1_), custom_call_target="tpu_custom_call" | custom-call | flops 3221225472 | bytes 11534336 | tf_op jit(solution)/shard_map/pallas_call | solution.py:201
  117.0 2.6 %collective-permute-done.29.refs_2_ = f32[512,256]{1,0:T(8,128)S(1)} collective-permute-done((f32[512,256]{1,0:T(8,128)S(1)}, f32[512,256]{1,0:T(8,128)S(1)}, u32[]{:S(2)}, u32[]{:S(2)}) %collective-permute-start.29) | collective-permute-done | bytes 524320 | tf_op jit(solution)/shard_map/ppermute | solution.py:281
  119.5 0.8 copy-done.4
  120.3 9.3 %shard_map.89 = (f32[512,256]{1,0:T(8,128)S(1)}, f32[512,256]{1,0:T(8,128)S(1)}, f32[512,256]{1,0:T(8,128)S(1)}, f32[512,256]{1,0:T(8,128)}, f32[512,256]{1,0:T(...) custom-call(s32[196]{0:T(256)S(1)} %concatenate.9.ids, f32[96,128,128]{2,1,0:T(8,128)} %bitcast.10, ...), custom_call_target="tpu_custom_call" | custom-call | flops 3221225472 | bytes 11534336 | tf_op jit(solution)/shard_map/pallas_call | solution.py:201
  130.3 1.5 collective-permute-done.35
  131.9 1.1 add.76
  133.0 2.2 %collective-permute-start.36 = (f32[256,256]{1,0:T(8,128)S(1)}, f32[256,256]{1,0:T(8,128)S(1)}, u32[]{:S(2)}, u32[]{:S(2)}) collective-permute-start(f32[256,256]{1,0:T(8,128)S(1)} %get-tuple-element.79), channel_id=1, source_target_pairs={{0,16},{4,20},{8,24},{12,28},{16,0},{20,4},{24,8},{28,12},{1,17},{... | collective-permute-start | bytes 786440 | tf_op jit(solution)/shard_map/ppermute | solution.py:277
  135.2 0.8 collective-permute-start.39
  136.1 5.0 %collective-permute-done.30 = f32[128,256]{1,0:T(8,128)S(1)} collective-permute-done((f32[128,256]{1,0:T(8,128)S(1)}, f32[128,256]{1,0:T(8,128)S(1)}, u32[]{:S(2)}, u32[]{:S(2)}) %collective-permute-start.30) | collective-permute-done | bytes 131104 | tf_op jit(solution)/shard_map/ppermute | solution.py:281
  141.1 2.2 %collective-permute-done.39 = f32[256,256]{1,0:T(8,128)S(1)} collective-permute-done((f32[256,256]{1,0:T(8,128)S(1)}, f32[256,256]{1,0:T(8,128)S(1)}, u32[]{:S(2)}, u32[]{:S(2)}) %collective-permute-start.39) | collective-permute-done | bytes 262176 | tf_op jit(solution)/shard_map/ppermute | solution.py:277
  143.4 0.9 collective-permute-start.37
  144.2 1.9 %pad_add_fusion = f32[512,256]{1,0:T(8,128)} fusion(f32[256,256]{1,0:T(8,128)S(1)} %collective-permute-done.39, f32[512,256]{1,0:T(8,128)} %get-tuple-element.76, f32[512,256]{1,0:T(8,128)S(1)} %collective-permute-done.38), kind=kLoop, calls=%fused_computation | loop fusion | flops 262144 | bytes 1835008 | tf_op jit(solution)/shard_map/add | solution.py:365
  146.2 1.1 collective-permute-start.40
  147.3 6.8 %collective-permute-done.31 = f32[128,256]{1,0:T(8,128)S(1)} collective-permute-done((f32[128,256]{1,0:T(8,128)S(1)}, f32[128,256]{1,0:T(8,128)S(1)}, u32[]{:S(2)}, u32[]{:S(2)}) %collective-permute-start.31) | collective-permute-done | bytes 131104 | tf_op jit(solution)/shard_map/ppermute | solution.py:281
  154.2 1.3 collective-permute-done.32
  155.6 0.7 fusion
  156.3 2.6 %collective-permute-done.40 = f32[512,256]{1,0:T(8,128)S(1)} collective-permute-done((f32[512,256]{1,0:T(8,128)}, f32[512,256]{1,0:T(8,128)S(1)}, u32[]{:S(2)}, u32[]{:S(2)}) %collective-permute-start.40) | collective-permute-done | bytes 524320 | tf_op jit(solution)/shard_map/ppermute | solution.py:277
  158.9 0.9 add_add_fusion
  (90 shorter events, 8.5 us)
Async XLA Ops:
  1.7 11.1 %collective-permute-start.5 = (f32[512,128]{1,0:T(8,128)S(1)}, f32[512,128]{1,0:T(8,128)S(1)}, u32[]{:S(2)}, u32[]{:S(2)}) collective-permute-start(f32[512,128]{1,0:T(8,128)S(1)} %get-tuple-element.82.refs_0_), channel_id=1, source_target_pairs={{0,24},{4,28},{8,16},{12,20},{16,8},{20,12},{24,0},{28,4},{1,25},{... | collective-permute-start | bytes 786440 | tf_op jit(solution)/shard_map/ppermute | solution.py:277
  5.7 11.9 %collective-permute-start.3 = (f32[512,128]{1,0:T(8,128)S(1)}, f32[512,128]{1,0:T(8,128)S(1)}, u32[]{:S(2)}, u32[]{:S(2)}) collective-permute-start(f32[512,128]{1,0:T(8,128)S(1)} %get-tuple-element.82.refs_0_), channel_id=1, source_target_pairs={{0,16},{4,20},{8,24},{12,28},{16,0},{20,4},{24,8},{28,12},{1,17},{... | collective-permute-start | bytes 786440 | tf_op jit(solution)/shard_map/ppermute | solution.py:277
  6.2 11.7 %collective-permute-start.1 = (f32[512,128]{1,0:T(8,128)S(1)}, f32[512,128]{1,0:T(8,128)S(1)}, u32[]{:S(2)}, u32[]{:S(2)}) collective-permute-start(f32[512,128]{1,0:T(8,128)S(1)} %get-tuple-element.82.refs_0_), channel_id=1, source_target_pairs={{0,8},{4,12},{8,0},{12,4},{16,24},{20,28},{24,16},{28,20},{1,9},{5... | collective-permute-start | bytes 786440 | tf_op jit(solution)/shard_map/ppermute | solution.py:277
  6.3 14.4 %collective-permute-start = (f32[512,128]{1,0:T(8,128)S(1)}, f32[512,128]{1,0:T(8,128)S(1)}, u32[]{:S(2)}, u32[]{:S(2)}) collective-permute-start(f32[512,128]{1,0:T(8,128)S(1)} %get-tuple-element.82.refs_0_), channel_id=1, source_target_pairs={{0,4},{4,0},{8,12},{12,8},{16,20},{20,16},{24,28},{28,24},{1,5},{5... | collective-permute-start | bytes 786440 | tf_op jit(solution)/shard_map/ppermute | solution.py:277
  12.8 9.5 %copy-start.7 = (f32[512,128]{1,0:T(8,128)}, f32[512,128]{1,0:T(8,128)S(1)}, u32[]{:S(2)}) copy-start(f32[512,128]{1,0:T(8,128)S(1)} %collective-permute-done.5.refs_6_) | copy-start | bytes 786436
  12.8 9.2 %collective-permute-start.6 = (f32[512,128]{1,0:T(8,128)S(1)}, f32[512,128]{1,0:T(8,128)S(1)}, u32[]{:S(2)}, u32[]{:S(2)}) collective-permute-start(f32[512,128]{1,0:T(8,128)S(1)} %collective-permute-done.5.refs_6_), channel_id=1, source_target_pairs={{0,4},{4,0},{8,12},{12,8},{16,20},{20,16},{24,28},{28,24},{1,5},{5... | collective-permute-start | bytes 786440 | tf_op jit(solution)/shard_map/ppermute | solution.py:277
  17.6 4.8 %copy-start.8 = (f32[512,128]{1,0:T(8,128)}, f32[512,128]{1,0:T(8,128)S(1)}, u32[]{:S(2)}) copy-start(f32[512,128]{1,0:T(8,128)S(1)} %collective-permute-done.3.refs_4_) | copy-start | bytes 786436
  17.6 4.8 %collective-permute-start.4 = (f32[512,128]{1,0:T(8,128)S(1)}, f32[512,128]{1,0:T(8,128)S(1)}, u32[]{:S(2)}, u32[]{:S(2)}) collective-permute-start(f32[512,128]{1,0:T(8,128)S(1)} %collective-permute-done.3.refs_4_), channel_id=1, source_target_pairs={{0,4},{4,0},{8,12},{12,8},{16,20},{20,16},{24,28},{28,24},{1,5},{5... | collective-permute-start | bytes 786440 | tf_op jit(solution)/shard_map/ppermute | solution.py:277
  17.9 4.5 %collective-permute-start.2 = (f32[512,128]{1,0:T(8,128)S(1)}, f32[512,128]{1,0:T(8,128)S(1)}, u32[]{:S(2)}, u32[]{:S(2)}) collective-permute-start(f32[512,128]{1,0:T(8,128)S(1)} %collective-permute-done.1.refs_2_), channel_id=1, source_target_pairs={{0,4},{4,0},{8,12},{12,8},{16,20},{20,16},{24,28},{28,24},{1,5},{5... | collective-permute-start | bytes 786440 | tf_op jit(solution)/shard_map/ppermute | solution.py:277
  18.8 12.4 %collective-permute-start.16 = (f32[512,128]{1,0:T(8,128)S(1)}, f32[512,128]{1,0:T(8,128)S(1)}, u32[]{:S(2)}, u32[]{:S(2)}) collective-permute-start(f32[512,128]{1,0:T(8,128)S(1)} %get-tuple-element.49.refs_0_), channel_id=1, source_target_pairs={{0,24},{4,28},{8,16},{12,20},{16,8},{20,12},{24,0},{28,4},{1,25},{... | collective-permute-start | bytes 786440 | tf_op jit(solution)/shard_map/ppermute | solution.py:277
  20.7 13.2 %collective-permute-start.14 = (f32[512,128]{1,0:T(8,128)S(1)}, f32[512,128]{1,0:T(8,128)S(1)}, u32[]{:S(2)}, u32[]{:S(2)}) collective-permute-start(f32[512,128]{1,0:T(8,128)S(1)} %get-tuple-element.49.refs_0_), channel_id=1, source_target_pairs={{0,16},{4,20},{8,24},{12,28},{16,0},{20,4},{24,8},{28,12},{1,17},{... | collective-permute-start | bytes 786440 | tf_op jit(solution)/shard_map/ppermute | solution.py:277
  22.0 11.9 %collective-permute-start.12 = (f32[512,128]{1,0:T(8,128)S(1)}, f32[512,128]{1,0:T(8,128)S(1)}, u32[]{:S(2)}, u32[]{:S(2)}) collective-permute-start(f32[512,128]{1,0:T(8,128)S(1)} %get-tuple-element.49.refs_0_), channel_id=1, source_target_pairs={{0,8},{4,12},{8,0},{12,4},{16,24},{20,28},{24,16},{28,20},{1,9},{5... | collective-permute-start | bytes 786440 | tf_op jit(solution)/shard_map/ppermute | solution.py:277
  28.7 7.7 %collective-permute-start.7 = (f32[512,128]{1,0:T(8,128)S(1)}, f32[512,128]{1,0:T(8,128)S(1)}, u32[]{:S(2)}, u32[]{:S(2)}) collective-permute-start(f32[512,128]{1,0:T(8,128)S(1)} %get-tuple-element.42), channel_id=1, source_target_pairs={{0,1},{1,0},{2,3},{3,2},{4,5},{5,4},{6,7},{7,6},{8,9},{9,8},{10,11... | collective-permute-start | bytes 786440 | tf_op jit(solution)/shard_map/ppermute | solution.py:281
  30.6 5.9 %collective-permute-start.8 = (f32[512,128]{1,0:T(8,128)S(1)}, f32[512,128]{1,0:T(8,128)S(1)}, u32[]{:S(2)}, u32[]{:S(2)}) collective-permute-start(f32[512,128]{1,0:T(8,128)S(1)} %get-tuple-element.46), channel_id=1, source_target_pairs={{1,2},{2,1},{5,6},{6,5},{9,10},{10,9},{13,14},{14,13},{17,18},{18,... | collective-permute-start | bytes 786440 | tf_op jit(solution)/shard_map/ppermute | solution.py:281
  31.3 12.4 %copy-start.5 = (f32[512,128]{1,0:T(8,128)}, f32[512,128]{1,0:T(8,128)S(1)}, u32[]{:S(2)}) copy-start(f32[512,128]{1,0:T(8,128)S(1)} %collective-permute-done.16.refs_6_) | copy-start | bytes 786436
  31.3 11.1 %collective-permute-start.11 = (f32[512,128]{1,0:T(8,128)S(1)}, f32[512,128]{1,0:T(8,128)S(1)}, u32[]{:S(2)}, u32[]{:S(2)}) collective-permute-start(f32[512,128]{1,0:T(8,128)S(1)} %get-tuple-element.49.refs_0_), channel_id=1, source_target_pairs={{0,4},{4,0},{8,12},{12,8},{16,20},{20,16},{24,28},{28,24},{1,5},{5... | collective-permute-start | bytes 786440 | tf_op jit(solution)/shard_map/ppermute | solution.py:277
  33.9 9.8 %copy-start.6 = (f32[512,128]{1,0:T(8,128)}, f32[512,128]{1,0:T(8,128)S(1)}, u32[]{:S(2)}) copy-start(f32[512,128]{1,0:T(8,128)S(1)} %collective-permute-done.14.refs_4_) | copy-start | bytes 786436
  33.9 9.7 %collective-permute-start.13 = (f32[512,128]{1,0:T(8,128)S(1)}, f32[512,128]{1,0:T(8,128)S(1)}, u32[]{:S(2)}, u32[]{:S(2)}) collective-permute-start(f32[512,128]{1,0:T(8,128)S(1)} %collective-permute-done.12.refs_2_), channel_id=1, source_target_pairs={{0,4},{4,0},{8,12},{12,8},{16,20},{20,16},{24,28},{28,24},{1,5},{5... | collective-permute-start | bytes 786440 | tf_op jit(solution)/shard_map/ppermute | solution.py:277
  33.9 9.7 %collective-permute-start.15 = (f32[512,128]{1,0:T(8,128)S(1)}, f32[512,128]{1,0:T(8,128)S(1)}, u32[]{:S(2)}, u32[]{:S(2)}) collective-permute-start(f32[512,128]{1,0:T(8,128)S(1)} %collective-permute-done.14.refs_4_), channel_id=1, source_target_pairs={{0,4},{4,0},{8,12},{12,8},{16,20},{20,16},{24,28},{28,24},{1,5},{5... | collective-permute-start | bytes 786440 | tf_op jit(solution)/shard_map/ppermute | solution.py:277
  36.5 7.2 %collective-permute-start.17 = (f32[512,128]{1,0:T(8,128)S(1)}, f32[512,128]{1,0:T(8,128)S(1)}, u32[]{:S(2)}, u32[]{:S(2)}) collective-permute-start(f32[512,128]{1,0:T(8,128)S(1)} %collective-permute-done.16.refs_6_), channel_id=1, source_target_pairs={{0,4},{4,0},{8,12},{12,8},{16,20},{20,16},{24,28},{28,24},{1,5},{5... | collective-permute-start | bytes 786440 | tf_op jit(solution)/shard_map/ppermute | solution.py:277
  36.5 16.0 %collective-permute-start.9 = (f32[512,128]{1,0:T(8,128)S(1)}, f32[512,128]{1,0:T(8,128)S(1)}, u32[]{:S(2)}, u32[]{:S(2)}) collective-permute-start(f32[512,128]{1,0:T(8,128)S(1)} %select_add_fusion.1), channel_id=1, source_target_pairs={{0,2},{1,3},{2,0},{3,1},{4,6},{5,7},{6,4},{7,5},{8,10},{9,11},{10,... | collective-permute-start | bytes 786440 | tf_op jit(solution)/shard_map/ppermute | solution.py:281
  42.3 10.1 %collective-permute-start.10 = (f32[512,128]{1,0:T(8,128)S(1)}, f32[512,128]{1,0:T(8,128)S(1)}, u32[]{:S(2)}, u32[]{:S(2)}) collective-permute-start(f32[512,128]{1,0:T(8,128)S(1)} %get-tuple-element.46), channel_id=1, source_target_pairs={{0,1},{3,2},{4,5},{7,6},{8,9},{11,10},{12,13},{15,14},{16,17},{19,... | collective-permute-start | bytes 786440 | tf_op jit(solution)/shard_map/ppermute | solution.py:281
  52.5 7.0 %collective-permute-start.18 = (f32[512,128]{1,0:T(8,128)S(1)}, f32[512,128]{1,0:T(8,128)S(1)}, u32[]{:S(2)}, u32[]{:S(2)}) collective-permute-start(f32[512,128]{1,0:T(8,128)S(1)} %get-tuple-element.55), channel_id=1, source_target_pairs={{0,1},{1,0},{2,3},{3,2},{4,5},{5,4},{6,7},{7,6},{8,9},{9,8},{10,11... | collective-permute-start | bytes 786440 | tf_op jit(solution)/shard_map/ppermute | solution.py:281
  54.3 5.2 %collective-permute-start.19 = (f32[512,128]{1,0:T(8,128)S(1)}, f32[512,128]{1,0:T(8,128)S(1)}, u32[]{:S(2)}, u32[]{:S(2)}) collective-permute-start(f32[512,128]{1,0:T(8,128)S(1)} %get-tuple-element.60), channel_id=1, source_target_pairs={{1,2},{2,1},{5,6},{6,5},{9,10},{10,9},{13,14},{14,13},{17,18},{18,... | collective-permute-start | bytes 786440 | tf_op jit(solution)/shard_map/ppermute | solution.py:281
  59.5 16.2 %copy-start.1 = (f32[512,128]{1,0:T(8,128)}, f32[512,128]{1,0:T(8,128)S(1)}, u32[]{:S(2)}) copy-start(f32[512,128]{1,0:T(8,128)S(1)} %collective-permute-done.18.refs_6_) | copy-start | bytes 786436
  59.5 16.2 %copy-start.15 = (f32[512,128]{1,0:T(8,128)}, f32[512,128]{1,0:T(8,128)S(1)}, u32[]{:S(2)}) copy-start(f32[512,128]{1,0:T(8,128)S(1)} %collective-permute-done.19.refs_7_) | copy-start | bytes 786436
  59.5 16.1 %collective-permute-start.20 = (f32[512,128]{1,0:T(8,128)S(1)}, f32[512,128]{1,0:T(8,128)S(1)}, u32[]{:S(2)}, u32[]{:S(2)}) collective-permute-start(f32[512,128]{1,0:T(8,128)S(1)} %select_add_fusion), channel_id=1, source_target_pairs={{0,2},{1,3},{2,0},{3,1},{4,6},{5,7},{6,4},{7,5},{8,10},{9,11},{10,... | collective-permute-start | bytes 786440 | tf_op jit(solution)/shard_map/ppermute | solution.py:281
  65.5 10.1 %collective-permute-start.21 = (f32[512,128]{1,0:T(8,128)S(1)}, f32[512,128]{1,0:T(8,128)S(1)}, u32[]{:S(2)}, u32[]{:S(2)}) collective-permute-start(f32[512,128]{1,0:T(8,128)S(1)} %get-tuple-element.60), channel_id=1, source_target_pairs={{0,1},{3,2},{4,5},{7,6},{8,9},{11,10},{12,13},{15,14},{16,17},{19,... | collective-permute-start | bytes 786440 | tf_op jit(solution)/shard_map/ppermute | solution.py:281
  79.7 12.8 %collective-permute-start.23 = (f32[512,256]{1,0:T(8,128)}, f32[512,256]{1,0:T(8,128)S(1)}, u32[]{:S(2)}, u32[]{:S(2)}) collective-permute-start(f32[512,256]{1,0:T(8,128)} %get-tuple-element.65.refs_0_), channel_id=1, source_target_pairs={{0,2},{3,1},{1,0},{2,3},{4,6},{7,5},{5,4},{6,7},{8,10},{11,9},{9,8... | collective-permute-start | bytes 1572872 | tf_op jit(solution)/shard_map/ppermute | solution.py:281
  81.4 16.4 %collective-permute-start.22 = (f32[128,256]{1,0:T(8,128)S(1)}, f32[128,256]{1,0:T(8,128)S(1)}, u32[]{:S(2)}, u32[]{:S(2)}) collective-permute-start(f32[128,256]{1,0:T(8,128)S(1)} %constant_dynamic-slice_fusion), channel_id=1, source_target_pairs={{0,4},{4,0},{8,12},{12,8},{16,20},{20,16},{24,28},{28,24},{1,5},{5... | collective-permute-start | bytes 393224 | tf_op jit(solution)/shard_map/ppermute | solution.py:277
  92.5 24.5 %collective-permute-start.28 = (f32[512,256]{1,0:T(8,128)}, f32[512,256]{1,0:T(8,128)S(1)}, u32[]{:S(2)}, u32[]{:S(2)}) collective-permute-start(f32[512,256]{1,0:T(8,128)} %get-tuple-element.65.refs_0_), channel_id=1, source_target_pairs={{1,2},{2,1},{5,6},{6,5},{9,10},{10,9},{13,14},{14,13},{17,18},{18,... | collective-permute-start | bytes 1572872 | tf_op jit(solution)/shard_map/ppermute | solution.py:281
  93.2 23.8 %collective-permute-start.27 = (f32[512,256]{1,0:T(8,128)}, f32[512,256]{1,0:T(8,128)S(1)}, u32[]{:S(2)}, u32[]{:S(2)}) collective-permute-start(f32[512,256]{1,0:T(8,128)} %get-tuple-element.65.refs_0_), channel_id=1, source_target_pairs={{2,0},{1,3},{0,1},{3,2},{6,4},{5,7},{4,5},{7,6},{10,8},{9,11},{8,9... | collective-permute-start | bytes 1572872 | tf_op jit(solution)/shard_map/ppermute | solution.py:281
  96.4 23.1 %collective-permute-start.29 = (f32[512,256]{1,0:T(8,128)S(1)}, f32[512,256]{1,0:T(8,128)S(1)}, u32[]{:S(2)}, u32[]{:S(2)}) collective-permute-start(f32[512,256]{1,0:T(8,128)S(1)} %collective-permute-done.23.refs_1_), channel_id=1, source_target_pairs={{1,0},{2,3},{5,4},{6,7},{9,8},{10,11},{13,12},{14,15},{17,16},{18,... | collective-permute-start | bytes 1572872 | tf_op jit(solution)/shard_map/ppermute | solution.py:281
  97.8 7.2 %collective-permute-start.26 = (f32[128,256]{1,0:T(8,128)S(1)}, f32[128,256]{1,0:T(8,128)S(1)}, u32[]{:S(2)}, u32[]{:S(2)}) collective-permute-start(f32[128,256]{1,0:T(8,128)S(1)} %dynamic-slice_add_fusion), channel_id=1, source_target_pairs={{0,24},{4,28},{8,16},{12,20},{16,8},{20,12},{24,0},{28,4},{1,25},{... | collective-permute-start | bytes 393224 | tf_op jit(solution)/shard_map/ppermute | solution.py:277
  99.6 17.3 %collective-permute-start.25 = (f32[128,256]{1,0:T(8,128)S(1)}, f32[128,256]{1,0:T(8,128)S(1)}, u32[]{:S(2)}, u32[]{:S(2)}) collective-permute-start(f32[128,256]{1,0:T(8,128)S(1)} %dynamic-slice_add_fusion), channel_id=1, source_target_pairs={{0,16},{4,20},{8,24},{12,28},{16,0},{20,4},{24,8},{28,12},{1,17},{... | collective-permute-start | bytes 393224 | tf_op jit(solution)/shard_map/ppermute | solution.py:277
  105.0 12.0 %collective-permute-start.24 = (f32[128,256]{1,0:T(8,128)S(1)}, f32[128,256]{1,0:T(8,128)S(1)}, u32[]{:S(2)}, u32[]{:S(2)}) collective-permute-start(f32[128,256]{1,0:T(8,128)S(1)} %dynamic-slice_add_fusion), channel_id=1, source_target_pairs={{0,8},{4,12},{8,0},{12,4},{16,24},{20,28},{24,16},{28,20},{1,9},{5... | collective-permute-start | bytes 393224 | tf_op jit(solution)/shard_map/ppermute | solution.py:277
  116.9 2.6 %copy-start.3 = (f32[512,256]{1,0:T(8,128)}, f32[512,256]{1,0:T(8,128)S(1)}, u32[]{:S(2)}) copy-start(f32[512,256]{1,0:T(8,128)S(1)} %collective-permute-done.27.refs_0_) | copy-start | bytes 1572868
  129.7 2.2 %collective-permute-start.35 = (f32[512,256]{1,0:T(8,128)}, f32[512,256]{1,0:T(8,128)S(1)}, u32[]{:S(2)}, u32[]{:S(2)}) collective-permute-start(f32[512,256]{1,0:T(8,128)} %get-tuple-element.75), channel_id=1, source_target_pairs={{0,4},{4,0},{8,12},{12,8},{16,20},{20,16},{24,28},{28,24},{1,5},{5... | collective-permute-start | bytes 1572872 | tf_op jit(solution)/shard_map/ppermute | solution.py:277
  129.7 13.5 %collective-permute-start.34 = (f32[512,256]{1,0:T(8,128)}, f32[512,256]{1,0:T(8,128)S(1)}, u32[]{:S(2)}, u32[]{:S(2)}) collective-permute-start(f32[512,256]{1,0:T(8,128)} %get-tuple-element.73), channel_id=1, source_target_pairs={{0,4},{4,0},{8,12},{12,8},{16,20},{20,16},{24,28},{28,24},{1,5},{5... | collective-permute-start | bytes 1572872 | tf_op jit(solution)/shard_map/ppermute | solution.py:277
  130.2 14.0 %collective-permute-start.38 = (f32[512,256]{1,0:T(8,128)}, f32[512,256]{1,0:T(8,128)S(1)}, u32[]{:S(2)}, u32[]{:S(2)}) collective-permute-start(f32[512,256]{1,0:T(8,128)} %get-tuple-element.77), channel_id=1, source_target_pairs={{0,4},{4,0},{8,12},{12,8},{16,20},{20,16},{24,28},{28,24},{1,5},{5... | collective-permute-start | bytes 1572872 | tf_op jit(solution)/shard_map/ppermute | solution.py:277
  133.0 10.3 %collective-permute-start.36 = (f32[256,256]{1,0:T(8,128)S(1)}, f32[256,256]{1,0:T(8,128)S(1)}, u32[]{:S(2)}, u32[]{:S(2)}) collective-permute-start(f32[256,256]{1,0:T(8,128)S(1)} %get-tuple-element.79), channel_id=1, source_target_pairs={{0,16},{4,20},{8,24},{12,28},{16,0},{20,4},{24,8},{28,12},{1,17},{... | collective-permute-start | bytes 786440 | tf_op jit(solution)/shard_map/ppermute | solution.py:277
  135.2 8.1 %collective-permute-start.39 = (f32[256,256]{1,0:T(8,128)S(1)}, f32[256,256]{1,0:T(8,128)S(1)}, u32[]{:S(2)}, u32[]{:S(2)}) collective-permute-start(f32[256,256]{1,0:T(8,128)S(1)} %get-tuple-element.80), channel_id=1, source_target_pairs={{0,8},{4,12},{8,0},{12,4},{16,24},{20,28},{24,16},{28,20},{1,9},{5... | collective-permute-start | bytes 786440 | tf_op jit(solution)/shard_map/ppermute | solution.py:277
  136.0 5.0 %collective-permute-start.30 = (f32[128,256]{1,0:T(8,128)S(1)}, f32[128,256]{1,0:T(8,128)S(1)}, u32[]{:S(2)}, u32[]{:S(2)}) collective-permute-start(f32[128,256]{1,0:T(8,128)S(1)} %add_add_fusion.1), channel_id=1, source_target_pairs={{0,1},{1,0},{2,3},{3,2},{4,5},{5,4},{6,7},{7,6},{8,9},{9,8},{10,11... | collective-permute-start | bytes 393224 | tf_op jit(solution)/shard_map/ppermute | solution.py:281
  141.1 15.2 %collective-permute-start.33 = (f32[512,256]{1,0:T(8,128)S(1)}, f32[512,256]{1,0:T(8,128)S(1)}, u32[]{:S(2)}, u32[]{:S(2)}) collective-permute-start(f32[512,256]{1,0:T(8,128)S(1)} %get-tuple-element.71), channel_id=1, source_target_pairs={{0,4},{4,0},{8,12},{12,8},{16,20},{20,16},{24,28},{28,24},{1,5},{5... | collective-permute-start | bytes 1572872 | tf_op jit(solution)/shard_map/ppermute | solution.py:277
  143.4 12.9 %collective-permute-start.37 = (f32[512,256]{1,0:T(8,128)S(1)}, f32[512,256]{1,0:T(8,128)S(1)}, u32[]{:S(2)}, u32[]{:S(2)}) collective-permute-start(f32[512,256]{1,0:T(8,128)S(1)} %pad_add_fusion.1), channel_id=1, source_target_pairs={{0,8},{4,12},{8,0},{12,4},{16,24},{20,28},{24,16},{28,20},{1,9},{5... | collective-permute-start | bytes 1572872 | tf_op jit(solution)/shard_map/ppermute | solution.py:277
  146.2 12.7 %collective-permute-start.40 = (f32[512,256]{1,0:T(8,128)}, f32[512,256]{1,0:T(8,128)S(1)}, u32[]{:S(2)}, u32[]{:S(2)}) collective-permute-start(f32[512,256]{1,0:T(8,128)} %pad_add_fusion), channel_id=1, source_target_pairs={{0,16},{4,20},{8,24},{12,28},{16,0},{20,4},{24,8},{28,12},{1,17},{... | collective-permute-start | bytes 1572872 | tf_op jit(solution)/shard_map/ppermute | solution.py:277
  147.3 6.9 %collective-permute-start.31 = (f32[128,256]{1,0:T(8,128)S(1)}, f32[128,256]{1,0:T(8,128)S(1)}, u32[]{:S(2)}, u32[]{:S(2)}) collective-permute-start(f32[128,256]{1,0:T(8,128)S(1)} %add.72), channel_id=1, source_target_pairs={{0,2},{1,3},{2,0},{3,1},{4,6},{5,7},{6,4},{7,5},{8,10},{9,11},{10,... | collective-permute-start | bytes 393224 | tf_op jit(solution)/shard_map/ppermute | solution.py:281
  154.2 1.4 collective-permute-start.32
  (11 other events, 10.3 us)

commit v4 on v3

--- a/solution.py
+++ b/solution.py
@@ -1,4 +1,5 @@
 import functools
+import math
 
 import jax
 import jax.numpy as jnp
@@ -7,7 +8,7 @@
 from jax.experimental.pallas import tpu as pltpu
 from jax.sharding import PartitionSpec as P
 
-VMEM_LIMIT = 52 * 1024 * 1024
+MIB = 1024 * 1024
 
 OUTER = ((0, 1), (1, 0), (2, 3), (3, 2))
 MIDDLE = ((1, 2), (2, 1))
@@ -198,6 +199,12 @@
     in_rows = sum(group[0].shape[0] for group in groups)
     smem, anywhere = pl.BlockSpec(memory_space=pltpu.SMEM), pl.BlockSpec(memory_space=pl.ANY)
     lists = only is not None and not rest
+    buffers = [
+        pltpu.VMEM((sum(piece.shape[0] for piece in pieces), width), jnp.float32),
+        pltpu.VMEM((in_rows // size + 1, halves, 2 * size, 2 * (width // halves)), jnp.bfloat16),
+        pltpu.VMEM((sum(out_rows), width), jnp.float32),
+        pltpu.VMEM(values.shape, jnp.float32),
+    ]
     return pl.pallas_call(
         functools.partial(
             spmm_kernel,
@@ -214,17 +221,18 @@
         + [jax.ShapeDtypeStruct((count + 1,), jnp.int32)] * lists,
         in_specs=[smem] + [anywhere] * (1 + len(pieces)) + [anywhere, smem][: len(rest)],
         out_specs=[anywhere] * len(out_rows) + [smem] * lists,
-        scratch_shapes=[
-            pltpu.VMEM((sum(piece.shape[0] for piece in pieces), width), jnp.float32),
-            pltpu.VMEM((in_rows // size + 1, halves, 2 * size, 2 * (width // halves)), jnp.bfloat16),
-            pltpu.VMEM((sum(out_rows), width), jnp.float32),
-            pltpu.VMEM(values.shape, jnp.float32),
+        scratch_shapes=buffers
+        + [
             pltpu.SemaphoreType.DMA((steps if only is None else count,)),
             pltpu.SemaphoreType.DMA((len(pieces),)),
             pltpu.SemaphoreType.DMA((1,)),
             pltpu.SemaphoreType.DMA((len(out_rows),)),
         ],
-        compiler_params=pltpu.CompilerParams(vmem_limit_bytes=VMEM_LIMIT),
+        compiler_params=pltpu.CompilerParams(
+            vmem_limit_bytes=40 * MIB
+            if only
+            else sum(math.prod(b.shape) * b.dtype.itemsize for b in buffers) + 4 * MIB
+        ),
         cost_estimate=pl.CostEstimate(
             flops=8 * count * size * size * width,
             bytes_accessed=4 * (values.size + (in_rows + sum(out_rows)) * width),
@@ -264,7 +272,7 @@
             jax.ShapeDtypeStruct((rows, width), jnp.float32),
             jax.ShapeDtypeStruct((width, width), jnp.float32),
         ],
-        compiler_params=pltpu.CompilerParams(vmem_limit_bytes=VMEM_LIMIT),
+        compiler_params=pltpu.CompilerParams(vmem_limit_bytes=20 * MIB),
         cost_estimate=pl.CostEstimate(
             flops=1000,
             bytes_accessed=1000,
@@ -334,7 +342,7 @@
         first, second = features
         diagonal = along_row(first, 6)
         mine = [first, along_row(first, 2), along_row(first, 4), diagonal]
-        pieces = both_cores(mine)
+        pieces = both_cores(mine, ids)
         slots = spmm(ids, values, [[p] for p in pieces], [rows_dev] * 4, per, False)
         second = after(second, diagonal)
         mine = [second, along_row(second, 2), along_row(second, 4), along_row(second, 6)]

time: 159 us -> 154 us (0.969); the launches traced: 160 us -> 153 us
  waiting for transfers between devices: 68.4 us -> 64.5 us
  Pallas kernels: 33.4 us -> 30.5 us
  other arithmetic: 4.92 us -> 2.82 us
  starting transfers between devices: 45.3 us -> 47 us
    ppermute x14, starting transfers between devices: 26.4 us -> 30 us  [along_col(): return lax.ppermute(x, 'col', pairs)]
    ppermute x27, waiting for transfers between devices: 26 us -> 23.5 us  [along_row(): lax.ppermute(x, 'row', [(i, i ^ bit) for i in range(lax.axis_size('row'))])]
    ppermute x27, starting transfers between devices: 18.8 us -> 17.1 us  [along_row(): lax.ppermute(x, 'row', [(i, i ^ bit) for i in range(lax.axis_size('row'))])]
    pallas_call x4, Pallas kernels: 30.2 us -> 28.6 us  [spmm(): pl.pallas_call(functools.partial(spmm_kernel, [len(group) for group in gr...]
    unnamed x36 -> x8, local copies, waits for them, and re-layouts: 4.87 us -> 5.58 us
  transfers between devices with their start and end apart: 41 -> 41, of which waited for: 18 -> 16; matrix products, arithmetic and copies ran while one was open for 3% -> 2% of each run, Pallas kernels for 13% -> 15%
where the time goes in v4:
time: 154 us; the launch traced here: 153 us
  waiting for transfers between devices  64.5 us (42%)
  starting transfers between devices  47 us (31%)
  Pallas kernels  30.5 us (20%)
  local copies, waits for them, and re-layouts  7.44 us (5%)
  other arithmetic  2.82 us (2%)
    ppermute x14, waiting for transfers between devices, along_col(): return lax.ppermute(x, 'col', pairs)  41 us
    ppermute x14, starting transfers between devices, along_col(): return lax.ppermute(x, 'col', pairs)  30 us
    pallas_call x4, Pallas kernels, spmm(): pl.pallas_call(functools.partial(spmm_kernel, [len(group) for group in gr...  28.6 us
    ppermute x27, waiting for transfers between devices, along_row(): lax.ppermute(x, 'row', [(i, i ^ bit) for i in range(lax.axis_size('row'))])  23.5 us
    ppermute x27, starting transfers between devices, along_row(): lax.ppermute(x, 'row', [(i, i ^ bit) for i in range(lax.axis_size('row'))])  17.1 us
    unnamed x8, local copies, waits for them, and re-layouts  5.58 us
  transfers between devices with their start and end apart: 41, of which 16 were waited for; matrix products, arithmetic and copies ran while one was open for 2% of the time, Pallas kernels for 15%

profile of v4, /device:TPU:0, one launch (start us, length us, event | category | flops | bytes accessed | tf_op | source)
XLA Modules:
  0.0 153.2 jit_solution(4613957917350981693)
XLA Ops:
  0.6 1.1 fusion.2
  1.7 4.0 %collective-permute-start.5 = (f32[512,128]{1,0:T(8,128)S(1)}, f32[512,128]{1,0:T(8,128)S(1)}, u32[]{:S(2)}, u32[]{:S(2)}) collective-permute-start(f32[512,128]{1,0:T(8,128)S(1)} %get-tuple-element.45.refs_0_), channel_id=1, source_target_pairs={{0,24},{4,28},{8,16},{12,20},{16,8},{20,12},{24,0},{28,4},{1,25},{... | collective-permute-start | bytes 786440 | tf_op jit(solution)/shard_map/ppermute | solution.py:285
  6.3 0.7 concatenate.9.ids
  7.1 5.8 %collective-permute-done.5.refs_6_ = f32[512,128]{1,0:T(8,128)S(1)} collective-permute-done((f32[512,128]{1,0:T(8,128)S(1)}, f32[512,128]{1,0:T(8,128)S(1)}, u32[]{:S(2)}, u32[]{:S(2)}) %collective-permute-start.5) | collective-permute-done | bytes 262176 | tf_op jit(solution)/shard_map/ppermute | solution.py:285
  12.8 4.7 %collective-permute-done.3.refs_4_ = f32[512,128]{1,0:T(8,128)S(1)} collective-permute-done((f32[512,128]{1,0:T(8,128)S(1)}, f32[512,128]{1,0:T(8,128)S(1)}, u32[]{:S(2)}, u32[]{:S(2)}) %collective-permute-start.3) | collective-permute-done | bytes 262176 | tf_op jit(solution)/shard_map/ppermute | solution.py:285
  18.1 1.8 %collective-permute-start.16 = (f32[512,128]{1,0:T(8,128)S(1)}, f32[512,128]{1,0:T(8,128)S(1)}, u32[]{:S(2)}, u32[]{:S(2)}) collective-permute-start(f32[512,128]{1,0:T(8,128)S(1)} %get-tuple-element.57.refs_0_), channel_id=1, source_target_pairs={{0,24},{4,28},{8,16},{12,20},{16,8},{20,12},{24,0},{28,4},{1,25},{... | collective-permute-start | bytes 786440 | tf_op jit(solution)/shard_map/ppermute | solution.py:285
  19.9 1.3 collective-permute-start.14
  21.6 2.8 %copy-done = f32[1,1,96,128,128]{4,3,2,1,0:T(8,128)S(1)} copy-done((f32[1,1,96,128,128]{4,3,2,1,0:T(8,128)S(1)}, f32[1,1,96,128,128]{4,3,2,1,0:T(8,128)}, u32[]{:S(2)}) %copy-start) | copy-done | bytes 6291480
  24.4 3.9 %shard_map.85 = (f32[512,128]{1,0:T(8,128)S(1)}, f32[512,128]{1,0:T(8,128)S(1)}, f32[512,128]{1,0:T(8,128)S(1)}, f32[512,128]{1,0:T(8,128)S(1)}) custom-call(s32[196]{0:T(256)S(1)} %concatenate.9.ids, f32[96,128,128]{2,1,0:T(8,128)S(1)} %bitcast.8, f32[512,128]{1,0:T(8,128)S(1)} %get-tuple-element.45.refs_0_, f32[512,128]{1,0:T(8,128)S(1)} %collective-permute-done.refs_1_, ...), custom_call_target="tpu_custom_call" | custom-call | flops 1610612736 | bytes 9437184 | tf_op jit(solution)/shard_map/pallas_call | solution.py:208
  28.3 1.8 %collective-permute-start.7 = (f32[512,128]{1,0:T(8,128)S(1)}, f32[512,128]{1,0:T(8,128)S(1)}, u32[]{:S(2)}, u32[]{:S(2)}) collective-permute-start(f32[512,128]{1,0:T(8,128)S(1)} %get-tuple-element.50), channel_id=1, source_target_pairs={{0,1},{1,0},{2,3},{3,2},{4,5},{5,4},{6,7},{7,6},{8,9},{9,8},{10,11... | collective-permute-start | bytes 786440 | tf_op jit(solution)/shard_map/ppermute | solution.py:289
  30.2 0.7 collective-permute-start.8
  30.9 2.2 %collective-permute-done.14.refs_4_ = f32[512,128]{1,0:T(8,128)S(1)} collective-permute-done((f32[512,128]{1,0:T(8,128)S(1)}, f32[512,128]{1,0:T(8,128)S(1)}, u32[]{:S(2)}, u32[]{:S(2)}) %collective-permute-start.14) | collective-permute-done | bytes 262176 | tf_op jit(solution)/shard_map/ppermute | solution.py:285
  33.1 0.5 collective-permute-start.15
  33.6 2.4 %collective-permute-done.7.refs_1_ = f32[512,128]{1,0:T(8,128)S(1)} collective-permute-done((f32[512,128]{1,0:T(8,128)S(1)}, f32[512,128]{1,0:T(8,128)S(1)}, u32[]{:S(2)}, u32[]{:S(2)}) %collective-permute-start.7) | collective-permute-done | bytes 262176 | tf_op jit(solution)/shard_map/ppermute | solution.py:289
  36.1 5.8 %collective-permute-start.9 = (f32[512,128]{1,0:T(8,128)S(1)}, f32[512,128]{1,0:T(8,128)S(1)}, u32[]{:S(2)}, u32[]{:S(2)}) collective-permute-start(f32[512,128]{1,0:T(8,128)S(1)} %select_add_fusion.1), channel_id=1, source_target_pairs={{0,2},{1,3},{2,0},{3,1},{4,6},{5,7},{6,4},{7,5},{8,10},{9,11},{10,... | collective-permute-start | bytes 786440 | tf_op jit(solution)/shard_map/ppermute | solution.py:289
  41.9 1.3 collective-permute-start.10
  43.3 3.9 %shard_map.86 = (f32[512,128]{1,0:T(8,128)S(1)}, f32[512,128]{1,0:T(8,128)S(1)}, f32[512,128]{1,0:T(8,128)S(1)}, f32[512,128]{1,0:T(8,128)S(1)}) custom-call(s32[196]{0:T(256)S(1)} %concatenate.9.ids, f32[96,128,128]{2,1,0:T(8,128)S(1)} %bitcast.9, f32[512,128]{1,0:T(8,128)S(1)} %get-tuple-element.57.refs_0_, ...), custom_call_target="tpu_custom_call" | custom-call | flops 1610612736 | bytes 9437184 | tf_op jit(solution)/shard_map/pallas_call | solution.py:208
  47.2 4.9 %collective-permute-done.9.refs_3_ = f32[512,128]{1,0:T(8,128)S(1)} collective-permute-done((f32[512,128]{1,0:T(8,128)S(1)}, f32[512,128]{1,0:T(8,128)S(1)}, u32[]{:S(2)}, u32[]{:S(2)}) %collective-permute-start.9) | collective-permute-done | bytes 262176 | tf_op jit(solution)/shard_map/ppermute | solution.py:289
  52.1 1.8 %collective-permute-start.18 = (f32[512,128]{1,0:T(8,128)S(1)}, f32[512,128]{1,0:T(8,128)S(1)}, u32[]{:S(2)}, u32[]{:S(2)}) collective-permute-start(f32[512,128]{1,0:T(8,128)S(1)} %get-tuple-element.63), channel_id=1, source_target_pairs={{0,1},{1,0},{2,3},{3,2},{4,5},{5,4},{6,7},{7,6},{8,9},{9,8},{10,11... | collective-permute-start | bytes 786440 | tf_op jit(solution)/shard_map/ppermute | solution.py:289
  53.9 0.7 collective-permute-start.19
  54.5 4.5 %collective-permute-done.18.refs_6_ = f32[512,128]{1,0:T(8,128)S(1)} collective-permute-done((f32[512,128]{1,0:T(8,128)S(1)}, f32[512,128]{1,0:T(8,128)S(1)}, u32[]{:S(2)}, u32[]{:S(2)}) %collective-permute-start.18) | collective-permute-done | bytes 262176 | tf_op jit(solution)/shard_map/ppermute | solution.py:289
  59.1 6.0 %collective-permute-start.20 = (f32[512,128]{1,0:T(8,128)S(1)}, f32[512,128]{1,0:T(8,128)S(1)}, u32[]{:S(2)}, u32[]{:S(2)}) collective-permute-start(f32[512,128]{1,0:T(8,128)S(1)} %select_add_fusion), channel_id=1, source_target_pairs={{0,2},{1,3},{2,0},{3,1},{4,6},{5,7},{6,4},{7,5},{8,10},{9,11},{10,... | collective-permute-start | bytes 786440 | tf_op jit(solution)/shard_map/ppermute | solution.py:289
  65.1 1.3 collective-permute-start.21
  66.4 8.8 %collective-permute-done.20.refs_8_ = f32[512,128]{1,0:T(8,128)S(1)} collective-permute-done((f32[512,128]{1,0:T(8,128)S(1)}, f32[512,128]{1,0:T(8,128)S(1)}, u32[]{:S(2)}, u32[]{:S(2)}) %collective-permute-start.20) | collective-permute-done | bytes 262176 | tf_op jit(solution)/shard_map/ppermute | solution.py:289
  75.2 1.9 %shard_map.87 = (f32[512,256]{1,0:T(8,128)}, f32[512,256]{1,0:T(8,128)S(1)}, f32[256,256]{1,0:T(8,128)S(1)}) custom-call(s32[196]{0:T(256)S(1)} %concatenate.9.ids, f32[512,128]{1,0:T(8,128)S(1)} %get-tuple-element.49.refs_0_, f32[512,128]{1,0:T(8,128)S(1)} %collective-permute-done.7.refs_1_, f32[512,128]{1,0:T(8,128)S(1)} %collective-permute-done.8.refs_2_, ...), custom_call_target="tpu_custom_call" | custom-call | flops 1000 | bytes 1000 | tf_op jit(solution)/shard_map/pallas_call | solution.py:267
  77.1 1.8 %collective-permute-start.23 = (f32[512,256]{1,0:T(8,128)S(1)}, f32[512,256]{1,0:T(8,128)S(1)}, u32[]{:S(2)}, u32[]{:S(2)}) collective-permute-start(f32[512,256]{1,0:T(8,128)S(1)} %get-tuple-element.73.refs_0_), channel_id=1, source_target_pairs={{0,2},{3,1},{1,0},{2,3},{4,6},{7,5},{5,4},{6,7},{8,10},{11,9},{9,8... | collective-permute-start | bytes 1572872 | tf_op jit(solution)/shard_map/ppermute | solution.py:289
  79.0 10.7 %collective-permute-done.23.refs_1_ = f32[512,256]{1,0:T(8,128)S(1)} collective-permute-done((f32[512,256]{1,0:T(8,128)S(1)}, f32[512,256]{1,0:T(8,128)S(1)}, u32[]{:S(2)}, u32[]{:S(2)}) %collective-permute-start.23) | collective-permute-done | bytes 524320 | tf_op jit(solution)/shard_map/ppermute | solution.py:289
  89.7 0.7 collective-permute-start.28
  90.4 3.4 %collective-permute-start.27 = (f32[512,256]{1,0:T(8,128)S(1)}, f32[512,256]{1,0:T(8,128)S(1)}, u32[]{:S(2)}, u32[]{:S(2)}) collective-permute-start(f32[512,256]{1,0:T(8,128)S(1)} %get-tuple-element.73.refs_0_), channel_id=1, source_target_pairs={{2,0},{1,3},{0,1},{3,2},{6,4},{5,7},{4,5},{7,6},{10,8},{9,11},{8,9... | collective-permute-start | bytes 1572872 | tf_op jit(solution)/shard_map/ppermute | solution.py:289
  93.8 1.3 collective-permute-start.29
  95.1 2.0 %collective-permute-start.26 = (f32[128,256]{1,0:T(8,128)S(1)}, f32[128,256]{1,0:T(8,128)S(1)}, u32[]{:S(2)}, u32[]{:S(2)}) collective-permute-start(f32[128,256]{1,0:T(8,128)S(1)} %dynamic-slice_add_fusion), channel_id=1, source_target_pairs={{0,24},{4,28},{8,16},{12,20},{16,8},{20,12},{24,0},{28,4},{1,25},{... | collective-permute-start | bytes 393224 | tf_op jit(solution)/shard_map/ppermute | solution.py:285
  97.1 1.0 collective-permute-start.25
  98.1 4.0 %collective-permute-done.26 = f32[128,256]{1,0:T(8,128)S(1)} collective-permute-done((f32[128,256]{1,0:T(8,128)S(1)}, f32[128,256]{1,0:T(8,128)S(1)}, u32[]{:S(2)}, u32[]{:S(2)}) %collective-permute-start.26) | collective-permute-done | bytes 131104 | tf_op jit(solution)/shard_map/ppermute | solution.py:285
  102.2 1.6 %collective-permute-start.24 = (f32[128,256]{1,0:T(8,128)S(1)}, f32[128,256]{1,0:T(8,128)S(1)}, u32[]{:S(2)}, u32[]{:S(2)}) collective-permute-start(f32[128,256]{1,0:T(8,128)S(1)} %dynamic-slice_add_fusion), channel_id=1, source_target_pairs={{0,8},{4,12},{8,0},{12,4},{16,24},{20,28},{24,16},{28,20},{1,9},{5... | collective-permute-start | bytes 393224 | tf_op jit(solution)/shard_map/ppermute | solution.py:285
  103.7 2.8 %copy-done.1 = f32[1,1,96,128,128]{4,3,2,1,0:T(8,128)S(1)} copy-done((f32[1,1,96,128,128]{4,3,2,1,0:T(8,128)S(1)}, f32[1,1,96,128,128]{4,3,2,1,0:T(8,128)}, u32[]{:S(2)}) %copy-start.1) | copy-done | bytes 6291480
  106.5 15.5 %shard_map.88 = (f32[4096,256]{1,0:T(8,128)S(1)}, s32[97]{0:T(128)S(1)}) custom-call(s32[196]{0:T(256)S(1)} %concatenate.9.ids, f32[96,128,128]{2,1,0:T(8,128)S(1)} %bitcast.10, f32[512,256]{1,0:T(8,128)S(1)} %get-tuple-element.73.refs_0_, f32[512,256]{1,0:T(8,128)S(1)} %collective-permute-done.23.refs_1_), custom_call_target="tpu_custom_call" | custom-call | flops 3221225472 | bytes 11534336 | tf_op jit(solution)/shard_map/pallas_call | solution.py:208
  122.1 5.2 %shard_map.89 = (f32[512,256]{1,0:T(8,128)S(1)}, f32[512,256]{1,0:T(8,128)S(1)}, f32[512,256]{1,0:T(8,128)S(1)}, f32[512,256]{1,0:T(8,128)S(1)}, f32[512,256]{1,...) custom-call(s32[196]{0:T(256)S(1)} %concatenate.9.ids, ...), custom_call_target="tpu_custom_call" | custom-call | flops 3221225472 | bytes 11534336 | tf_op jit(solution)/shard_map/pallas_call | solution.py:208
  128.0 1.3 collective-permute-done.35
  130.3 5.0 %collective-permute-done.30 = f32[128,256]{1,0:T(8,128)S(1)} collective-permute-done((f32[128,256]{1,0:T(8,128)S(1)}, f32[128,256]{1,0:T(8,128)S(1)}, u32[]{:S(2)}, u32[]{:S(2)}) %collective-permute-start.30) | collective-permute-done | bytes 131104 | tf_op jit(solution)/shard_map/ppermute | solution.py:289
  135.2 2.7 %collective-permute-done.39 = f32[256,256]{1,0:T(8,128)S(1)} collective-permute-done((f32[256,256]{1,0:T(8,128)S(1)}, f32[256,256]{1,0:T(8,128)S(1)}, u32[]{:S(2)}, u32[]{:S(2)}) %collective-permute-start.39) | collective-permute-done | bytes 262176 | tf_op jit(solution)/shard_map/ppermute | solution.py:285
  138.4 0.9 pad_add_fusion
  139.3 1.6 %collective-permute-start.40 = (f32[512,256]{1,0:T(8,128)}, f32[512,256]{1,0:T(8,128)S(1)}, u32[]{:S(2)}, u32[]{:S(2)}) collective-permute-start(f32[512,256]{1,0:T(8,128)} %pad_add_fusion), channel_id=1, source_target_pairs={{0,16},{4,20},{8,24},{12,28},{16,0},{20,4},{24,8},{28,12},{1,17},{... | collective-permute-start | bytes 1572872 | tf_op jit(solution)/shard_map/ppermute | solution.py:285
  140.9 3.4 %collective-permute-start.31 = (f32[128,256]{1,0:T(8,128)S(1)}, f32[128,256]{1,0:T(8,128)S(1)}, u32[]{:S(2)}, u32[]{:S(2)}) collective-permute-start(f32[128,256]{1,0:T(8,128)S(1)} %add.72), channel_id=1, source_target_pairs={{0,2},{1,3},{2,0},{3,1},{4,6},{5,7},{6,4},{7,5},{8,10},{9,11},{10,... | collective-permute-start | bytes 393224 | tf_op jit(solution)/shard_map/ppermute | solution.py:289
  144.3 4.7 %collective-permute-done.31 = f32[128,256]{1,0:T(8,128)S(1)} collective-permute-done((f32[128,256]{1,0:T(8,128)S(1)}, f32[128,256]{1,0:T(8,128)S(1)}, u32[]{:S(2)}, u32[]{:S(2)}) %collective-permute-start.31) | collective-permute-done | bytes 131104 | tf_op jit(solution)/shard_map/ppermute | solution.py:289
  149.1 1.3 collective-permute-done.32
  150.4 0.7 fusion
  151.1 1.2 collective-permute-done.40
  152.3 0.9 add_add_fusion
  (62 shorter events, 4.0 us)
Async XLA Ops:
  1.7 11.1 %collective-permute-start.5 = (f32[512,128]{1,0:T(8,128)S(1)}, f32[512,128]{1,0:T(8,128)S(1)}, u32[]{:S(2)}, u32[]{:S(2)}) collective-permute-start(f32[512,128]{1,0:T(8,128)S(1)} %get-tuple-element.45.refs_0_), channel_id=1, source_target_pairs={{0,24},{4,28},{8,16},{12,20},{16,8},{20,12},{24,0},{28,4},{1,25},{... | collective-permute-start | bytes 786440 | tf_op jit(solution)/shard_map/ppermute | solution.py:285
  5.7 11.9 %collective-permute-start.3 = (f32[512,128]{1,0:T(8,128)S(1)}, f32[512,128]{1,0:T(8,128)S(1)}, u32[]{:S(2)}, u32[]{:S(2)}) collective-permute-start(f32[512,128]{1,0:T(8,128)S(1)} %get-tuple-element.45.refs_0_), channel_id=1, source_target_pairs={{0,16},{4,20},{8,24},{12,28},{16,0},{20,4},{24,8},{28,12},{1,17},{... | collective-permute-start | bytes 786440 | tf_op jit(solution)/shard_map/ppermute | solution.py:285
  6.2 11.7 %collective-permute-start.1 = (f32[512,128]{1,0:T(8,128)S(1)}, f32[512,128]{1,0:T(8,128)S(1)}, u32[]{:S(2)}, u32[]{:S(2)}) collective-permute-start(f32[512,128]{1,0:T(8,128)S(1)} %get-tuple-element.45.refs_0_), channel_id=1, source_target_pairs={{0,8},{4,12},{8,0},{12,4},{16,24},{20,28},{24,16},{28,20},{1,9},{5... | collective-permute-start | bytes 786440 | tf_op jit(solution)/shard_map/ppermute | solution.py:285
  7.1 12.9 %collective-permute-start = (f32[512,128]{1,0:T(8,128)S(1)}, f32[512,128]{1,0:T(8,128)S(1)}, u32[]{:S(2)}, u32[]{:S(2)}) collective-permute-start(f32[512,128]{1,0:T(8,128)S(1)} %get-tuple-element.45.refs_0_), channel_id=1, source_target_pairs={{0,4},{4,0},{8,12},{12,8},{16,20},{20,16},{24,28},{28,24},{1,5},{5... | collective-permute-start | bytes 786440 | tf_op jit(solution)/shard_map/ppermute | solution.py:285
  12.8 8.4 %collective-permute-start.6 = (f32[512,128]{1,0:T(8,128)S(1)}, f32[512,128]{1,0:T(8,128)S(1)}, u32[]{:S(2)}, u32[]{:S(2)}) collective-permute-start(f32[512,128]{1,0:T(8,128)S(1)} %collective-permute-done.5.refs_6_), channel_id=1, source_target_pairs={{0,4},{4,0},{8,12},{12,8},{16,20},{20,16},{24,28},{28,24},{1,5},{5... | collective-permute-start | bytes 786440 | tf_op jit(solution)/shard_map/ppermute | solution.py:285
  17.6 4.0 %collective-permute-start.4 = (f32[512,128]{1,0:T(8,128)S(1)}, f32[512,128]{1,0:T(8,128)S(1)}, u32[]{:S(2)}, u32[]{:S(2)}) collective-permute-start(f32[512,128]{1,0:T(8,128)S(1)} %collective-permute-done.3.refs_4_), channel_id=1, source_target_pairs={{0,4},{4,0},{8,12},{12,8},{16,20},{20,16},{24,28},{28,24},{1,5},{5... | collective-permute-start | bytes 786440 | tf_op jit(solution)/shard_map/ppermute | solution.py:285
  17.9 3.7 %collective-permute-start.2 = (f32[512,128]{1,0:T(8,128)S(1)}, f32[512,128]{1,0:T(8,128)S(1)}, u32[]{:S(2)}, u32[]{:S(2)}) collective-permute-start(f32[512,128]{1,0:T(8,128)S(1)} %collective-permute-done.1.refs_2_), channel_id=1, source_target_pairs={{0,4},{4,0},{8,12},{12,8},{16,20},{20,16},{24,28},{28,24},{1,5},{5... | collective-permute-start | bytes 786440 | tf_op jit(solution)/shard_map/ppermute | solution.py:285
  18.1 12.8 %collective-permute-start.16 = (f32[512,128]{1,0:T(8,128)S(1)}, f32[512,128]{1,0:T(8,128)S(1)}, u32[]{:S(2)}, u32[]{:S(2)}) collective-permute-start(f32[512,128]{1,0:T(8,128)S(1)} %get-tuple-element.57.refs_0_), channel_id=1, source_target_pairs={{0,24},{4,28},{8,16},{12,20},{16,8},{20,12},{24,0},{28,4},{1,25},{... | collective-permute-start | bytes 786440 | tf_op jit(solution)/shard_map/ppermute | solution.py:285
  19.9 13.2 %collective-permute-start.14 = (f32[512,128]{1,0:T(8,128)S(1)}, f32[512,128]{1,0:T(8,128)S(1)}, u32[]{:S(2)}, u32[]{:S(2)}) collective-permute-start(f32[512,128]{1,0:T(8,128)S(1)} %get-tuple-element.57.refs_0_), channel_id=1, source_target_pairs={{0,16},{4,20},{8,24},{12,28},{16,0},{20,4},{24,8},{28,12},{1,17},{... | collective-permute-start | bytes 786440 | tf_op jit(solution)/shard_map/ppermute | solution.py:285
  21.2 11.9 %collective-permute-start.12 = (f32[512,128]{1,0:T(8,128)S(1)}, f32[512,128]{1,0:T(8,128)S(1)}, u32[]{:S(2)}, u32[]{:S(2)}) collective-permute-start(f32[512,128]{1,0:T(8,128)S(1)} %get-tuple-element.57.refs_0_), channel_id=1, source_target_pairs={{0,8},{4,12},{8,0},{12,4},{16,24},{20,28},{24,16},{28,20},{1,9},{5... | collective-permute-start | bytes 786440 | tf_op jit(solution)/shard_map/ppermute | solution.py:285
  21.6 2.8 %copy-start = (f32[1,1,96,128,128]{4,3,2,1,0:T(8,128)S(1)}, f32[1,1,96,128,128]{4,3,2,1,0:T(8,128)}, u32[]{:S(2)}) copy-start(f32[1,1,96,128,128]{4,3,2,1,0:T(8,128)} %param.11) | copy-start | bytes 18874372
  28.3 46.9 %copy-start.2 = (f32[512,256]{1,0:T(8,128)S(1)}, f32[512,256]{1,0:T(8,128)}, u32[]{:S(2)}) copy-start(f32[512,256]{1,0:T(8,128)} %refs_10_.1) | copy-start | bytes 1572868
  28.3 46.9 %copy-start.3 = (f32[256,256]{1,0:T(8,128)S(1)}, f32[256,256]{1,0:T(8,128)}, u32[]{:S(2)}) copy-start(f32[256,256]{1,0:T(8,128)} %refs_11_.1) | copy-start | bytes 786436
  28.3 7.7 %collective-permute-start.7 = (f32[512,128]{1,0:T(8,128)S(1)}, f32[512,128]{1,0:T(8,128)S(1)}, u32[]{:S(2)}, u32[]{:S(2)}) collective-permute-start(f32[512,128]{1,0:T(8,128)S(1)} %get-tuple-element.50), channel_id=1, source_target_pairs={{0,1},{1,0},{2,3},{3,2},{4,5},{5,4},{6,7},{7,6},{8,9},{9,8},{10,11... | collective-permute-start | bytes 786440 | tf_op jit(solution)/shard_map/ppermute | solution.py:289
  30.2 5.9 %collective-permute-start.8 = (f32[512,128]{1,0:T(8,128)S(1)}, f32[512,128]{1,0:T(8,128)S(1)}, u32[]{:S(2)}, u32[]{:S(2)}) collective-permute-start(f32[512,128]{1,0:T(8,128)S(1)} %get-tuple-element.54), channel_id=1, source_target_pairs={{1,2},{2,1},{5,6},{6,5},{9,10},{10,9},{13,14},{14,13},{17,18},{18,... | collective-permute-start | bytes 786440 | tf_op jit(solution)/shard_map/ppermute | solution.py:289
  30.9 11.1 %collective-permute-start.11 = (f32[512,128]{1,0:T(8,128)S(1)}, f32[512,128]{1,0:T(8,128)S(1)}, u32[]{:S(2)}, u32[]{:S(2)}) collective-permute-start(f32[512,128]{1,0:T(8,128)S(1)} %get-tuple-element.57.refs_0_), channel_id=1, source_target_pairs={{0,4},{4,0},{8,12},{12,8},{16,20},{20,16},{24,28},{28,24},{1,5},{5... | collective-permute-start | bytes 786440 | tf_op jit(solution)/shard_map/ppermute | solution.py:285
  33.1 10.1 %collective-permute-start.13 = (f32[512,128]{1,0:T(8,128)S(1)}, f32[512,128]{1,0:T(8,128)S(1)}, u32[]{:S(2)}, u32[]{:S(2)}) collective-permute-start(f32[512,128]{1,0:T(8,128)S(1)} %collective-permute-done.12.refs_2_), channel_id=1, source_target_pairs={{0,4},{4,0},{8,12},{12,8},{16,20},{20,16},{24,28},{28,24},{1,5},{5... | collective-permute-start | bytes 786440 | tf_op jit(solution)/shard_map/ppermute | solution.py:285
  33.1 10.1 %collective-permute-start.15 = (f32[512,128]{1,0:T(8,128)S(1)}, f32[512,128]{1,0:T(8,128)S(1)}, u32[]{:S(2)}, u32[]{:S(2)}) collective-permute-start(f32[512,128]{1,0:T(8,128)S(1)} %collective-permute-done.14.refs_4_), channel_id=1, source_target_pairs={{0,4},{4,0},{8,12},{12,8},{16,20},{20,16},{24,28},{28,24},{1,5},{5... | collective-permute-start | bytes 786440 | tf_op jit(solution)/shard_map/ppermute | solution.py:285
  36.1 7.2 %collective-permute-start.17 = (f32[512,128]{1,0:T(8,128)S(1)}, f32[512,128]{1,0:T(8,128)S(1)}, u32[]{:S(2)}, u32[]{:S(2)}) collective-permute-start(f32[512,128]{1,0:T(8,128)S(1)} %collective-permute-done.16.refs_6_), channel_id=1, source_target_pairs={{0,4},{4,0},{8,12},{12,8},{16,20},{20,16},{24,28},{28,24},{1,5},{5... | collective-permute-start | bytes 786440 | tf_op jit(solution)/shard_map/ppermute | solution.py:285
  36.1 16.0 %collective-permute-start.9 = (f32[512,128]{1,0:T(8,128)S(1)}, f32[512,128]{1,0:T(8,128)S(1)}, u32[]{:S(2)}, u32[]{:S(2)}) collective-permute-start(f32[512,128]{1,0:T(8,128)S(1)} %select_add_fusion.1), channel_id=1, source_target_pairs={{0,2},{1,3},{2,0},{3,1},{4,6},{5,7},{6,4},{7,5},{8,10},{9,11},{10,... | collective-permute-start | bytes 786440 | tf_op jit(solution)/shard_map/ppermute | solution.py:289
  41.9 10.1 %collective-permute-start.10 = (f32[512,128]{1,0:T(8,128)S(1)}, f32[512,128]{1,0:T(8,128)S(1)}, u32[]{:S(2)}, u32[]{:S(2)}) collective-permute-start(f32[512,128]{1,0:T(8,128)S(1)} %get-tuple-element.54), channel_id=1, source_target_pairs={{0,1},{3,2},{4,5},{7,6},{8,9},{11,10},{12,13},{15,14},{16,17},{19,... | collective-permute-start | bytes 786440 | tf_op jit(solution)/shard_map/ppermute | solution.py:289
  52.1 7.0 %collective-permute-start.18 = (f32[512,128]{1,0:T(8,128)S(1)}, f32[512,128]{1,0:T(8,128)S(1)}, u32[]{:S(2)}, u32[]{:S(2)}) collective-permute-start(f32[512,128]{1,0:T(8,128)S(1)} %get-tuple-element.63), channel_id=1, source_target_pairs={{0,1},{1,0},{2,3},{3,2},{4,5},{5,4},{6,7},{7,6},{8,9},{9,8},{10,11... | collective-permute-start | bytes 786440 | tf_op jit(solution)/shard_map/ppermute | solution.py:289
  53.9 5.2 %collective-permute-start.19 = (f32[512,128]{1,0:T(8,128)S(1)}, f32[512,128]{1,0:T(8,128)S(1)}, u32[]{:S(2)}, u32[]{:S(2)}) collective-permute-start(f32[512,128]{1,0:T(8,128)S(1)} %get-tuple-element.68), channel_id=1, source_target_pairs={{1,2},{2,1},{5,6},{6,5},{9,10},{10,9},{13,14},{14,13},{17,18},{18,... | collective-permute-start | bytes 786440 | tf_op jit(solution)/shard_map/ppermute | solution.py:289
  59.1 16.1 %collective-permute-start.20 = (f32[512,128]{1,0:T(8,128)S(1)}, f32[512,128]{1,0:T(8,128)S(1)}, u32[]{:S(2)}, u32[]{:S(2)}) collective-permute-start(f32[512,128]{1,0:T(8,128)S(1)} %select_add_fusion), channel_id=1, source_target_pairs={{0,2},{1,3},{2,0},{3,1},{4,6},{5,7},{6,4},{7,5},{8,10},{9,11},{10,... | collective-permute-start | bytes 786440 | tf_op jit(solution)/shard_map/ppermute | solution.py:289
  65.1 10.1 %collective-permute-start.21 = (f32[512,128]{1,0:T(8,128)S(1)}, f32[512,128]{1,0:T(8,128)S(1)}, u32[]{:S(2)}, u32[]{:S(2)}) collective-permute-start(f32[512,128]{1,0:T(8,128)S(1)} %get-tuple-element.68), channel_id=1, source_target_pairs={{0,1},{3,2},{4,5},{7,6},{8,9},{11,10},{12,13},{15,14},{16,17},{19,... | collective-permute-start | bytes 786440 | tf_op jit(solution)/shard_map/ppermute | solution.py:289
  77.1 12.6 %collective-permute-start.23 = (f32[512,256]{1,0:T(8,128)S(1)}, f32[512,256]{1,0:T(8,128)S(1)}, u32[]{:S(2)}, u32[]{:S(2)}) collective-permute-start(f32[512,256]{1,0:T(8,128)S(1)} %get-tuple-element.73.refs_0_), channel_id=1, source_target_pairs={{0,2},{3,1},{1,0},{2,3},{4,6},{7,5},{5,4},{6,7},{8,10},{11,9},{9,8... | collective-permute-start | bytes 1572872 | tf_op jit(solution)/shard_map/ppermute | solution.py:289
  78.9 16.2 %collective-permute-start.22 = (f32[128,256]{1,0:T(8,128)S(1)}, f32[128,256]{1,0:T(8,128)S(1)}, u32[]{:S(2)}, u32[]{:S(2)}) collective-permute-start(f32[128,256]{1,0:T(8,128)S(1)} %constant_dynamic-slice_fusion), channel_id=1, source_target_pairs={{0,4},{4,0},{8,12},{12,8},{16,20},{20,16},{24,28},{28,24},{1,5},{5... | collective-permute-start | bytes 393224 | tf_op jit(solution)/shard_map/ppermute | solution.py:285
  89.7 32.3 %collective-permute-start.28 = (f32[512,256]{1,0:T(8,128)S(1)}, f32[512,256]{1,0:T(8,128)S(1)}, u32[]{:S(2)}, u32[]{:S(2)}) collective-permute-start(f32[512,256]{1,0:T(8,128)S(1)} %get-tuple-element.73.refs_0_), channel_id=1, source_target_pairs={{1,2},{2,1},{5,6},{6,5},{9,10},{10,9},{13,14},{14,13},{17,18},{18,... | collective-permute-start | bytes 1572872 | tf_op jit(solution)/shard_map/ppermute | solution.py:289
  90.4 31.6 %collective-permute-start.27 = (f32[512,256]{1,0:T(8,128)S(1)}, f32[512,256]{1,0:T(8,128)S(1)}, u32[]{:S(2)}, u32[]{:S(2)}) collective-permute-start(f32[512,256]{1,0:T(8,128)S(1)} %get-tuple-element.73.refs_0_), channel_id=1, source_target_pairs={{2,0},{1,3},{0,1},{3,2},{6,4},{5,7},{4,5},{7,6},{10,8},{9,11},{8,9... | collective-permute-start | bytes 1572872 | tf_op jit(solution)/shard_map/ppermute | solution.py:289
  93.8 28.2 %collective-permute-start.29 = (f32[512,256]{1,0:T(8,128)S(1)}, f32[512,256]{1,0:T(8,128)S(1)}, u32[]{:S(2)}, u32[]{:S(2)}) collective-permute-start(f32[512,256]{1,0:T(8,128)S(1)} %collective-permute-done.23.refs_1_), channel_id=1, source_target_pairs={{1,0},{2,3},{5,4},{6,7},{9,8},{10,11},{13,12},{14,15},{17,16},{18,... | collective-permute-start | bytes 1572872 | tf_op jit(solution)/shard_map/ppermute | solution.py:289
  95.1 7.0 %collective-permute-start.26 = (f32[128,256]{1,0:T(8,128)S(1)}, f32[128,256]{1,0:T(8,128)S(1)}, u32[]{:S(2)}, u32[]{:S(2)}) collective-permute-start(f32[128,256]{1,0:T(8,128)S(1)} %dynamic-slice_add_fusion), channel_id=1, source_target_pairs={{0,24},{4,28},{8,16},{12,20},{16,8},{20,12},{24,0},{28,4},{1,25},{... | collective-permute-start | bytes 393224 | tf_op jit(solution)/shard_map/ppermute | solution.py:285
  97.1 24.9 %collective-permute-start.25 = (f32[128,256]{1,0:T(8,128)S(1)}, f32[128,256]{1,0:T(8,128)S(1)}, u32[]{:S(2)}, u32[]{:S(2)}) collective-permute-start(f32[128,256]{1,0:T(8,128)S(1)} %dynamic-slice_add_fusion), channel_id=1, source_target_pairs={{0,16},{4,20},{8,24},{12,28},{16,0},{20,4},{24,8},{28,12},{1,17},{... | collective-permute-start | bytes 393224 | tf_op jit(solution)/shard_map/ppermute | solution.py:285
  102.2 19.9 %collective-permute-start.24 = (f32[128,256]{1,0:T(8,128)S(1)}, f32[128,256]{1,0:T(8,128)S(1)}, u32[]{:S(2)}, u32[]{:S(2)}) collective-permute-start(f32[128,256]{1,0:T(8,128)S(1)} %dynamic-slice_add_fusion), channel_id=1, source_target_pairs={{0,8},{4,12},{8,0},{12,4},{16,24},{20,28},{24,16},{28,20},{1,9},{5... | collective-permute-start | bytes 393224 | tf_op jit(solution)/shard_map/ppermute | solution.py:285
  103.7 2.8 %copy-start.1 = (f32[1,1,96,128,128]{4,3,2,1,0:T(8,128)S(1)}, f32[1,1,96,128,128]{4,3,2,1,0:T(8,128)}, u32[]{:S(2)}) copy-start(f32[1,1,96,128,128]{4,3,2,1,0:T(8,128)} %param.11) | copy-start | bytes 18874372
  127.3 2.0 %collective-permute-start.35 = (f32[512,256]{1,0:T(8,128)S(1)}, f32[512,256]{1,0:T(8,128)S(1)}, u32[]{:S(2)}, u32[]{:S(2)}) collective-permute-start(f32[512,256]{1,0:T(8,128)S(1)} %get-tuple-element.83), channel_id=1, source_target_pairs={{0,4},{4,0},{8,12},{12,8},{16,20},{20,16},{24,28},{28,24},{1,5},{5... | collective-permute-start | bytes 1572872 | tf_op jit(solution)/shard_map/ppermute | solution.py:285
  127.4 10.5 %collective-permute-start.34 = (f32[512,256]{1,0:T(8,128)S(1)}, f32[512,256]{1,0:T(8,128)S(1)}, u32[]{:S(2)}, u32[]{:S(2)}) collective-permute-start(f32[512,256]{1,0:T(8,128)S(1)} %get-tuple-element.81), channel_id=1, source_target_pairs={{0,4},{4,0},{8,12},{12,8},{16,20},{20,16},{24,28},{28,24},{1,5},{5... | collective-permute-start | bytes 1572872 | tf_op jit(solution)/shard_map/ppermute | solution.py:285
  127.9 10.5 %collective-permute-start.38 = (f32[512,256]{1,0:T(8,128)S(1)}, f32[512,256]{1,0:T(8,128)S(1)}, u32[]{:S(2)}, u32[]{:S(2)}) collective-permute-start(f32[512,256]{1,0:T(8,128)S(1)} %get-tuple-element.85), channel_id=1, source_target_pairs={{0,4},{4,0},{8,12},{12,8},{16,20},{20,16},{24,28},{28,24},{1,5},{5... | collective-permute-start | bytes 1572872 | tf_op jit(solution)/shard_map/ppermute | solution.py:285
  129.4 8.5 %collective-permute-start.36 = (f32[256,256]{1,0:T(8,128)S(1)}, f32[256,256]{1,0:T(8,128)S(1)}, u32[]{:S(2)}, u32[]{:S(2)}) collective-permute-start(f32[256,256]{1,0:T(8,128)S(1)} %get-tuple-element.87), channel_id=1, source_target_pairs={{0,16},{4,20},{8,24},{12,28},{16,0},{20,4},{24,8},{28,12},{1,17},{... | collective-permute-start | bytes 786440 | tf_op jit(solution)/shard_map/ppermute | solution.py:285
  129.7 8.2 %collective-permute-start.39 = (f32[256,256]{1,0:T(8,128)S(1)}, f32[256,256]{1,0:T(8,128)S(1)}, u32[]{:S(2)}, u32[]{:S(2)}) collective-permute-start(f32[256,256]{1,0:T(8,128)S(1)} %get-tuple-element.88), channel_id=1, source_target_pairs={{0,8},{4,12},{8,0},{12,4},{16,24},{20,28},{24,16},{28,20},{1,9},{5... | collective-permute-start | bytes 786440 | tf_op jit(solution)/shard_map/ppermute | solution.py:285
  130.2 5.0 %collective-permute-start.30 = (f32[128,256]{1,0:T(8,128)S(1)}, f32[128,256]{1,0:T(8,128)S(1)}, u32[]{:S(2)}, u32[]{:S(2)}) collective-permute-start(f32[128,256]{1,0:T(8,128)S(1)} %add_add_fusion.1), channel_id=1, source_target_pairs={{0,1},{1,0},{2,3},{3,2},{4,5},{5,4},{6,7},{7,6},{8,9},{9,8},{10,11... | collective-permute-start | bytes 393224 | tf_op jit(solution)/shard_map/ppermute | solution.py:289
  135.2 15.9 %collective-permute-start.33 = (f32[512,256]{1,0:T(8,128)S(1)}, f32[512,256]{1,0:T(8,128)S(1)}, u32[]{:S(2)}, u32[]{:S(2)}) collective-permute-start(f32[512,256]{1,0:T(8,128)S(1)} %get-tuple-element.79), channel_id=1, source_target_pairs={{0,4},{4,0},{8,12},{12,8},{16,20},{20,16},{24,28},{28,24},{1,5},{5... | collective-permute-start | bytes 1572872 | tf_op jit(solution)/shard_map/ppermute | solution.py:285
  138.0 13.1 %collective-permute-start.37 = (f32[512,256]{1,0:T(8,128)S(1)}, f32[512,256]{1,0:T(8,128)S(1)}, u32[]{:S(2)}, u32[]{:S(2)}) collective-permute-start(f32[512,256]{1,0:T(8,128)S(1)} %pad_add_fusion.1), channel_id=1, source_target_pairs={{0,8},{4,12},{8,0},{12,4},{16,24},{20,28},{24,16},{28,20},{1,9},{5... | collective-permute-start | bytes 1572872 | tf_op jit(solution)/shard_map/ppermute | solution.py:285
  139.3 13.0 %collective-permute-start.40 = (f32[512,256]{1,0:T(8,128)}, f32[512,256]{1,0:T(8,128)S(1)}, u32[]{:S(2)}, u32[]{:S(2)}) collective-permute-start(f32[512,256]{1,0:T(8,128)} %pad_add_fusion), channel_id=1, source_target_pairs={{0,16},{4,20},{8,24},{12,28},{16,0},{20,4},{24,8},{28,12},{1,17},{... | collective-permute-start | bytes 1572872 | tf_op jit(solution)/shard_map/ppermute | solution.py:285
  140.9 8.1 %collective-permute-start.31 = (f32[128,256]{1,0:T(8,128)S(1)}, f32[128,256]{1,0:T(8,128)S(1)}, u32[]{:S(2)}, u32[]{:S(2)}) collective-permute-start(f32[128,256]{1,0:T(8,128)S(1)} %add.72), channel_id=1, source_target_pairs={{0,2},{1,3},{2,0},{3,1},{4,6},{5,7},{6,4},{7,5},{8,10},{9,11},{10,... | collective-permute-start | bytes 393224 | tf_op jit(solution)/shard_map/ppermute | solution.py:289
  149.0 1.4 collective-permute-start.32

commit v5 on v4

--- a/solution.py
+++ b/solution.py
@@ -58,10 +58,9 @@
 def spmm_kernel(groups, only, has_base, count_out, steps, unroll, per, transposed, ids, values_hbm, *refs):
     count_in = sum(groups)
     pieces, refs = refs[:count_in], refs[count_in:]
-    (base, listed), refs = (refs[:2], refs[2:]) if has_base else ((None, None), refs)
+    listed, refs = (refs[0], refs[1:]) if only is not None else (None, refs)
+    base, refs = (refs[0], refs[1:]) if has_base else (None, refs)
     outs, refs = refs[:count_out], refs[count_out:]
-    if only is not None and not has_base:
-        listed, refs = refs[0], refs[1:]
     landed, source, total, values, value_sem, piece_sem, base_sem, out_sem = refs
     count, size = values.shape[0], values.shape[-1]
     halves = source.shape[1]
@@ -98,16 +97,6 @@
     if only is not None:
         source[zero_slot] = jnp.zeros_like(source[zero_slot])
 
-        if not has_base:
-
-            def pick(index, found):
-                take, _ = slots_of(index)
-                wanted = (take >= only[0]) & (take < only[1])
-                listed[jnp.where(wanted, found, count - 1 - index + found)] = index
-                return found + wanted.astype(jnp.int32)
-
-            listed[count] = lax.fori_loop(0, count, pick, 0)
-
         found = count - listed[count] if has_base else listed[count]
 
         def picked(place):
@@ -189,7 +178,29 @@
         copy.wait()
 
 
-def spmm(ids, values, groups, out_rows, per, transposed, only=None, rest=()):
+def list_kernel(slots, per, ids, listed):
+    count = listed.shape[0] - 1
+
+    def add(index, found):
+        wanted = row_slot(ids[4 + index], ids, per, True) < slots
+        listed[jnp.where(wanted, found, count - 1 - index + found)] = index
+        return found + wanted.astype(jnp.int32)
+
+    listed[count] = lax.fori_loop(0, count, add, 0)
+
+
+def list_blocks(ids, count, slots, per):
+    smem = pl.BlockSpec(memory_space=pltpu.SMEM)
+    return pl.pallas_call(
+        functools.partial(list_kernel, slots, per),
+        out_shape=jax.ShapeDtypeStruct((count + 1,), jnp.int32),
+        in_specs=[smem],
+        out_specs=smem,
+        compiler_params=pltpu.CompilerParams(vmem_limit_bytes=MIB),
+    )(ids)
+
+
+def spmm(ids, values, groups, out_rows, per, transposed, only=None, listed=None, base=None):
     pieces = [piece for group in groups for piece in group]
     count, size = values.shape[0], values.shape[-1]
     width = pieces[0].shape[1]
@@ -198,7 +209,7 @@
     steps = count // unroll if only is None else 1
     in_rows = sum(group[0].shape[0] for group in groups)
     smem, anywhere = pl.BlockSpec(memory_space=pltpu.SMEM), pl.BlockSpec(memory_space=pl.ANY)
-    lists = only is not None and not rest
+    more = [(smem, listed)] * (only is not None) + [(anywhere, base)] * (base is not None)
     buffers = [
         pltpu.VMEM((sum(piece.shape[0] for piece in pieces), width), jnp.float32),
         pltpu.VMEM((in_rows // size + 1, halves, 2 * size, 2 * (width // halves)), jnp.bfloat16),
@@ -210,17 +221,16 @@
             spmm_kernel,
             [len(group) for group in groups],
             only,
-            bool(rest),
+            base is not None,
             len(out_rows),
             steps,
             unroll,
             per,
             transposed,
         ),
-        out_shape=[jax.ShapeDtypeStruct((rows, width), jnp.float32) for rows in out_rows]
-        + [jax.ShapeDtypeStruct((count + 1,), jnp.int32)] * lists,
-        in_specs=[smem] + [anywhere] * (1 + len(pieces)) + [anywhere, smem][: len(rest)],
-        out_specs=[anywhere] * len(out_rows) + [smem] * lists,
+        out_shape=[jax.ShapeDtypeStruct((rows, width), jnp.float32) for rows in out_rows],
+        in_specs=[smem] + [anywhere] * (1 + len(pieces)) + [space for space, _ in more],
+        out_specs=[anywhere] * len(out_rows),
         scratch_shapes=buffers
         + [
             pltpu.SemaphoreType.DMA((steps if only is None else count,)),
@@ -238,7 +248,7 @@
             bytes_accessed=4 * (values.size + (in_rows + sum(out_rows)) * width),
             transcendentals=0,
         ),
-    )(ids, values, *pieces, *rest)
+    )(ids, values, *pieces, *(operand for _, operand in more))
 
 
 def dense_kernel(count_parts, ids, *refs):
@@ -354,15 +364,16 @@
         hidden, back, grad = dense(ids, terms, cotangent, weight_matrix)
 
         ends_across = along_col(back, ENDS_ACROSS)
-        later = after(back, ends_across)
+        listed = list_blocks(after(ids, back), values.shape[0], 2 * per, per)
+        later = after(back, ends_across, listed)
         ends_inward, middle = along_col(later, ENDS_INWARD), along_col(later, MIDDLE)
         outward = along_col(ends_across, OUTWARD)
-        rest = spmm(ids, values, [[back], [ends_across]], [rows_dev * count_row], per, True, (0, 2 * per))
+        rest = spmm(ids, values, [[back], [ends_across]], [rows_dev * count_row], per, True, (0, 2 * per), listed)[0]
         grad = core_half(grad)
         grads = [along_row(after(grad, ends_across), bit) for bit in (2, 4, 6)]
         groups = [[after(ends_inward, *grads)], [middle, outward]]
         sums = plane_exchange(
-            spmm(ids, values, groups, [rows_dev] * 8, per, True, (2 * per, 4 * per), rest)
+            spmm(ids, values, groups, [rows_dev] * 8, per, True, (2 * per, 4 * per), listed, rest)
         )
         grad = after(grad + grads[0] + grads[1] + grads[2], ends_inward, middle, outward)
         grad = grad + along_col(grad, OUTER)

time: 154 us -> 152 us (0.987)
  Pallas kernels: 30.5 us -> 28.4 us
    pallas_call x4, Pallas kernels: 28.6 us -> 23.6 us  [spmm(): pl.pallas_call(functools.partial(spmm_kernel, [len(group) for group in gr...]
    pallas_call x0 -> x1, Pallas kernels: none -> 2.86 us  [list_blocks(): pl.pallas_call(functools.partial(list_kernel, slots, per), out_shape=jax....]
    ppermute x27, starting transfers between devices: 17.1 us -> 19.2 us  [along_row(): lax.ppermute(x, 'row', [(i, i ^ bit) for i in range(lax.axis_size('row'))])]
    ppermute x14, starting transfers between devices: 30 us -> 27.9 us  [along_col(): return lax.ppermute(x, 'col', pairs)]
  transfers between devices with their start and end apart: 41 -> 41, of which waited for: 16 -> 17; matrix products, arithmetic and copies ran while one was open for 2% -> 2% of each run, Pallas kernels for 15% -> 13%
where the time goes in v5:
time: 152 us
  waiting for transfers between devices  65.1 us (43%)
  starting transfers between devices  47.2 us (31%)
  Pallas kernels  28.4 us (19%)
  local copies, waits for them, and re-layouts  7.44 us (5%)
  other arithmetic  2.85 us (2%)
    ppermute x14, waiting for transfers between devices, along_col(): return lax.ppermute(x, 'col', pairs)  41.5 us
    ppermute x14, starting transfers between devices, along_col(): return lax.ppermute(x, 'col', pairs)  27.9 us
    ppermute x27, waiting for transfers between devices, along_row(): lax.ppermute(x, 'row', [(i, i ^ bit) for i in range(lax.axis_size('row'))])  23.6 us
    pallas_call x4, Pallas kernels, spmm(): pl.pallas_call(functools.partial(spmm_kernel, [len(group) for group in gr...  23.6 us
    ppermute x27, starting transfers between devices, along_row(): lax.ppermute(x, 'row', [(i, i ^ bit) for i in range(lax.axis_size('row'))])  19.2 us
    unnamed x8, local copies, waits for them, and re-layouts  5.58 us
  transfers between devices with their start and end apart: 41, of which 17 were waited for; matrix products, arithmetic and copies ran while one was open for 2% of the time, Pallas kernels for 13%

profile of v5, /device:TPU:0, one launch (start us, length us, event | category | flops | bytes accessed | tf_op | source)
XLA Modules:
  0.0 151.8 jit_solution(17779151352991058077)
XLA Ops:
  0.6 1.1 fusion.2
  1.7 4.0 %collective-permute-start.5 = (f32[512,128]{1,0:T(8,128)S(1)}, f32[512,128]{1,0:T(8,128)S(1)}, u32[]{:S(2)}, u32[]{:S(2)}) collective-permute-start(f32[512,128]{1,0:T(8,128)S(1)} %get-tuple-element.44.refs_0_), channel_id=1, source_target_pairs={{0,24},{4,28},{8,16},{12,20},{16,8},{20,12},{24,0},{28,4},{1,25},{... | collective-permute-start | bytes 786440 | tf_op jit(solution)/shard_map/ppermute | solution.py:295
  6.3 0.7 concatenate.9.ids
  7.1 5.8 %collective-permute-done.5.refs_6_ = f32[512,128]{1,0:T(8,128)S(1)} collective-permute-done((f32[512,128]{1,0:T(8,128)S(1)}, f32[512,128]{1,0:T(8,128)S(1)}, u32[]{:S(2)}, u32[]{:S(2)}) %collective-permute-start.5) | collective-permute-done | bytes 262176 | tf_op jit(solution)/shard_map/ppermute | solution.py:295
  12.8 4.7 %collective-permute-done.3.refs_4_ = f32[512,128]{1,0:T(8,128)S(1)} collective-permute-done((f32[512,128]{1,0:T(8,128)S(1)}, f32[512,128]{1,0:T(8,128)S(1)}, u32[]{:S(2)}, u32[]{:S(2)}) %collective-permute-start.3) | collective-permute-done | bytes 262176 | tf_op jit(solution)/shard_map/ppermute | solution.py:295
  18.1 1.8 %collective-permute-start.16 = (f32[512,128]{1,0:T(8,128)S(1)}, f32[512,128]{1,0:T(8,128)S(1)}, u32[]{:S(2)}, u32[]{:S(2)}) collective-permute-start(f32[512,128]{1,0:T(8,128)S(1)} %get-tuple-element.56.refs_0_), channel_id=1, source_target_pairs={{0,24},{4,28},{8,16},{12,20},{16,8},{20,12},{24,0},{28,4},{1,25},{... | collective-permute-start | bytes 786440 | tf_op jit(solution)/shard_map/ppermute | solution.py:295
  19.9 1.3 collective-permute-start.14
  21.6 2.8 %copy-done = f32[1,1,96,128,128]{4,3,2,1,0:T(8,128)S(1)} copy-done((f32[1,1,96,128,128]{4,3,2,1,0:T(8,128)S(1)}, f32[1,1,96,128,128]{4,3,2,1,0:T(8,128)}, u32[]{:S(2)}) %copy-start) | copy-done | bytes 6291480
  24.4 3.9 %shard_map.85 = (f32[512,128]{1,0:T(8,128)S(1)}, f32[512,128]{1,0:T(8,128)S(1)}, f32[512,128]{1,0:T(8,128)S(1)}, f32[512,128]{1,0:T(8,128)S(1)}) custom-call(s32[196]{0:T(256)S(1)} %concatenate.9.ids, f32[96,128,128]{2,1,0:T(8,128)S(1)} %bitcast.8, f32[512,128]{1,0:T(8,128)S(1)} %get-tuple-element.44.refs_0_, f32[512,128]{1,0:T(8,128)S(1)} %collective-permute-done.refs_1_, ...), custom_call_target="tpu_custom_call" | custom-call | flops 1610612736 | bytes 9437184 | tf_op jit(solution)/shard_map/pallas_call | solution.py:219
  28.3 1.8 %collective-permute-start.7 = (f32[512,128]{1,0:T(8,128)S(1)}, f32[512,128]{1,0:T(8,128)S(1)}, u32[]{:S(2)}, u32[]{:S(2)}) collective-permute-start(f32[512,128]{1,0:T(8,128)S(1)} %get-tuple-element.49), channel_id=1, source_target_pairs={{0,1},{1,0},{2,3},{3,2},{4,5},{5,4},{6,7},{7,6},{8,9},{9,8},{10,11... | collective-permute-start | bytes 786440 | tf_op jit(solution)/shard_map/ppermute | solution.py:299
  30.9 2.2 %collective-permute-done.14.refs_4_ = f32[512,128]{1,0:T(8,128)S(1)} collective-permute-done((f32[512,128]{1,0:T(8,128)S(1)}, f32[512,128]{1,0:T(8,128)S(1)}, u32[]{:S(2)}, u32[]{:S(2)}) %collective-permute-start.14) | collective-permute-done | bytes 262176 | tf_op jit(solution)/shard_map/ppermute | solution.py:295
  33.6 2.4 %collective-permute-done.7.refs_1_ = f32[512,128]{1,0:T(8,128)S(1)} collective-permute-done((f32[512,128]{1,0:T(8,128)S(1)}, f32[512,128]{1,0:T(8,128)S(1)}, u32[]{:S(2)}, u32[]{:S(2)}) %collective-permute-start.7) | collective-permute-done | bytes 262176 | tf_op jit(solution)/shard_map/ppermute | solution.py:299
  36.1 5.8 %collective-permute-start.9 = (f32[512,128]{1,0:T(8,128)S(1)}, f32[512,128]{1,0:T(8,128)S(1)}, u32[]{:S(2)}, u32[]{:S(2)}) collective-permute-start(f32[512,128]{1,0:T(8,128)S(1)} %select_add_fusion.1), channel_id=1, source_target_pairs={{0,2},{1,3},{2,0},{3,1},{4,6},{5,7},{6,4},{7,5},{8,10},{9,11},{10,... | collective-permute-start | bytes 786440 | tf_op jit(solution)/shard_map/ppermute | solution.py:299
  41.9 1.3 collective-permute-start.10
  43.3 3.9 %shard_map.86 = (f32[512,128]{1,0:T(8,128)S(1)}, f32[512,128]{1,0:T(8,128)S(1)}, f32[512,128]{1,0:T(8,128)S(1)}, f32[512,128]{1,0:T(8,128)S(1)}) custom-call(s32[196]{0:T(256)S(1)} %concatenate.9.ids, f32[96,128,128]{2,1,0:T(8,128)S(1)} %bitcast.9, f32[512,128]{1,0:T(8,128)S(1)} %get-tuple-element.56.refs_0_, ...), custom_call_target="tpu_custom_call" | custom-call | flops 1610612736 | bytes 9437184 | tf_op jit(solution)/shard_map/pallas_call | solution.py:219
  47.2 4.9 %collective-permute-done.9.refs_3_ = f32[512,128]{1,0:T(8,128)S(1)} collective-permute-done((f32[512,128]{1,0:T(8,128)S(1)}, f32[512,128]{1,0:T(8,128)S(1)}, u32[]{:S(2)}, u32[]{:S(2)}) %collective-permute-start.9) | collective-permute-done | bytes 262176 | tf_op jit(solution)/shard_map/ppermute | solution.py:299
  52.1 1.8 %collective-permute-start.18 = (f32[512,128]{1,0:T(8,128)S(1)}, f32[512,128]{1,0:T(8,128)S(1)}, u32[]{:S(2)}, u32[]{:S(2)}) collective-permute-start(f32[512,128]{1,0:T(8,128)S(1)} %get-tuple-element.62), channel_id=1, source_target_pairs={{0,1},{1,0},{2,3},{3,2},{4,5},{5,4},{6,7},{7,6},{8,9},{9,8},{10,11... | collective-permute-start | bytes 786440 | tf_op jit(solution)/shard_map/ppermute | solution.py:299
  54.5 4.5 %collective-permute-done.18.refs_6_ = f32[512,128]{1,0:T(8,128)S(1)} collective-permute-done((f32[512,128]{1,0:T(8,128)S(1)}, f32[512,128]{1,0:T(8,128)S(1)}, u32[]{:S(2)}, u32[]{:S(2)}) %collective-permute-start.18) | collective-permute-done | bytes 262176 | tf_op jit(solution)/shard_map/ppermute | solution.py:299
  59.1 6.0 %collective-permute-start.20 = (f32[512,128]{1,0:T(8,128)S(1)}, f32[512,128]{1,0:T(8,128)S(1)}, u32[]{:S(2)}, u32[]{:S(2)}) collective-permute-start(f32[512,128]{1,0:T(8,128)S(1)} %select_add_fusion), channel_id=1, source_target_pairs={{0,2},{1,3},{2,0},{3,1},{4,6},{5,7},{6,4},{7,5},{8,10},{9,11},{10,... | collective-permute-start | bytes 786440 | tf_op jit(solution)/shard_map/ppermute | solution.py:299
  65.1 1.3 collective-permute-start.21
  66.4 8.8 %collective-permute-done.20.refs_8_ = f32[512,128]{1,0:T(8,128)S(1)} collective-permute-done((f32[512,128]{1,0:T(8,128)S(1)}, f32[512,128]{1,0:T(8,128)S(1)}, u32[]{:S(2)}, u32[]{:S(2)}) %collective-permute-start.20) | collective-permute-done | bytes 262176 | tf_op jit(solution)/shard_map/ppermute | solution.py:299
  75.2 1.9 %shard_map.87 = (f32[512,256]{1,0:T(8,128)}, f32[512,256]{1,0:T(8,128)S(1)}, f32[256,256]{1,0:T(8,128)S(1)}) custom-call(s32[196]{0:T(256)S(1)} %concatenate.9.ids, f32[512,128]{1,0:T(8,128)S(1)} %get-tuple-element.48.refs_0_, f32[512,128]{1,0:T(8,128)S(1)} %collective-permute-done.7.refs_1_, f32[512,128]{1,0:T(8,128)S(1)} %collective-permute-done.8.refs_2_, ...), custom_call_target="tpu_custom_call" | custom-call | flops 1000 | bytes 1000 | tf_op jit(solution)/shard_map/pallas_call | solution.py:277
  77.1 1.8 %collective-permute-start.23 = (f32[512,256]{1,0:T(8,128)S(1)}, f32[512,256]{1,0:T(8,128)S(1)}, u32[]{:S(2)}, u32[]{:S(2)}) collective-permute-start(f32[512,256]{1,0:T(8,128)S(1)} %get-tuple-element.73.refs_0_), channel_id=1, source_target_pairs={{0,2},{3,1},{1,0},{2,3},{4,6},{7,5},{5,4},{6,7},{8,10},{11,9},{9,8... | collective-permute-start | bytes 1572872 | tf_op jit(solution)/shard_map/ppermute | solution.py:299
  79.0 2.9 %shard_map.88.refs_2_.refs_3_ = s32[97]{0:T(128)S(1)} custom-call(s32[196]{0:T(256)S(1)} %concatenate.9.ids), custom_call_target="tpu_custom_call" | custom-call | tf_op jit(solution)/shard_map/pallas_call | solution.py:194
  81.9 7.8 %collective-permute-done.23.refs_1_ = f32[512,256]{1,0:T(8,128)S(1)} collective-permute-done((f32[512,256]{1,0:T(8,128)S(1)}, f32[512,256]{1,0:T(8,128)S(1)}, u32[]{:S(2)}, u32[]{:S(2)}) %collective-permute-start.23) | collective-permute-done | bytes 524320 | tf_op jit(solution)/shard_map/ppermute | solution.py:299
  90.4 3.4 %collective-permute-start.27 = (f32[512,256]{1,0:T(8,128)S(1)}, f32[512,256]{1,0:T(8,128)S(1)}, u32[]{:S(2)}, u32[]{:S(2)}) collective-permute-start(f32[512,256]{1,0:T(8,128)S(1)} %get-tuple-element.73.refs_0_), channel_id=1, source_target_pairs={{2,0},{1,3},{0,1},{3,2},{6,4},{5,7},{4,5},{7,6},{10,8},{9,11},{8,9... | collective-permute-start | bytes 1572872 | tf_op jit(solution)/shard_map/ppermute | solution.py:299
  93.8 1.3 collective-permute-start.29
  95.1 2.0 %collective-permute-start.26 = (f32[128,256]{1,0:T(8,128)S(1)}, f32[128,256]{1,0:T(8,128)S(1)}, u32[]{:S(2)}, u32[]{:S(2)}) collective-permute-start(f32[128,256]{1,0:T(8,128)S(1)} %dynamic-slice_add_fusion), channel_id=1, source_target_pairs={{0,24},{4,28},{8,16},{12,20},{16,8},{20,12},{24,0},{28,4},{1,25},{... | collective-permute-start | bytes 393224 | tf_op jit(solution)/shard_map/ppermute | solution.py:295
  97.1 1.0 collective-permute-start.25
  98.2 4.0 %collective-permute-done.26 = f32[128,256]{1,0:T(8,128)S(1)} collective-permute-done((f32[128,256]{1,0:T(8,128)S(1)}, f32[128,256]{1,0:T(8,128)S(1)}, u32[]{:S(2)}, u32[]{:S(2)}) %collective-permute-start.26) | collective-permute-done | bytes 131104 | tf_op jit(solution)/shard_map/ppermute | solution.py:295
  102.2 1.6 %collective-permute-start.24 = (f32[128,256]{1,0:T(8,128)S(1)}, f32[128,256]{1,0:T(8,128)S(1)}, u32[]{:S(2)}, u32[]{:S(2)}) collective-permute-start(f32[128,256]{1,0:T(8,128)S(1)} %dynamic-slice_add_fusion), channel_id=1, source_target_pairs={{0,8},{4,12},{8,0},{12,4},{16,24},{20,28},{24,16},{28,20},{1,9},{5... | collective-permute-start | bytes 393224 | tf_op jit(solution)/shard_map/ppermute | solution.py:295
  103.7 2.8 %copy-done.1 = f32[1,1,96,128,128]{4,3,2,1,0:T(8,128)S(1)} copy-done((f32[1,1,96,128,128]{4,3,2,1,0:T(8,128)S(1)}, f32[1,1,96,128,128]{4,3,2,1,0:T(8,128)}, u32[]{:S(2)}) %copy-start.1) | copy-done | bytes 6291480
  106.5 9.0 %shard_map.89.refs_4_ = f32[4096,256]{1,0:T(8,128)S(1)} custom-call(s32[196]{0:T(256)S(1)} %concatenate.9.ids, f32[96,128,128]{2,1,0:T(8,128)S(1)} %bitcast.10, f32[512,256]{1,0:T(8,128)S(1)} %get-tuple-element.73.refs_0_, f32[512,256]{1,0:T(8,128)S(1)} %collective-permute-done.23.refs_1_, s32[97]{0:T(128)S(1)} %shard_map.88.refs_2_.refs_3_), custom_call_target="tpu_custom_call" | custom-call | flops 3221225472 | bytes 11534336 | tf_op jit(solution)/shard_map/pallas_call | solution.py:219
  115.6 1.3 collective-permute-done.29.refs_2_
  116.9 6.7 %shard_map.90 = (f32[512,256]{1,0:T(8,128)S(1)}, f32[512,256]{1,0:T(8,128)S(1)}, f32[512,256]{1,0:T(8,128)S(1)}, f32[512,256]{1,0:T(8,128)S(1)}, f32[512,256]{1,...) custom-call(s32[196]{0:T(256)S(1)} %concatenate.9.ids, ...), custom_call_target="tpu_custom_call" | custom-call | flops 3221225472 | bytes 11534336 | tf_op jit(solution)/shard_map/pallas_call | solution.py:219
  124.3 1.3 collective-permute-done.35
  125.8 2.3 %collective-permute-start.36 = (f32[256,256]{1,0:T(8,128)S(1)}, f32[256,256]{1,0:T(8,128)S(1)}, u32[]{:S(2)}, u32[]{:S(2)}) collective-permute-start(f32[256,256]{1,0:T(8,128)S(1)} %get-tuple-element.85), channel_id=1, source_target_pairs={{0,16},{4,20},{8,24},{12,28},{16,0},{20,4},{24,8},{28,12},{1,17},{... | collective-permute-start | bytes 786440 | tf_op jit(solution)/shard_map/ppermute | solution.py:295
  128.0 0.8 collective-permute-start.39
  128.9 1.4 collective-permute-start.30
  130.3 3.7 %collective-permute-done.30 = f32[128,256]{1,0:T(8,128)S(1)} collective-permute-done((f32[128,256]{1,0:T(8,128)S(1)}, f32[128,256]{1,0:T(8,128)S(1)}, u32[]{:S(2)}, u32[]{:S(2)}) %collective-permute-start.30) | collective-permute-done | bytes 131104 | tf_op jit(solution)/shard_map/ppermute | solution.py:299
  134.0 2.1 %collective-permute-done.39 = f32[256,256]{1,0:T(8,128)S(1)} collective-permute-done((f32[256,256]{1,0:T(8,128)S(1)}, f32[256,256]{1,0:T(8,128)S(1)}, u32[]{:S(2)}, u32[]{:S(2)}) %collective-permute-start.39) | collective-permute-done | bytes 262176 | tf_op jit(solution)/shard_map/ppermute | solution.py:295
  136.2 0.9 collective-permute-start.37
  137.1 0.9 pad_add_fusion
  138.0 0.9 collective-permute-start.40
  139.0 8.0 %collective-permute-done.31 = f32[128,256]{1,0:T(8,128)S(1)} collective-permute-done((f32[128,256]{1,0:T(8,128)S(1)}, f32[128,256]{1,0:T(8,128)S(1)}, u32[]{:S(2)}, u32[]{:S(2)}) %collective-permute-start.31) | collective-permute-done | bytes 131104 | tf_op jit(solution)/shard_map/ppermute | solution.py:299
  147.0 1.3 collective-permute-done.32
  149.1 1.8 %collective-permute-done.40 = f32[512,256]{1,0:T(8,128)S(1)} collective-permute-done((f32[512,256]{1,0:T(8,128)}, f32[512,256]{1,0:T(8,128)S(1)}, u32[]{:S(2)}, u32[]{:S(2)}) %collective-permute-start.40) | collective-permute-done | bytes 524320 | tf_op jit(solution)/shard_map/ppermute | solution.py:295
  150.9 0.9 add_add_fusion
  (63 shorter events, 6.1 us)
Async XLA Ops:
  1.7 11.1 %collective-permute-start.5 = (f32[512,128]{1,0:T(8,128)S(1)}, f32[512,128]{1,0:T(8,128)S(1)}, u32[]{:S(2)}, u32[]{:S(2)}) collective-permute-start(f32[512,128]{1,0:T(8,128)S(1)} %get-tuple-element.44.refs_0_), channel_id=1, source_target_pairs={{0,24},{4,28},{8,16},{12,20},{16,8},{20,12},{24,0},{28,4},{1,25},{... | collective-permute-start | bytes 786440 | tf_op jit(solution)/shard_map/ppermute | solution.py:295
  5.7 11.9 %collective-permute-start.3 = (f32[512,128]{1,0:T(8,128)S(1)}, f32[512,128]{1,0:T(8,128)S(1)}, u32[]{:S(2)}, u32[]{:S(2)}) collective-permute-start(f32[512,128]{1,0:T(8,128)S(1)} %get-tuple-element.44.refs_0_), channel_id=1, source_target_pairs={{0,16},{4,20},{8,24},{12,28},{16,0},{20,4},{24,8},{28,12},{1,17},{... | collective-permute-start | bytes 786440 | tf_op jit(solution)/shard_map/ppermute | solution.py:295
  6.2 11.7 %collective-permute-start.1 = (f32[512,128]{1,0:T(8,128)S(1)}, f32[512,128]{1,0:T(8,128)S(1)}, u32[]{:S(2)}, u32[]{:S(2)}) collective-permute-start(f32[512,128]{1,0:T(8,128)S(1)} %get-tuple-element.44.refs_0_), channel_id=1, source_target_pairs={{0,8},{4,12},{8,0},{12,4},{16,24},{20,28},{24,16},{28,20},{1,9},{5... | collective-permute-start | bytes 786440 | tf_op jit(solution)/shard_map/ppermute | solution.py:295
  7.1 12.9 %collective-permute-start = (f32[512,128]{1,0:T(8,128)S(1)}, f32[512,128]{1,0:T(8,128)S(1)}, u32[]{:S(2)}, u32[]{:S(2)}) collective-permute-start(f32[512,128]{1,0:T(8,128)S(1)} %get-tuple-element.44.refs_0_), channel_id=1, source_target_pairs={{0,4},{4,0},{8,12},{12,8},{16,20},{20,16},{24,28},{28,24},{1,5},{5... | collective-permute-start | bytes 786440 | tf_op jit(solution)/shard_map/ppermute | solution.py:295
  12.8 8.4 %collective-permute-start.6 = (f32[512,128]{1,0:T(8,128)S(1)}, f32[512,128]{1,0:T(8,128)S(1)}, u32[]{:S(2)}, u32[]{:S(2)}) collective-permute-start(f32[512,128]{1,0:T(8,128)S(1)} %collective-permute-done.5.refs_6_), channel_id=1, source_target_pairs={{0,4},{4,0},{8,12},{12,8},{16,20},{20,16},{24,28},{28,24},{1,5},{5... | collective-permute-start | bytes 786440 | tf_op jit(solution)/shard_map/ppermute | solution.py:295
  17.6 4.0 %collective-permute-start.4 = (f32[512,128]{1,0:T(8,128)S(1)}, f32[512,128]{1,0:T(8,128)S(1)}, u32[]{:S(2)}, u32[]{:S(2)}) collective-permute-start(f32[512,128]{1,0:T(8,128)S(1)} %collective-permute-done.3.refs_4_), channel_id=1, source_target_pairs={{0,4},{4,0},{8,12},{12,8},{16,20},{20,16},{24,28},{28,24},{1,5},{5... | collective-permute-start | bytes 786440 | tf_op jit(solution)/shard_map/ppermute | solution.py:295
  17.9 3.7 %collective-permute-start.2 = (f32[512,128]{1,0:T(8,128)S(1)}, f32[512,128]{1,0:T(8,128)S(1)}, u32[]{:S(2)}, u32[]{:S(2)}) collective-permute-start(f32[512,128]{1,0:T(8,128)S(1)} %collective-permute-done.1.refs_2_), channel_id=1, source_target_pairs={{0,4},{4,0},{8,12},{12,8},{16,20},{20,16},{24,28},{28,24},{1,5},{5... | collective-permute-start | bytes 786440 | tf_op jit(solution)/shard_map/ppermute | solution.py:295
  18.1 12.8 %collective-permute-start.16 = (f32[512,128]{1,0:T(8,128)S(1)}, f32[512,128]{1,0:T(8,128)S(1)}, u32[]{:S(2)}, u32[]{:S(2)}) collective-permute-start(f32[512,128]{1,0:T(8,128)S(1)} %get-tuple-element.56.refs_0_), channel_id=1, source_target_pairs={{0,24},{4,28},{8,16},{12,20},{16,8},{20,12},{24,0},{28,4},{1,25},{... | collective-permute-start | bytes 786440 | tf_op jit(solution)/shard_map/ppermute | solution.py:295
  19.9 13.2 %collective-permute-start.14 = (f32[512,128]{1,0:T(8,128)S(1)}, f32[512,128]{1,0:T(8,128)S(1)}, u32[]{:S(2)}, u32[]{:S(2)}) collective-permute-start(f32[512,128]{1,0:T(8,128)S(1)} %get-tuple-element.56.refs_0_), channel_id=1, source_target_pairs={{0,16},{4,20},{8,24},{12,28},{16,0},{20,4},{24,8},{28,12},{1,17},{... | collective-permute-start | bytes 786440 | tf_op jit(solution)/shard_map/ppermute | solution.py:295
  21.2 11.9 %collective-permute-start.12 = (f32[512,128]{1,0:T(8,128)S(1)}, f32[512,128]{1,0:T(8,128)S(1)}, u32[]{:S(2)}, u32[]{:S(2)}) collective-permute-start(f32[512,128]{1,0:T(8,128)S(1)} %get-tuple-element.56.refs_0_), channel_id=1, source_target_pairs={{0,8},{4,12},{8,0},{12,4},{16,24},{20,28},{24,16},{28,20},{1,9},{5... | collective-permute-start | bytes 786440 | tf_op jit(solution)/shard_map/ppermute | solution.py:295
  21.6 2.8 %copy-start = (f32[1,1,96,128,128]{4,3,2,1,0:T(8,128)S(1)}, f32[1,1,96,128,128]{4,3,2,1,0:T(8,128)}, u32[]{:S(2)}) copy-start(f32[1,1,96,128,128]{4,3,2,1,0:T(8,128)} %param.11) | copy-start | bytes 18874372
  28.3 46.9 %copy-start.2 = (f32[512,256]{1,0:T(8,128)S(1)}, f32[512,256]{1,0:T(8,128)}, u32[]{:S(2)}) copy-start(f32[512,256]{1,0:T(8,128)} %refs_10_.1) | copy-start | bytes 1572868
  28.3 46.9 %copy-start.3 = (f32[256,256]{1,0:T(8,128)S(1)}, f32[256,256]{1,0:T(8,128)}, u32[]{:S(2)}) copy-start(f32[256,256]{1,0:T(8,128)} %refs_11_.1) | copy-start | bytes 786436
  28.3 7.7 %collective-permute-start.7 = (f32[512,128]{1,0:T(8,128)S(1)}, f32[512,128]{1,0:T(8,128)S(1)}, u32[]{:S(2)}, u32[]{:S(2)}) collective-permute-start(f32[512,128]{1,0:T(8,128)S(1)} %get-tuple-element.49), channel_id=1, source_target_pairs={{0,1},{1,0},{2,3},{3,2},{4,5},{5,4},{6,7},{7,6},{8,9},{9,8},{10,11... | collective-permute-start | bytes 786440 | tf_op jit(solution)/shard_map/ppermute | solution.py:299
  30.2 5.9 %collective-permute-start.8 = (f32[512,128]{1,0:T(8,128)S(1)}, f32[512,128]{1,0:T(8,128)S(1)}, u32[]{:S(2)}, u32[]{:S(2)}) collective-permute-start(f32[512,128]{1,0:T(8,128)S(1)} %get-tuple-element.53), channel_id=1, source_target_pairs={{1,2},{2,1},{5,6},{6,5},{9,10},{10,9},{13,14},{14,13},{17,18},{18,... | collective-permute-start | bytes 786440 | tf_op jit(solution)/shard_map/ppermute | solution.py:299
  30.9 11.1 %collective-permute-start.11 = (f32[512,128]{1,0:T(8,128)S(1)}, f32[512,128]{1,0:T(8,128)S(1)}, u32[]{:S(2)}, u32[]{:S(2)}) collective-permute-start(f32[512,128]{1,0:T(8,128)S(1)} %get-tuple-element.56.refs_0_), channel_id=1, source_target_pairs={{0,4},{4,0},{8,12},{12,8},{16,20},{20,16},{24,28},{28,24},{1,5},{5... | collective-permute-start | bytes 786440 | tf_op jit(solution)/shard_map/ppermute | solution.py:295
  33.1 10.1 %collective-permute-start.13 = (f32[512,128]{1,0:T(8,128)S(1)}, f32[512,128]{1,0:T(8,128)S(1)}, u32[]{:S(2)}, u32[]{:S(2)}) collective-permute-start(f32[512,128]{1,0:T(8,128)S(1)} %collective-permute-done.12.refs_2_), channel_id=1, source_target_pairs={{0,4},{4,0},{8,12},{12,8},{16,20},{20,16},{24,28},{28,24},{1,5},{5... | collective-permute-start | bytes 786440 | tf_op jit(solution)/shard_map/ppermute | solution.py:295
  33.1 10.1 %collective-permute-start.15 = (f32[512,128]{1,0:T(8,128)S(1)}, f32[512,128]{1,0:T(8,128)S(1)}, u32[]{:S(2)}, u32[]{:S(2)}) collective-permute-start(f32[512,128]{1,0:T(8,128)S(1)} %collective-permute-done.14.refs_4_), channel_id=1, source_target_pairs={{0,4},{4,0},{8,12},{12,8},{16,20},{20,16},{24,28},{28,24},{1,5},{5... | collective-permute-start | bytes 786440 | tf_op jit(solution)/shard_map/ppermute | solution.py:295
  36.1 7.2 %collective-permute-start.17 = (f32[512,128]{1,0:T(8,128)S(1)}, f32[512,128]{1,0:T(8,128)S(1)}, u32[]{:S(2)}, u32[]{:S(2)}) collective-permute-start(f32[512,128]{1,0:T(8,128)S(1)} %collective-permute-done.16.refs_6_), channel_id=1, source_target_pairs={{0,4},{4,0},{8,12},{12,8},{16,20},{20,16},{24,28},{28,24},{1,5},{5... | collective-permute-start | bytes 786440 | tf_op jit(solution)/shard_map/ppermute | solution.py:295
  36.1 16.0 %collective-permute-start.9 = (f32[512,128]{1,0:T(8,128)S(1)}, f32[512,128]{1,0:T(8,128)S(1)}, u32[]{:S(2)}, u32[]{:S(2)}) collective-permute-start(f32[512,128]{1,0:T(8,128)S(1)} %select_add_fusion.1), channel_id=1, source_target_pairs={{0,2},{1,3},{2,0},{3,1},{4,6},{5,7},{6,4},{7,5},{8,10},{9,11},{10,... | collective-permute-start | bytes 786440 | tf_op jit(solution)/shard_map/ppermute | solution.py:299
  41.9 10.1 %collective-permute-start.10 = (f32[512,128]{1,0:T(8,128)S(1)}, f32[512,128]{1,0:T(8,128)S(1)}, u32[]{:S(2)}, u32[]{:S(2)}) collective-permute-start(f32[512,128]{1,0:T(8,128)S(1)} %get-tuple-element.53), channel_id=1, source_target_pairs={{0,1},{3,2},{4,5},{7,6},{8,9},{11,10},{12,13},{15,14},{16,17},{19,... | collective-permute-start | bytes 786440 | tf_op jit(solution)/shard_map/ppermute | solution.py:299
  52.1 7.0 %collective-permute-start.18 = (f32[512,128]{1,0:T(8,128)S(1)}, f32[512,128]{1,0:T(8,128)S(1)}, u32[]{:S(2)}, u32[]{:S(2)}) collective-permute-start(f32[512,128]{1,0:T(8,128)S(1)} %get-tuple-element.62), channel_id=1, source_target_pairs={{0,1},{1,0},{2,3},{3,2},{4,5},{5,4},{6,7},{7,6},{8,9},{9,8},{10,11... | collective-permute-start | bytes 786440 | tf_op jit(solution)/shard_map/ppermute | solution.py:299
  53.9 5.2 %collective-permute-start.19 = (f32[512,128]{1,0:T(8,128)S(1)}, f32[512,128]{1,0:T(8,128)S(1)}, u32[]{:S(2)}, u32[]{:S(2)}) collective-permute-start(f32[512,128]{1,0:T(8,128)S(1)} %get-tuple-element.67), channel_id=1, source_target_pairs={{1,2},{2,1},{5,6},{6,5},{9,10},{10,9},{13,14},{14,13},{17,18},{18,... | collective-permute-start | bytes 786440 | tf_op jit(solution)/shard_map/ppermute | solution.py:299
  59.1 16.1 %collective-permute-start.20 = (f32[512,128]{1,0:T(8,128)S(1)}, f32[512,128]{1,0:T(8,128)S(1)}, u32[]{:S(2)}, u32[]{:S(2)}) collective-permute-start(f32[512,128]{1,0:T(8,128)S(1)} %select_add_fusion), channel_id=1, source_target_pairs={{0,2},{1,3},{2,0},{3,1},{4,6},{5,7},{6,4},{7,5},{8,10},{9,11},{10,... | collective-permute-start | bytes 786440 | tf_op jit(solution)/shard_map/ppermute | solution.py:299
  65.1 10.1 %collective-permute-start.21 = (f32[512,128]{1,0:T(8,128)S(1)}, f32[512,128]{1,0:T(8,128)S(1)}, u32[]{:S(2)}, u32[]{:S(2)}) collective-permute-start(f32[512,128]{1,0:T(8,128)S(1)} %get-tuple-element.67), channel_id=1, source_target_pairs={{0,1},{3,2},{4,5},{7,6},{8,9},{11,10},{12,13},{15,14},{16,17},{19,... | collective-permute-start | bytes 786440 | tf_op jit(solution)/shard_map/ppermute | solution.py:299
  77.1 12.6 %collective-permute-start.23 = (f32[512,256]{1,0:T(8,128)S(1)}, f32[512,256]{1,0:T(8,128)S(1)}, u32[]{:S(2)}, u32[]{:S(2)}) collective-permute-start(f32[512,256]{1,0:T(8,128)S(1)} %get-tuple-element.73.refs_0_), channel_id=1, source_target_pairs={{0,2},{3,1},{1,0},{2,3},{4,6},{7,5},{5,4},{6,7},{8,10},{11,9},{9,8... | collective-permute-start | bytes 1572872 | tf_op jit(solution)/shard_map/ppermute | solution.py:299
  78.9 16.2 %collective-permute-start.22 = (f32[128,256]{1,0:T(8,128)S(1)}, f32[128,256]{1,0:T(8,128)S(1)}, u32[]{:S(2)}, u32[]{:S(2)}) collective-permute-start(f32[128,256]{1,0:T(8,128)S(1)} %constant_dynamic-slice_fusion), channel_id=1, source_target_pairs={{0,4},{4,0},{8,12},{12,8},{16,20},{20,16},{24,28},{28,24},{1,5},{5... | collective-permute-start | bytes 393224 | tf_op jit(solution)/shard_map/ppermute | solution.py:295
  89.7 25.8 %collective-permute-start.28 = (f32[512,256]{1,0:T(8,128)S(1)}, f32[512,256]{1,0:T(8,128)S(1)}, u32[]{:S(2)}, u32[]{:S(2)}) collective-permute-start(f32[512,256]{1,0:T(8,128)S(1)} %get-tuple-element.73.refs_0_), channel_id=1, source_target_pairs={{1,2},{2,1},{5,6},{6,5},{9,10},{10,9},{13,14},{14,13},{17,18},{18,... | collective-permute-start | bytes 1572872 | tf_op jit(solution)/shard_map/ppermute | solution.py:299
  90.4 25.1 %collective-permute-start.27 = (f32[512,256]{1,0:T(8,128)S(1)}, f32[512,256]{1,0:T(8,128)S(1)}, u32[]{:S(2)}, u32[]{:S(2)}) collective-permute-start(f32[512,256]{1,0:T(8,128)S(1)} %get-tuple-element.73.refs_0_), channel_id=1, source_target_pairs={{2,0},{1,3},{0,1},{3,2},{6,4},{5,7},{4,5},{7,6},{10,8},{9,11},{8,9... | collective-permute-start | bytes 1572872 | tf_op jit(solution)/shard_map/ppermute | solution.py:299
  93.8 23.1 %collective-permute-start.29 = (f32[512,256]{1,0:T(8,128)S(1)}, f32[512,256]{1,0:T(8,128)S(1)}, u32[]{:S(2)}, u32[]{:S(2)}) collective-permute-start(f32[512,256]{1,0:T(8,128)S(1)} %collective-permute-done.23.refs_1_), channel_id=1, source_target_pairs={{1,0},{2,3},{5,4},{6,7},{9,8},{10,11},{13,12},{14,15},{17,16},{18,... | collective-permute-start | bytes 1572872 | tf_op jit(solution)/shard_map/ppermute | solution.py:299
  95.1 7.0 %collective-permute-start.26 = (f32[128,256]{1,0:T(8,128)S(1)}, f32[128,256]{1,0:T(8,128)S(1)}, u32[]{:S(2)}, u32[]{:S(2)}) collective-permute-start(f32[128,256]{1,0:T(8,128)S(1)} %dynamic-slice_add_fusion), channel_id=1, source_target_pairs={{0,24},{4,28},{8,16},{12,20},{16,8},{20,12},{24,0},{28,4},{1,25},{... | collective-permute-start | bytes 393224 | tf_op jit(solution)/shard_map/ppermute | solution.py:295
  97.1 18.4 %collective-permute-start.25 = (f32[128,256]{1,0:T(8,128)S(1)}, f32[128,256]{1,0:T(8,128)S(1)}, u32[]{:S(2)}, u32[]{:S(2)}) collective-permute-start(f32[128,256]{1,0:T(8,128)S(1)} %dynamic-slice_add_fusion), channel_id=1, source_target_pairs={{0,16},{4,20},{8,24},{12,28},{16,0},{20,4},{24,8},{28,12},{1,17},{... | collective-permute-start | bytes 393224 | tf_op jit(solution)/shard_map/ppermute | solution.py:295
  102.2 13.4 %collective-permute-start.24 = (f32[128,256]{1,0:T(8,128)S(1)}, f32[128,256]{1,0:T(8,128)S(1)}, u32[]{:S(2)}, u32[]{:S(2)}) collective-permute-start(f32[128,256]{1,0:T(8,128)S(1)} %dynamic-slice_add_fusion), channel_id=1, source_target_pairs={{0,8},{4,12},{8,0},{12,4},{16,24},{20,28},{24,16},{28,20},{1,9},{5... | collective-permute-start | bytes 393224 | tf_op jit(solution)/shard_map/ppermute | solution.py:295
  103.7 2.8 %copy-start.1 = (f32[1,1,96,128,128]{4,3,2,1,0:T(8,128)S(1)}, f32[1,1,96,128,128]{4,3,2,1,0:T(8,128)}, u32[]{:S(2)}) copy-start(f32[1,1,96,128,128]{4,3,2,1,0:T(8,128)} %param.11) | copy-start | bytes 18874372
  123.7 2.0 %collective-permute-start.35 = (f32[512,256]{1,0:T(8,128)S(1)}, f32[512,256]{1,0:T(8,128)S(1)}, u32[]{:S(2)}, u32[]{:S(2)}) collective-permute-start(f32[512,256]{1,0:T(8,128)S(1)} %get-tuple-element.81), channel_id=1, source_target_pairs={{0,4},{4,0},{8,12},{12,8},{16,20},{20,16},{24,28},{28,24},{1,5},{5... | collective-permute-start | bytes 1572872 | tf_op jit(solution)/shard_map/ppermute | solution.py:295
  123.7 12.4 %collective-permute-start.34 = (f32[512,256]{1,0:T(8,128)S(1)}, f32[512,256]{1,0:T(8,128)S(1)}, u32[]{:S(2)}, u32[]{:S(2)}) collective-permute-start(f32[512,256]{1,0:T(8,128)S(1)} %get-tuple-element.79), channel_id=1, source_target_pairs={{0,4},{4,0},{8,12},{12,8},{16,20},{20,16},{24,28},{28,24},{1,5},{5... | collective-permute-start | bytes 1572872 | tf_op jit(solution)/shard_map/ppermute | solution.py:295
  124.2 12.9 %collective-permute-start.38 = (f32[512,256]{1,0:T(8,128)S(1)}, f32[512,256]{1,0:T(8,128)S(1)}, u32[]{:S(2)}, u32[]{:S(2)}) collective-permute-start(f32[512,256]{1,0:T(8,128)S(1)} %get-tuple-element.83), channel_id=1, source_target_pairs={{0,4},{4,0},{8,12},{12,8},{16,20},{20,16},{24,28},{28,24},{1,5},{5... | collective-permute-start | bytes 1572872 | tf_op jit(solution)/shard_map/ppermute | solution.py:295
  125.8 10.4 %collective-permute-start.36 = (f32[256,256]{1,0:T(8,128)S(1)}, f32[256,256]{1,0:T(8,128)S(1)}, u32[]{:S(2)}, u32[]{:S(2)}) collective-permute-start(f32[256,256]{1,0:T(8,128)S(1)} %get-tuple-element.85), channel_id=1, source_target_pairs={{0,16},{4,20},{8,24},{12,28},{16,0},{20,4},{24,8},{28,12},{1,17},{... | collective-permute-start | bytes 786440 | tf_op jit(solution)/shard_map/ppermute | solution.py:295
  128.0 8.1 %collective-permute-start.39 = (f32[256,256]{1,0:T(8,128)S(1)}, f32[256,256]{1,0:T(8,128)S(1)}, u32[]{:S(2)}, u32[]{:S(2)}) collective-permute-start(f32[256,256]{1,0:T(8,128)S(1)} %get-tuple-element.86), channel_id=1, source_target_pairs={{0,8},{4,12},{8,0},{12,4},{16,24},{20,28},{24,16},{28,20},{1,9},{5... | collective-permute-start | bytes 786440 | tf_op jit(solution)/shard_map/ppermute | solution.py:295
  128.9 5.0 %collective-permute-start.30 = (f32[128,256]{1,0:T(8,128)S(1)}, f32[128,256]{1,0:T(8,128)S(1)}, u32[]{:S(2)}, u32[]{:S(2)}) collective-permute-start(f32[128,256]{1,0:T(8,128)S(1)} %add_add_fusion.1), channel_id=1, source_target_pairs={{0,1},{1,0},{2,3},{3,2},{4,5},{5,4},{6,7},{7,6},{8,9},{9,8},{10,11... | collective-permute-start | bytes 393224 | tf_op jit(solution)/shard_map/ppermute | solution.py:299
  134.0 15.1 %collective-permute-start.33 = (f32[512,256]{1,0:T(8,128)S(1)}, f32[512,256]{1,0:T(8,128)S(1)}, u32[]{:S(2)}, u32[]{:S(2)}) collective-permute-start(f32[512,256]{1,0:T(8,128)S(1)} %get-tuple-element.77), channel_id=1, source_target_pairs={{0,4},{4,0},{8,12},{12,8},{16,20},{20,16},{24,28},{28,24},{1,5},{5... | collective-permute-start | bytes 1572872 | tf_op jit(solution)/shard_map/ppermute | solution.py:295
  136.2 12.9 %collective-permute-start.37 = (f32[512,256]{1,0:T(8,128)S(1)}, f32[512,256]{1,0:T(8,128)S(1)}, u32[]{:S(2)}, u32[]{:S(2)}) collective-permute-start(f32[512,256]{1,0:T(8,128)S(1)} %pad_add_fusion.1), channel_id=1, source_target_pairs={{0,8},{4,12},{8,0},{12,4},{16,24},{20,28},{24,16},{28,20},{1,9},{5... | collective-permute-start | bytes 1572872 | tf_op jit(solution)/shard_map/ppermute | solution.py:295
  138.0 12.9 %collective-permute-start.40 = (f32[512,256]{1,0:T(8,128)}, f32[512,256]{1,0:T(8,128)S(1)}, u32[]{:S(2)}, u32[]{:S(2)}) collective-permute-start(f32[512,256]{1,0:T(8,128)} %pad_add_fusion), channel_id=1, source_target_pairs={{0,16},{4,20},{8,24},{12,28},{16,0},{20,4},{24,8},{28,12},{1,17},{... | collective-permute-start | bytes 1572872 | tf_op jit(solution)/shard_map/ppermute | solution.py:295
  138.9 8.0 %collective-permute-start.31 = (f32[128,256]{1,0:T(8,128)S(1)}, f32[128,256]{1,0:T(8,128)S(1)}, u32[]{:S(2)}, u32[]{:S(2)}) collective-permute-start(f32[128,256]{1,0:T(8,128)S(1)} %add.72), channel_id=1, source_target_pairs={{0,2},{1,3},{2,0},{3,1},{4,6},{5,7},{6,4},{7,5},{8,10},{9,11},{10,... | collective-permute-start | bytes 393224 | tf_op jit(solution)/shard_map/ppermute | solution.py:299
  146.9 1.4 collective-permute-start.32

commit v6 on v5

--- a/solution.py
+++ b/solution.py
@@ -205,7 +205,7 @@
     count, size = values.shape[0], values.shape[-1]
     width = pieces[0].shape[1]
     halves = max(1, width // size)
-    unroll = next(p for p in ((32, 16, 8, 4, 2, 1) if only is None else (8, 4, 2, 1)) if count % p == 0)
+    unroll = next(p for p in ((32, 16, 8, 4, 2, 1) if only is None else (16, 8, 4, 2, 1)) if count % p == 0)
     steps = count // unroll if only is None else 1
     in_rows = sum(group[0].shape[0] for group in groups)
     smem, anywhere = pl.BlockSpec(memory_space=pltpu.SMEM), pl.BlockSpec(memory_space=pl.ANY)

time: 152 us -> 152 us (level)
  waiting for transfers between devices: 65.1 us -> 62.4 us
  starting transfers between devices: 47.2 us -> 49.3 us
    ppermute x14, starting transfers between devices: 27.9 us -> 30.6 us  [along_col(): return lax.ppermute(x, 'col', pairs)]
  transfers between devices with their start and end apart: 41 -> 41, of which waited for: 17 -> 18; matrix products, arithmetic and copies ran while one was open for 2% -> 2% of each run, Pallas kernels for 13% -> 14%
where the time goes in v6:
time: 152 us; the launch traced here: 151 us
  waiting for transfers between devices  62.4 us (41%)
  starting transfers between devices  49.3 us (32%)
  Pallas kernels  28.5 us (19%)
  local copies, waits for them, and re-layouts  7.44 us (5%)
  other arithmetic  2.85 us (2%)
    ppermute x14, waiting for transfers between devices, along_col(): return lax.ppermute(x, 'col', pairs)  40.3 us
    ppermute x14, starting transfers between devices, along_col(): return lax.ppermute(x, 'col', pairs)  30.6 us
    pallas_call x4, Pallas kernels, spmm(): pl.pallas_call(functools.partial(spmm_kernel, [len(group) for group in gr...  23.8 us
    ppermute x27, waiting for transfers between devices, along_row(): lax.ppermute(x, 'row', [(i, i ^ bit) for i in range(lax.axis_size('row'))])  22.1 us
    ppermute x27, starting transfers between devices, along_row(): lax.ppermute(x, 'row', [(i, i ^ bit) for i in range(lax.axis_size('row'))])  18.7 us
    unnamed x8, local copies, waits for them, and re-layouts  5.58 us
  transfers between devices with their start and end apart: 41, of which 18 were waited for; matrix products, arithmetic and copies ran while one was open for 2% of the time, Pallas kernels for 14%

profile of v6, /device:TPU:0, one launch (start us, length us, event | category | flops | bytes accessed | tf_op | source)
XLA Modules:
  0.0 151.4 jit_solution(5401614300182606383)
XLA Ops:
  0.6 1.1 fusion.2
  1.7 4.0 %collective-permute-start.5 = (f32[512,128]{1,0:T(8,128)S(1)}, f32[512,128]{1,0:T(8,128)S(1)}, u32[]{:S(2)}, u32[]{:S(2)}) collective-permute-start(f32[512,128]{1,0:T(8,128)S(1)} %get-tuple-element.44.refs_0_), channel_id=1, source_target_pairs={{0,24},{4,28},{8,16},{12,20},{16,8},{20,12},{24,0},{28,4},{1,25},{... | collective-permute-start | bytes 786440 | tf_op jit(solution)/shard_map/ppermute | solution.py:295
  6.3 0.7 concatenate.9.ids
  7.1 5.8 %collective-permute-done.5.refs_6_ = f32[512,128]{1,0:T(8,128)S(1)} collective-permute-done((f32[512,128]{1,0:T(8,128)S(1)}, f32[512,128]{1,0:T(8,128)S(1)}, u32[]{:S(2)}, u32[]{:S(2)}) %collective-permute-start.5) | collective-permute-done | bytes 262176 | tf_op jit(solution)/shard_map/ppermute | solution.py:295
  12.8 4.7 %collective-permute-done.3.refs_4_ = f32[512,128]{1,0:T(8,128)S(1)} collective-permute-done((f32[512,128]{1,0:T(8,128)S(1)}, f32[512,128]{1,0:T(8,128)S(1)}, u32[]{:S(2)}, u32[]{:S(2)}) %collective-permute-start.3) | collective-permute-done | bytes 262176 | tf_op jit(solution)/shard_map/ppermute | solution.py:295
  18.1 1.8 %collective-permute-start.16 = (f32[512,128]{1,0:T(8,128)S(1)}, f32[512,128]{1,0:T(8,128)S(1)}, u32[]{:S(2)}, u32[]{:S(2)}) collective-permute-start(f32[512,128]{1,0:T(8,128)S(1)} %get-tuple-element.56.refs_0_), channel_id=1, source_target_pairs={{0,24},{4,28},{8,16},{12,20},{16,8},{20,12},{24,0},{28,4},{1,25},{... | collective-permute-start | bytes 786440 | tf_op jit(solution)/shard_map/ppermute | solution.py:295
  19.9 1.3 collective-permute-start.14
  21.6 2.8 %copy-done = f32[1,1,96,128,128]{4,3,2,1,0:T(8,128)S(1)} copy-done((f32[1,1,96,128,128]{4,3,2,1,0:T(8,128)S(1)}, f32[1,1,96,128,128]{4,3,2,1,0:T(8,128)}, u32[]{:S(2)}) %copy-start) | copy-done | bytes 6291480
  24.4 3.9 %shard_map.85 = (f32[512,128]{1,0:T(8,128)S(1)}, f32[512,128]{1,0:T(8,128)S(1)}, f32[512,128]{1,0:T(8,128)S(1)}, f32[512,128]{1,0:T(8,128)S(1)}) custom-call(s32[196]{0:T(256)S(1)} %concatenate.9.ids, f32[96,128,128]{2,1,0:T(8,128)S(1)} %bitcast.8, f32[512,128]{1,0:T(8,128)S(1)} %get-tuple-element.44.refs_0_, f32[512,128]{1,0:T(8,128)S(1)} %collective-permute-done.refs_1_, ...), custom_call_target="tpu_custom_call" | custom-call | flops 1610612736 | bytes 9437184 | tf_op jit(solution)/shard_map/pallas_call | solution.py:219
  28.4 1.8 %collective-permute-start.7 = (f32[512,128]{1,0:T(8,128)S(1)}, f32[512,128]{1,0:T(8,128)S(1)}, u32[]{:S(2)}, u32[]{:S(2)}) collective-permute-start(f32[512,128]{1,0:T(8,128)S(1)} %get-tuple-element.49), channel_id=1, source_target_pairs={{0,1},{1,0},{2,3},{3,2},{4,5},{5,4},{6,7},{7,6},{8,9},{9,8},{10,11... | collective-permute-start | bytes 786440 | tf_op jit(solution)/shard_map/ppermute | solution.py:299
  30.9 2.2 %collective-permute-done.14.refs_4_ = f32[512,128]{1,0:T(8,128)S(1)} collective-permute-done((f32[512,128]{1,0:T(8,128)S(1)}, f32[512,128]{1,0:T(8,128)S(1)}, u32[]{:S(2)}, u32[]{:S(2)}) %collective-permute-start.14) | collective-permute-done | bytes 262176 | tf_op jit(solution)/shard_map/ppermute | solution.py:295
  33.6 2.4 %collective-permute-done.7.refs_1_ = f32[512,128]{1,0:T(8,128)S(1)} collective-permute-done((f32[512,128]{1,0:T(8,128)S(1)}, f32[512,128]{1,0:T(8,128)S(1)}, u32[]{:S(2)}, u32[]{:S(2)}) %collective-permute-start.7) | collective-permute-done | bytes 262176 | tf_op jit(solution)/shard_map/ppermute | solution.py:299
  36.1 5.8 %collective-permute-start.9 = (f32[512,128]{1,0:T(8,128)S(1)}, f32[512,128]{1,0:T(8,128)S(1)}, u32[]{:S(2)}, u32[]{:S(2)}) collective-permute-start(f32[512,128]{1,0:T(8,128)S(1)} %select_add_fusion.1), channel_id=1, source_target_pairs={{0,2},{1,3},{2,0},{3,1},{4,6},{5,7},{6,4},{7,5},{8,10},{9,11},{10,... | collective-permute-start | bytes 786440 | tf_op jit(solution)/shard_map/ppermute | solution.py:299
  41.9 1.3 collective-permute-start.10
  43.3 3.9 %shard_map.86 = (f32[512,128]{1,0:T(8,128)S(1)}, f32[512,128]{1,0:T(8,128)S(1)}, f32[512,128]{1,0:T(8,128)S(1)}, f32[512,128]{1,0:T(8,128)S(1)}) custom-call(s32[196]{0:T(256)S(1)} %concatenate.9.ids, f32[96,128,128]{2,1,0:T(8,128)S(1)} %bitcast.9, f32[512,128]{1,0:T(8,128)S(1)} %get-tuple-element.56.refs_0_, ...), custom_call_target="tpu_custom_call" | custom-call | flops 1610612736 | bytes 9437184 | tf_op jit(solution)/shard_map/pallas_call | solution.py:219
  47.2 4.9 %collective-permute-done.9.refs_3_ = f32[512,128]{1,0:T(8,128)S(1)} collective-permute-done((f32[512,128]{1,0:T(8,128)S(1)}, f32[512,128]{1,0:T(8,128)S(1)}, u32[]{:S(2)}, u32[]{:S(2)}) %collective-permute-start.9) | collective-permute-done | bytes 262176 | tf_op jit(solution)/shard_map/ppermute | solution.py:299
  52.1 1.8 %collective-permute-start.18 = (f32[512,128]{1,0:T(8,128)S(1)}, f32[512,128]{1,0:T(8,128)S(1)}, u32[]{:S(2)}, u32[]{:S(2)}) collective-permute-start(f32[512,128]{1,0:T(8,128)S(1)} %get-tuple-element.62), channel_id=1, source_target_pairs={{0,1},{1,0},{2,3},{3,2},{4,5},{5,4},{6,7},{7,6},{8,9},{9,8},{10,11... | collective-permute-start | bytes 786440 | tf_op jit(solution)/shard_map/ppermute | solution.py:299
  54.5 4.5 %collective-permute-done.18.refs_6_ = f32[512,128]{1,0:T(8,128)S(1)} collective-permute-done((f32[512,128]{1,0:T(8,128)S(1)}, f32[512,128]{1,0:T(8,128)S(1)}, u32[]{:S(2)}, u32[]{:S(2)}) %collective-permute-start.18) | collective-permute-done | bytes 262176 | tf_op jit(solution)/shard_map/ppermute | solution.py:299
  59.1 6.0 %collective-permute-start.20 = (f32[512,128]{1,0:T(8,128)S(1)}, f32[512,128]{1,0:T(8,128)S(1)}, u32[]{:S(2)}, u32[]{:S(2)}) collective-permute-start(f32[512,128]{1,0:T(8,128)S(1)} %select_add_fusion), channel_id=1, source_target_pairs={{0,2},{1,3},{2,0},{3,1},{4,6},{5,7},{6,4},{7,5},{8,10},{9,11},{10,... | collective-permute-start | bytes 786440 | tf_op jit(solution)/shard_map/ppermute | solution.py:299
  65.1 1.3 collective-permute-start.21
  66.4 8.8 %collective-permute-done.20.refs_8_ = f32[512,128]{1,0:T(8,128)S(1)} collective-permute-done((f32[512,128]{1,0:T(8,128)S(1)}, f32[512,128]{1,0:T(8,128)S(1)}, u32[]{:S(2)}, u32[]{:S(2)}) %collective-permute-start.20) | collective-permute-done | bytes 262176 | tf_op jit(solution)/shard_map/ppermute | solution.py:299
  75.2 1.9 %shard_map.87 = (f32[512,256]{1,0:T(8,128)}, f32[512,256]{1,0:T(8,128)S(1)}, f32[256,256]{1,0:T(8,128)S(1)}) custom-call(s32[196]{0:T(256)S(1)} %concatenate.9.ids, f32[512,128]{1,0:T(8,128)S(1)} %get-tuple-element.48.refs_0_, f32[512,128]{1,0:T(8,128)S(1)} %collective-permute-done.7.refs_1_, f32[512,128]{1,0:T(8,128)S(1)} %collective-permute-done.8.refs_2_, ...), custom_call_target="tpu_custom_call" | custom-call | flops 1000 | bytes 1000 | tf_op jit(solution)/shard_map/pallas_call | solution.py:277
  77.1 1.8 %collective-permute-start.23 = (f32[512,256]{1,0:T(8,128)S(1)}, f32[512,256]{1,0:T(8,128)S(1)}, u32[]{:S(2)}, u32[]{:S(2)}) collective-permute-start(f32[512,256]{1,0:T(8,128)S(1)} %get-tuple-element.73.refs_0_), channel_id=1, source_target_pairs={{0,2},{3,1},{1,0},{2,3},{4,6},{7,5},{5,4},{6,7},{8,10},{11,9},{9,8... | collective-permute-start | bytes 1572872 | tf_op jit(solution)/shard_map/ppermute | solution.py:299
  79.0 2.9 %shard_map.88.refs_2_.refs_3_ = s32[97]{0:T(128)S(1)} custom-call(s32[196]{0:T(256)S(1)} %concatenate.9.ids), custom_call_target="tpu_custom_call" | custom-call | tf_op jit(solution)/shard_map/pallas_call | solution.py:194
  81.9 7.8 %collective-permute-done.23.refs_1_ = f32[512,256]{1,0:T(8,128)S(1)} collective-permute-done((f32[512,256]{1,0:T(8,128)S(1)}, f32[512,256]{1,0:T(8,128)S(1)}, u32[]{:S(2)}, u32[]{:S(2)}) %collective-permute-start.23) | collective-permute-done | bytes 524320 | tf_op jit(solution)/shard_map/ppermute | solution.py:299
  90.4 3.4 %collective-permute-start.27 = (f32[512,256]{1,0:T(8,128)S(1)}, f32[512,256]{1,0:T(8,128)S(1)}, u32[]{:S(2)}, u32[]{:S(2)}) collective-permute-start(f32[512,256]{1,0:T(8,128)S(1)} %get-tuple-element.73.refs_0_), channel_id=1, source_target_pairs={{2,0},{1,3},{0,1},{3,2},{6,4},{5,7},{4,5},{7,6},{10,8},{9,11},{8,9... | collective-permute-start | bytes 1572872 | tf_op jit(solution)/shard_map/ppermute | solution.py:299
  93.8 1.3 collective-permute-start.29
  95.1 2.0 %collective-permute-start.26 = (f32[128,256]{1,0:T(8,128)S(1)}, f32[128,256]{1,0:T(8,128)S(1)}, u32[]{:S(2)}, u32[]{:S(2)}) collective-permute-start(f32[128,256]{1,0:T(8,128)S(1)} %dynamic-slice_add_fusion), channel_id=1, source_target_pairs={{0,24},{4,28},{8,16},{12,20},{16,8},{20,12},{24,0},{28,4},{1,25},{... | collective-permute-start | bytes 393224 | tf_op jit(solution)/shard_map/ppermute | solution.py:295
  97.1 1.0 collective-permute-start.25
  98.1 4.0 %collective-permute-done.26 = f32[128,256]{1,0:T(8,128)S(1)} collective-permute-done((f32[128,256]{1,0:T(8,128)S(1)}, f32[128,256]{1,0:T(8,128)S(1)}, u32[]{:S(2)}, u32[]{:S(2)}) %collective-permute-start.26) | collective-permute-done | bytes 131104 | tf_op jit(solution)/shard_map/ppermute | solution.py:295
  102.1 1.6 %collective-permute-start.24 = (f32[128,256]{1,0:T(8,128)S(1)}, f32[128,256]{1,0:T(8,128)S(1)}, u32[]{:S(2)}, u32[]{:S(2)}) collective-permute-start(f32[128,256]{1,0:T(8,128)S(1)} %dynamic-slice_add_fusion), channel_id=1, source_target_pairs={{0,8},{4,12},{8,0},{12,4},{16,24},{20,28},{24,16},{28,20},{1,9},{5... | collective-permute-start | bytes 393224 | tf_op jit(solution)/shard_map/ppermute | solution.py:295
  103.7 2.8 %copy-done.1 = f32[1,1,96,128,128]{4,3,2,1,0:T(8,128)S(1)} copy-done((f32[1,1,96,128,128]{4,3,2,1,0:T(8,128)S(1)}, f32[1,1,96,128,128]{4,3,2,1,0:T(8,128)}, u32[]{:S(2)}) %copy-start.1) | copy-done | bytes 6291480
  106.5 10.1 %shard_map.89.refs_4_ = f32[4096,256]{1,0:T(8,128)S(1)} custom-call(s32[196]{0:T(256)S(1)} %concatenate.9.ids, f32[96,128,128]{2,1,0:T(8,128)S(1)} %bitcast.10, f32[512,256]{1,0:T(8,128)S(1)} %get-tuple-element.73.refs_0_, f32[512,256]{1,0:T(8,128)S(1)} %collective-permute-done.23.refs_1_, s32[97]{0:T(128)S(1)} %shard_map.88.refs_2_.refs_3_), custom_call_target="tpu_custom_call" | custom-call | flops 3221225472 | bytes 11534336 | tf_op jit(solution)/shard_map/pallas_call | solution.py:219
  116.9 5.8 %shard_map.90 = (f32[512,256]{1,0:T(8,128)S(1)}, f32[512,256]{1,0:T(8,128)S(1)}, f32[512,256]{1,0:T(8,128)S(1)}, f32[512,256]{1,0:T(8,128)S(1)}, f32[512,256]{1,...) custom-call(s32[196]{0:T(256)S(1)} %concatenate.9.ids, ...), custom_call_target="tpu_custom_call" | custom-call | flops 3221225472 | bytes 11534336 | tf_op jit(solution)/shard_map/pallas_call | solution.py:219
  123.4 1.3 collective-permute-done.35
  124.8 1.8 %collective-permute-start.36 = (f32[256,256]{1,0:T(8,128)S(1)}, f32[256,256]{1,0:T(8,128)S(1)}, u32[]{:S(2)}, u32[]{:S(2)}) collective-permute-start(f32[256,256]{1,0:T(8,128)S(1)} %get-tuple-element.85), channel_id=1, source_target_pairs={{0,16},{4,20},{8,24},{12,28},{16,0},{20,4},{24,8},{28,12},{1,17},{... | collective-permute-start | bytes 786440 | tf_op jit(solution)/shard_map/ppermute | solution.py:295
  126.6 0.8 collective-permute-start.39
  127.5 3.4 %collective-permute-start.30 = (f32[128,256]{1,0:T(8,128)S(1)}, f32[128,256]{1,0:T(8,128)S(1)}, u32[]{:S(2)}, u32[]{:S(2)}) collective-permute-start(f32[128,256]{1,0:T(8,128)S(1)} %add_add_fusion.1), channel_id=1, source_target_pairs={{0,1},{1,0},{2,3},{3,2},{4,5},{5,4},{6,7},{7,6},{8,9},{9,8},{10,11... | collective-permute-start | bytes 393224 | tf_op jit(solution)/shard_map/ppermute | solution.py:299
  130.9 3.2 %collective-permute-done.30 = f32[128,256]{1,0:T(8,128)S(1)} collective-permute-done((f32[128,256]{1,0:T(8,128)S(1)}, f32[128,256]{1,0:T(8,128)S(1)}, u32[]{:S(2)}, u32[]{:S(2)}) %collective-permute-start.30) | collective-permute-done | bytes 131104 | tf_op jit(solution)/shard_map/ppermute | solution.py:299
  134.8 0.9 collective-permute-start.37
  135.7 0.9 pad_add_fusion
  136.6 0.9 collective-permute-start.40
  137.5 0.7 collective-permute-start.31
  138.2 8.3 %collective-permute-done.31 = f32[128,256]{1,0:T(8,128)S(1)} collective-permute-done((f32[128,256]{1,0:T(8,128)S(1)}, f32[128,256]{1,0:T(8,128)S(1)}, u32[]{:S(2)}, u32[]{:S(2)}) %collective-permute-start.31) | collective-permute-done | bytes 131104 | tf_op jit(solution)/shard_map/ppermute | solution.py:299
  146.6 1.3 collective-permute-done.32
  147.9 0.7 fusion
  148.7 1.8 %collective-permute-done.40 = f32[512,256]{1,0:T(8,128)S(1)} collective-permute-done((f32[512,256]{1,0:T(8,128)}, f32[512,256]{1,0:T(8,128)S(1)}, u32[]{:S(2)}, u32[]{:S(2)}) %collective-permute-start.40) | collective-permute-done | bytes 524320 | tf_op jit(solution)/shard_map/ppermute | solution.py:295
  150.5 0.9 add_add_fusion
  (63 shorter events, 6.2 us)
Async XLA Ops:
  1.7 11.1 %collective-permute-start.5 = (f32[512,128]{1,0:T(8,128)S(1)}, f32[512,128]{1,0:T(8,128)S(1)}, u32[]{:S(2)}, u32[]{:S(2)}) collective-permute-start(f32[512,128]{1,0:T(8,128)S(1)} %get-tuple-element.44.refs_0_), channel_id=1, source_target_pairs={{0,24},{4,28},{8,16},{12,20},{16,8},{20,12},{24,0},{28,4},{1,25},{... | collective-permute-start | bytes 786440 | tf_op jit(solution)/shard_map/ppermute | solution.py:295
  5.7 11.9 %collective-permute-start.3 = (f32[512,128]{1,0:T(8,128)S(1)}, f32[512,128]{1,0:T(8,128)S(1)}, u32[]{:S(2)}, u32[]{:S(2)}) collective-permute-start(f32[512,128]{1,0:T(8,128)S(1)} %get-tuple-element.44.refs_0_), channel_id=1, source_target_pairs={{0,16},{4,20},{8,24},{12,28},{16,0},{20,4},{24,8},{28,12},{1,17},{... | collective-permute-start | bytes 786440 | tf_op jit(solution)/shard_map/ppermute | solution.py:295
  6.2 11.7 %collective-permute-start.1 = (f32[512,128]{1,0:T(8,128)S(1)}, f32[512,128]{1,0:T(8,128)S(1)}, u32[]{:S(2)}, u32[]{:S(2)}) collective-permute-start(f32[512,128]{1,0:T(8,128)S(1)} %get-tuple-element.44.refs_0_), channel_id=1, source_target_pairs={{0,8},{4,12},{8,0},{12,4},{16,24},{20,28},{24,16},{28,20},{1,9},{5... | collective-permute-start | bytes 786440 | tf_op jit(solution)/shard_map/ppermute | solution.py:295
  7.1 12.9 %collective-permute-start = (f32[512,128]{1,0:T(8,128)S(1)}, f32[512,128]{1,0:T(8,128)S(1)}, u32[]{:S(2)}, u32[]{:S(2)}) collective-permute-start(f32[512,128]{1,0:T(8,128)S(1)} %get-tuple-element.44.refs_0_), channel_id=1, source_target_pairs={{0,4},{4,0},{8,12},{12,8},{16,20},{20,16},{24,28},{28,24},{1,5},{5... | collective-permute-start | bytes 786440 | tf_op jit(solution)/shard_map/ppermute | solution.py:295
  12.8 8.4 %collective-permute-start.6 = (f32[512,128]{1,0:T(8,128)S(1)}, f32[512,128]{1,0:T(8,128)S(1)}, u32[]{:S(2)}, u32[]{:S(2)}) collective-permute-start(f32[512,128]{1,0:T(8,128)S(1)} %collective-permute-done.5.refs_6_), channel_id=1, source_target_pairs={{0,4},{4,0},{8,12},{12,8},{16,20},{20,16},{24,28},{28,24},{1,5},{5... | collective-permute-start | bytes 786440 | tf_op jit(solution)/shard_map/ppermute | solution.py:295
  17.6 4.0 %collective-permute-start.4 = (f32[512,128]{1,0:T(8,128)S(1)}, f32[512,128]{1,0:T(8,128)S(1)}, u32[]{:S(2)}, u32[]{:S(2)}) collective-permute-start(f32[512,128]{1,0:T(8,128)S(1)} %collective-permute-done.3.refs_4_), channel_id=1, source_target_pairs={{0,4},{4,0},{8,12},{12,8},{16,20},{20,16},{24,28},{28,24},{1,5},{5... | collective-permute-start | bytes 786440 | tf_op jit(solution)/shard_map/ppermute | solution.py:295
  17.9 3.7 %collective-permute-start.2 = (f32[512,128]{1,0:T(8,128)S(1)}, f32[512,128]{1,0:T(8,128)S(1)}, u32[]{:S(2)}, u32[]{:S(2)}) collective-permute-start(f32[512,128]{1,0:T(8,128)S(1)} %collective-permute-done.1.refs_2_), channel_id=1, source_target_pairs={{0,4},{4,0},{8,12},{12,8},{16,20},{20,16},{24,28},{28,24},{1,5},{5... | collective-permute-start | bytes 786440 | tf_op jit(solution)/shard_map/ppermute | solution.py:295
  18.1 12.8 %collective-permute-start.16 = (f32[512,128]{1,0:T(8,128)S(1)}, f32[512,128]{1,0:T(8,128)S(1)}, u32[]{:S(2)}, u32[]{:S(2)}) collective-permute-start(f32[512,128]{1,0:T(8,128)S(1)} %get-tuple-element.56.refs_0_), channel_id=1, source_target_pairs={{0,24},{4,28},{8,16},{12,20},{16,8},{20,12},{24,0},{28,4},{1,25},{... | collective-permute-start | bytes 786440 | tf_op jit(solution)/shard_map/ppermute | solution.py:295
  19.9 13.2 %collective-permute-start.14 = (f32[512,128]{1,0:T(8,128)S(1)}, f32[512,128]{1,0:T(8,128)S(1)}, u32[]{:S(2)}, u32[]{:S(2)}) collective-permute-start(f32[512,128]{1,0:T(8,128)S(1)} %get-tuple-element.56.refs_0_), channel_id=1, source_target_pairs={{0,16},{4,20},{8,24},{12,28},{16,0},{20,4},{24,8},{28,12},{1,17},{... | collective-permute-start | bytes 786440 | tf_op jit(solution)/shard_map/ppermute | solution.py:295
  21.2 11.9 %collective-permute-start.12 = (f32[512,128]{1,0:T(8,128)S(1)}, f32[512,128]{1,0:T(8,128)S(1)}, u32[]{:S(2)}, u32[]{:S(2)}) collective-permute-start(f32[512,128]{1,0:T(8,128)S(1)} %get-tuple-element.56.refs_0_), channel_id=1, source_target_pairs={{0,8},{4,12},{8,0},{12,4},{16,24},{20,28},{24,16},{28,20},{1,9},{5... | collective-permute-start | bytes 786440 | tf_op jit(solution)/shard_map/ppermute | solution.py:295
  21.6 2.8 %copy-start = (f32[1,1,96,128,128]{4,3,2,1,0:T(8,128)S(1)}, f32[1,1,96,128,128]{4,3,2,1,0:T(8,128)}, u32[]{:S(2)}) copy-start(f32[1,1,96,128,128]{4,3,2,1,0:T(8,128)} %param.11) | copy-start | bytes 18874372
  28.3 46.9 %copy-start.2 = (f32[512,256]{1,0:T(8,128)S(1)}, f32[512,256]{1,0:T(8,128)}, u32[]{:S(2)}) copy-start(f32[512,256]{1,0:T(8,128)} %refs_10_.1) | copy-start | bytes 1572868
  28.3 46.9 %copy-start.3 = (f32[256,256]{1,0:T(8,128)S(1)}, f32[256,256]{1,0:T(8,128)}, u32[]{:S(2)}) copy-start(f32[256,256]{1,0:T(8,128)} %refs_11_.1) | copy-start | bytes 786436
  28.4 7.7 %collective-permute-start.7 = (f32[512,128]{1,0:T(8,128)S(1)}, f32[512,128]{1,0:T(8,128)S(1)}, u32[]{:S(2)}, u32[]{:S(2)}) collective-permute-start(f32[512,128]{1,0:T(8,128)S(1)} %get-tuple-element.49), channel_id=1, source_target_pairs={{0,1},{1,0},{2,3},{3,2},{4,5},{5,4},{6,7},{7,6},{8,9},{9,8},{10,11... | collective-permute-start | bytes 786440 | tf_op jit(solution)/shard_map/ppermute | solution.py:299
  30.2 5.9 %collective-permute-start.8 = (f32[512,128]{1,0:T(8,128)S(1)}, f32[512,128]{1,0:T(8,128)S(1)}, u32[]{:S(2)}, u32[]{:S(2)}) collective-permute-start(f32[512,128]{1,0:T(8,128)S(1)} %get-tuple-element.53), channel_id=1, source_target_pairs={{1,2},{2,1},{5,6},{6,5},{9,10},{10,9},{13,14},{14,13},{17,18},{18,... | collective-permute-start | bytes 786440 | tf_op jit(solution)/shard_map/ppermute | solution.py:299
  30.9 11.1 %collective-permute-start.11 = (f32[512,128]{1,0:T(8,128)S(1)}, f32[512,128]{1,0:T(8,128)S(1)}, u32[]{:S(2)}, u32[]{:S(2)}) collective-permute-start(f32[512,128]{1,0:T(8,128)S(1)} %get-tuple-element.56.refs_0_), channel_id=1, source_target_pairs={{0,4},{4,0},{8,12},{12,8},{16,20},{20,16},{24,28},{28,24},{1,5},{5... | collective-permute-start | bytes 786440 | tf_op jit(solution)/shard_map/ppermute | solution.py:295
  33.1 10.1 %collective-permute-start.13 = (f32[512,128]{1,0:T(8,128)S(1)}, f32[512,128]{1,0:T(8,128)S(1)}, u32[]{:S(2)}, u32[]{:S(2)}) collective-permute-start(f32[512,128]{1,0:T(8,128)S(1)} %collective-permute-done.12.refs_2_), channel_id=1, source_target_pairs={{0,4},{4,0},{8,12},{12,8},{16,20},{20,16},{24,28},{28,24},{1,5},{5... | collective-permute-start | bytes 786440 | tf_op jit(solution)/shard_map/ppermute | solution.py:295
  33.1 10.1 %collective-permute-start.15 = (f32[512,128]{1,0:T(8,128)S(1)}, f32[512,128]{1,0:T(8,128)S(1)}, u32[]{:S(2)}, u32[]{:S(2)}) collective-permute-start(f32[512,128]{1,0:T(8,128)S(1)} %collective-permute-done.14.refs_4_), channel_id=1, source_target_pairs={{0,4},{4,0},{8,12},{12,8},{16,20},{20,16},{24,28},{28,24},{1,5},{5... | collective-permute-start | bytes 786440 | tf_op jit(solution)/shard_map/ppermute | solution.py:295
  36.1 7.2 %collective-permute-start.17 = (f32[512,128]{1,0:T(8,128)S(1)}, f32[512,128]{1,0:T(8,128)S(1)}, u32[]{:S(2)}, u32[]{:S(2)}) collective-permute-start(f32[512,128]{1,0:T(8,128)S(1)} %collective-permute-done.16.refs_6_), channel_id=1, source_target_pairs={{0,4},{4,0},{8,12},{12,8},{16,20},{20,16},{24,28},{28,24},{1,5},{5... | collective-permute-start | bytes 786440 | tf_op jit(solution)/shard_map/ppermute | solution.py:295
  36.1 16.0 %collective-permute-start.9 = (f32[512,128]{1,0:T(8,128)S(1)}, f32[512,128]{1,0:T(8,128)S(1)}, u32[]{:S(2)}, u32[]{:S(2)}) collective-permute-start(f32[512,128]{1,0:T(8,128)S(1)} %select_add_fusion.1), channel_id=1, source_target_pairs={{0,2},{1,3},{2,0},{3,1},{4,6},{5,7},{6,4},{7,5},{8,10},{9,11},{10,... | collective-permute-start | bytes 786440 | tf_op jit(solution)/shard_map/ppermute | solution.py:299
  41.9 10.1 %collective-permute-start.10 = (f32[512,128]{1,0:T(8,128)S(1)}, f32[512,128]{1,0:T(8,128)S(1)}, u32[]{:S(2)}, u32[]{:S(2)}) collective-permute-start(f32[512,128]{1,0:T(8,128)S(1)} %get-tuple-element.53), channel_id=1, source_target_pairs={{0,1},{3,2},{4,5},{7,6},{8,9},{11,10},{12,13},{15,14},{16,17},{19,... | collective-permute-start | bytes 786440 | tf_op jit(solution)/shard_map/ppermute | solution.py:299
  52.1 7.0 %collective-permute-start.18 = (f32[512,128]{1,0:T(8,128)S(1)}, f32[512,128]{1,0:T(8,128)S(1)}, u32[]{:S(2)}, u32[]{:S(2)}) collective-permute-start(f32[512,128]{1,0:T(8,128)S(1)} %get-tuple-element.62), channel_id=1, source_target_pairs={{0,1},{1,0},{2,3},{3,2},{4,5},{5,4},{6,7},{7,6},{8,9},{9,8},{10,11... | collective-permute-start | bytes 786440 | tf_op jit(solution)/shard_map/ppermute | solution.py:299
  53.9 5.2 %collective-permute-start.19 = (f32[512,128]{1,0:T(8,128)S(1)}, f32[512,128]{1,0:T(8,128)S(1)}, u32[]{:S(2)}, u32[]{:S(2)}) collective-permute-start(f32[512,128]{1,0:T(8,128)S(1)} %get-tuple-element.67), channel_id=1, source_target_pairs={{1,2},{2,1},{5,6},{6,5},{9,10},{10,9},{13,14},{14,13},{17,18},{18,... | collective-permute-start | bytes 786440 | tf_op jit(solution)/shard_map/ppermute | solution.py:299
  59.1 16.1 %collective-permute-start.20 = (f32[512,128]{1,0:T(8,128)S(1)}, f32[512,128]{1,0:T(8,128)S(1)}, u32[]{:S(2)}, u32[]{:S(2)}) collective-permute-start(f32[512,128]{1,0:T(8,128)S(1)} %select_add_fusion), channel_id=1, source_target_pairs={{0,2},{1,3},{2,0},{3,1},{4,6},{5,7},{6,4},{7,5},{8,10},{9,11},{10,... | collective-permute-start | bytes 786440 | tf_op jit(solution)/shard_map/ppermute | solution.py:299
  65.1 10.1 %collective-permute-start.21 = (f32[512,128]{1,0:T(8,128)S(1)}, f32[512,128]{1,0:T(8,128)S(1)}, u32[]{:S(2)}, u32[]{:S(2)}) collective-permute-start(f32[512,128]{1,0:T(8,128)S(1)} %get-tuple-element.67), channel_id=1, source_target_pairs={{0,1},{3,2},{4,5},{7,6},{8,9},{11,10},{12,13},{15,14},{16,17},{19,... | collective-permute-start | bytes 786440 | tf_op jit(solution)/shard_map/ppermute | solution.py:299
  77.1 12.6 %collective-permute-start.23 = (f32[512,256]{1,0:T(8,128)S(1)}, f32[512,256]{1,0:T(8,128)S(1)}, u32[]{:S(2)}, u32[]{:S(2)}) collective-permute-start(f32[512,256]{1,0:T(8,128)S(1)} %get-tuple-element.73.refs_0_), channel_id=1, source_target_pairs={{0,2},{3,1},{1,0},{2,3},{4,6},{7,5},{5,4},{6,7},{8,10},{11,9},{9,8... | collective-permute-start | bytes 1572872 | tf_op jit(solution)/shard_map/ppermute | solution.py:299
  78.9 16.2 %collective-permute-start.22 = (f32[128,256]{1,0:T(8,128)S(1)}, f32[128,256]{1,0:T(8,128)S(1)}, u32[]{:S(2)}, u32[]{:S(2)}) collective-permute-start(f32[128,256]{1,0:T(8,128)S(1)} %constant_dynamic-slice_fusion), channel_id=1, source_target_pairs={{0,4},{4,0},{8,12},{12,8},{16,20},{20,16},{24,28},{28,24},{1,5},{5... | collective-permute-start | bytes 393224 | tf_op jit(solution)/shard_map/ppermute | solution.py:295
  89.7 26.9 %collective-permute-start.28 = (f32[512,256]{1,0:T(8,128)S(1)}, f32[512,256]{1,0:T(8,128)S(1)}, u32[]{:S(2)}, u32[]{:S(2)}) collective-permute-start(f32[512,256]{1,0:T(8,128)S(1)} %get-tuple-element.73.refs_0_), channel_id=1, source_target_pairs={{1,2},{2,1},{5,6},{6,5},{9,10},{10,9},{13,14},{14,13},{17,18},{18,... | collective-permute-start | bytes 1572872 | tf_op jit(solution)/shard_map/ppermute | solution.py:299
  90.4 26.2 %collective-permute-start.27 = (f32[512,256]{1,0:T(8,128)S(1)}, f32[512,256]{1,0:T(8,128)S(1)}, u32[]{:S(2)}, u32[]{:S(2)}) collective-permute-start(f32[512,256]{1,0:T(8,128)S(1)} %get-tuple-element.73.refs_0_), channel_id=1, source_target_pairs={{2,0},{1,3},{0,1},{3,2},{6,4},{5,7},{4,5},{7,6},{10,8},{9,11},{8,9... | collective-permute-start | bytes 1572872 | tf_op jit(solution)/shard_map/ppermute | solution.py:299
  93.8 23.1 %collective-permute-start.29 = (f32[512,256]{1,0:T(8,128)S(1)}, f32[512,256]{1,0:T(8,128)S(1)}, u32[]{:S(2)}, u32[]{:S(2)}) collective-permute-start(f32[512,256]{1,0:T(8,128)S(1)} %collective-permute-done.23.refs_1_), channel_id=1, source_target_pairs={{1,0},{2,3},{5,4},{6,7},{9,8},{10,11},{13,12},{14,15},{17,16},{18,... | collective-permute-start | bytes 1572872 | tf_op jit(solution)/shard_map/ppermute | solution.py:299
  95.1 7.0 %collective-permute-start.26 = (f32[128,256]{1,0:T(8,128)S(1)}, f32[128,256]{1,0:T(8,128)S(1)}, u32[]{:S(2)}, u32[]{:S(2)}) collective-permute-start(f32[128,256]{1,0:T(8,128)S(1)} %dynamic-slice_add_fusion), channel_id=1, source_target_pairs={{0,24},{4,28},{8,16},{12,20},{16,8},{20,12},{24,0},{28,4},{1,25},{... | collective-permute-start | bytes 393224 | tf_op jit(solution)/shard_map/ppermute | solution.py:295
  97.1 19.5 %collective-permute-start.25 = (f32[128,256]{1,0:T(8,128)S(1)}, f32[128,256]{1,0:T(8,128)S(1)}, u32[]{:S(2)}, u32[]{:S(2)}) collective-permute-start(f32[128,256]{1,0:T(8,128)S(1)} %dynamic-slice_add_fusion), channel_id=1, source_target_pairs={{0,16},{4,20},{8,24},{12,28},{16,0},{20,4},{24,8},{28,12},{1,17},{... | collective-permute-start | bytes 393224 | tf_op jit(solution)/shard_map/ppermute | solution.py:295
  102.1 14.5 %collective-permute-start.24 = (f32[128,256]{1,0:T(8,128)S(1)}, f32[128,256]{1,0:T(8,128)S(1)}, u32[]{:S(2)}, u32[]{:S(2)}) collective-permute-start(f32[128,256]{1,0:T(8,128)S(1)} %dynamic-slice_add_fusion), channel_id=1, source_target_pairs={{0,8},{4,12},{8,0},{12,4},{16,24},{20,28},{24,16},{28,20},{1,9},{5... | collective-permute-start | bytes 393224 | tf_op jit(solution)/shard_map/ppermute | solution.py:295
  103.7 2.8 %copy-start.1 = (f32[1,1,96,128,128]{4,3,2,1,0:T(8,128)S(1)}, f32[1,1,96,128,128]{4,3,2,1,0:T(8,128)}, u32[]{:S(2)}) copy-start(f32[1,1,96,128,128]{4,3,2,1,0:T(8,128)} %param.11) | copy-start | bytes 18874372
  122.7 2.0 %collective-permute-start.35 = (f32[512,256]{1,0:T(8,128)S(1)}, f32[512,256]{1,0:T(8,128)S(1)}, u32[]{:S(2)}, u32[]{:S(2)}) collective-permute-start(f32[512,256]{1,0:T(8,128)S(1)} %get-tuple-element.81), channel_id=1, source_target_pairs={{0,4},{4,0},{8,12},{12,8},{16,20},{20,16},{24,28},{28,24},{1,5},{5... | collective-permute-start | bytes 1572872 | tf_op jit(solution)/shard_map/ppermute | solution.py:295
  122.8 11.9 %collective-permute-start.34 = (f32[512,256]{1,0:T(8,128)S(1)}, f32[512,256]{1,0:T(8,128)S(1)}, u32[]{:S(2)}, u32[]{:S(2)}) collective-permute-start(f32[512,256]{1,0:T(8,128)S(1)} %get-tuple-element.79), channel_id=1, source_target_pairs={{0,4},{4,0},{8,12},{12,8},{16,20},{20,16},{24,28},{28,24},{1,5},{5... | collective-permute-start | bytes 1572872 | tf_op jit(solution)/shard_map/ppermute | solution.py:295
  123.3 12.4 %collective-permute-start.38 = (f32[512,256]{1,0:T(8,128)S(1)}, f32[512,256]{1,0:T(8,128)S(1)}, u32[]{:S(2)}, u32[]{:S(2)}) collective-permute-start(f32[512,256]{1,0:T(8,128)S(1)} %get-tuple-element.83), channel_id=1, source_target_pairs={{0,4},{4,0},{8,12},{12,8},{16,20},{20,16},{24,28},{28,24},{1,5},{5... | collective-permute-start | bytes 1572872 | tf_op jit(solution)/shard_map/ppermute | solution.py:295
  124.8 9.9 %collective-permute-start.36 = (f32[256,256]{1,0:T(8,128)S(1)}, f32[256,256]{1,0:T(8,128)S(1)}, u32[]{:S(2)}, u32[]{:S(2)}) collective-permute-start(f32[256,256]{1,0:T(8,128)S(1)} %get-tuple-element.85), channel_id=1, source_target_pairs={{0,16},{4,20},{8,24},{12,28},{16,0},{20,4},{24,8},{28,12},{1,17},{... | collective-permute-start | bytes 786440 | tf_op jit(solution)/shard_map/ppermute | solution.py:295
  126.6 8.1 %collective-permute-start.39 = (f32[256,256]{1,0:T(8,128)S(1)}, f32[256,256]{1,0:T(8,128)S(1)}, u32[]{:S(2)}, u32[]{:S(2)}) collective-permute-start(f32[256,256]{1,0:T(8,128)S(1)} %get-tuple-element.86), channel_id=1, source_target_pairs={{0,8},{4,12},{8,0},{12,4},{16,24},{20,28},{24,16},{28,20},{1,9},{5... | collective-permute-start | bytes 786440 | tf_op jit(solution)/shard_map/ppermute | solution.py:295
  127.5 6.6 %collective-permute-start.30 = (f32[128,256]{1,0:T(8,128)S(1)}, f32[128,256]{1,0:T(8,128)S(1)}, u32[]{:S(2)}, u32[]{:S(2)}) collective-permute-start(f32[128,256]{1,0:T(8,128)S(1)} %add_add_fusion.1), channel_id=1, source_target_pairs={{0,1},{1,0},{2,3},{3,2},{4,5},{5,4},{6,7},{7,6},{8,9},{9,8},{10,11... | collective-permute-start | bytes 393224 | tf_op jit(solution)/shard_map/ppermute | solution.py:299
  134.1 14.5 %collective-permute-start.33 = (f32[512,256]{1,0:T(8,128)S(1)}, f32[512,256]{1,0:T(8,128)S(1)}, u32[]{:S(2)}, u32[]{:S(2)}) collective-permute-start(f32[512,256]{1,0:T(8,128)S(1)} %get-tuple-element.77), channel_id=1, source_target_pairs={{0,4},{4,0},{8,12},{12,8},{16,20},{20,16},{24,28},{28,24},{1,5},{5... | collective-permute-start | bytes 1572872 | tf_op jit(solution)/shard_map/ppermute | solution.py:295
  134.8 13.9 %collective-permute-start.37 = (f32[512,256]{1,0:T(8,128)S(1)}, f32[512,256]{1,0:T(8,128)S(1)}, u32[]{:S(2)}, u32[]{:S(2)}) collective-permute-start(f32[512,256]{1,0:T(8,128)S(1)} %pad_add_fusion.1), channel_id=1, source_target_pairs={{0,8},{4,12},{8,0},{12,4},{16,24},{20,28},{24,16},{28,20},{1,9},{5... | collective-permute-start | bytes 1572872 | tf_op jit(solution)/shard_map/ppermute | solution.py:295
  136.6 13.9 %collective-permute-start.40 = (f32[512,256]{1,0:T(8,128)}, f32[512,256]{1,0:T(8,128)S(1)}, u32[]{:S(2)}, u32[]{:S(2)}) collective-permute-start(f32[512,256]{1,0:T(8,128)} %pad_add_fusion), channel_id=1, source_target_pairs={{0,16},{4,20},{8,24},{12,28},{16,0},{20,4},{24,8},{28,12},{1,17},{... | collective-permute-start | bytes 1572872 | tf_op jit(solution)/shard_map/ppermute | solution.py:295
  137.5 9.0 %collective-permute-start.31 = (f32[128,256]{1,0:T(8,128)S(1)}, f32[128,256]{1,0:T(8,128)S(1)}, u32[]{:S(2)}, u32[]{:S(2)}) collective-permute-start(f32[128,256]{1,0:T(8,128)S(1)} %add.72), channel_id=1, source_target_pairs={{0,2},{1,3},{2,0},{3,1},{4,6},{5,7},{6,4},{7,5},{8,10},{9,11},{10,... | collective-permute-start | bytes 393224 | tf_op jit(solution)/shard_map/ppermute | solution.py:299
  146.5 1.4 collective-permute-start.32
